TPU v7x, 512 devices: a whole 4x8x8 slice. The times are simulated.
512 devices in a mesh: dp: 8 (over z), seq: 64 (over y, x, core).
Axes of the slice: x: 4, y: 8, z: 8, core: 2. Of those that a mesh axis runs over, the one named last changes fastest.
Arguments:
- q_raw: bfloat16 [8, 8192, 1536], P('dp', 'seq'), may hold values from -6 to 6
- k_raw: bfloat16 [8, 8192, 1536], P('dp', 'seq'), may hold values from -6 to 6
- values: bfloat16 [8, 8192, 1536], P('dp', 'seq'), may hold values from -6 to 6
- d_out: bfloat16 [8, 8192, 1536], P('dp', 'seq'), may hold values from -6 to 6
- q_gain: float32 [128], replicated, may hold values from 0.1 to 1.9
- k_gain: float32 [128], replicated, may hold values from 0.1 to 1.9
- offsets: int32 [12, 5], replicated, may hold values from 0 to 4, each once within a row
- counts: int32 [128, 12], replicated, may hold values from 1 to 5, as said below
Outputs:
- attn_out: bfloat16 [8, 8192, 1536], P('dp', 'seq')
- q_grad: bfloat16 [8, 8192, 1536], P('dp', 'seq')
- k_grad: bfloat16 [8, 8192, 1536], P('dp', 'seq')
- v_grad: bfloat16 [8, 8192, 1536], P('dp', 'seq')
- q_gain_grad: float32 [128], replicated
- k_gain_grad: float32 [128], replicated
Inputs may be any that keep to these rules, and one draw needn't show every extreme that they name: Each row of offsets holds every slot 0 .. 4 once. counts[i, h] is how many leading entries of offsets[h] query tile i of head h uses.
All inputs are finite; a program needn't handle non-finite values.
Results may differ from a plain program's by a relative error of at most 0.01.
Values may be sent and summed in bfloat16 or wider, within the bound.
No kernel may reach another device: no remote copies, remote signals or barrier semaphores. Data moves between devices by JAX's collectives and lax.ppermute only.
A program may use at most 64 MiB of HBM per device.

v0:
```python
import jax
import jax.numpy as jnp
from jax import lax
from jax.sharding import PartitionSpec as P

TILE = 64
SPAN = 1


def from_behind(block, axis, distance):
    devices = range(lax.axis_size(axis))
    route = [(i - distance, i) for i in devices if i - distance in devices]
    return lax.ppermute(block, axis, route)


def normalize(raw_rows, gain_vec):
    as_float = raw_rows.astype(jnp.float32)
    spread = jnp.sqrt(jnp.mean(as_float * as_float, axis=-1, keepdims=True) + 1e-06)
    unit_rows = as_float / spread
    return (unit_rows, spread, (unit_rows * gain_vec).astype(jnp.bfloat16))


def norm_grad(grad_n, unit_rows, spread, gain_vec):
    scaled = grad_n * gain_vec
    return (scaled - unit_rows * jnp.mean(scaled * unit_rows, axis=-1, keepdims=True)) / spread


def tile_mask(offsets, counts, query_tiles, key_tiles, ntiles, reach_tiles):
    slot_total = 2 * reach_tiles + 1
    slot_ids = jnp.arange(slot_total, dtype=jnp.int32)
    slot_rank = jnp.sum(
        slot_ids[None, :, None]
        * (offsets[:, :, None] == slot_ids[None, None, :]).astype(jnp.int32),
        axis=1,
    )
    relative = key_tiles[None, :] - query_tiles[:, None]
    inside = (
        (jnp.abs(relative) <= reach_tiles)
        & (key_tiles[None, :] >= 0)
        & (key_tiles[None, :] < ntiles)
    )
    inside = inside & (query_tiles[:, None] >= 0) & (query_tiles[:, None] < ntiles)
    slot_pick = (
        jnp.clip(relative + reach_tiles, 0, slot_total - 1)[:, :, None] == slot_ids
    ).astype(jnp.int32)
    rank_at = jnp.sum(slot_rank[:, None, None, :] * slot_pick[None], axis=-1)
    tile_counts = counts[jnp.clip(query_tiles, 0, ntiles - 1)]
    chosen = (relative == 0)[None] | (rank_at < tile_counts.T[:, :, None])
    tiles_seen = inside[None] & chosen
    return jnp.repeat(jnp.repeat(tiles_seen, TILE, axis=1), TILE, axis=2)


def shards(q_raw, k_raw, values, d_out, q_gain, k_gain, offsets, counts):
    tokens_here = q_raw.shape[1]
    head_count = offsets.shape[0]
    head_width = q_gain.shape[0]
    head_shape = (tokens_here, head_count, head_width)
    tiles_here = tokens_here // TILE
    reach_tiles = SPAN * tiles_here
    ntiles = tiles_here * lax.axis_size("seq")
    position = lax.axis_index("seq")
    score_scale = head_width ** (-0.5)
    q_unit, q_spread, q_norm = normalize(q_raw[0].reshape(head_shape), q_gain)
    k_unit, k_spread, k_norm = normalize(k_raw[0].reshape(head_shape), k_gain)
    value_rows = values[0].reshape(head_shape)
    grad_rows = d_out[0].reshape(head_shape)
    key_value = jnp.stack([k_norm, value_rows])
    lower_parts = []
    distance = 1
    lower_parts.insert(0, from_behind(key_value, "seq", distance))
    upper_parts = [from_behind(key_value, "seq", -distance)]
    window = jnp.concatenate(lower_parts + [key_value] + upper_parts, axis=1)
    own_tiles = position * tiles_here + jnp.arange(tiles_here, dtype=jnp.int32)
    win_tiles = (position - SPAN) * tiles_here + jnp.arange(
        (2 * SPAN + 1) * tiles_here, dtype=jnp.int32
    )
    visible = tile_mask(offsets, counts, own_tiles, win_tiles, ntiles, reach_tiles)
    scores = (
        jnp.einsum("qhd,khd->hqk", q_norm, window[0], preferred_element_type=jnp.float32)
        * score_scale
    )
    scores = jnp.where(visible, scores, -jnp.inf)
    row_max = jnp.max(scores, axis=-1, keepdims=True)
    log_total = row_max[..., 0] + jnp.log(jnp.sum(jnp.exp(scores - row_max), axis=-1))
    chances = jnp.exp(scores - log_total[..., None])
    weights = chances.astype(jnp.bfloat16)
    attended = jnp.einsum(
        "hqk,khd->qhd", weights, window[1], preferred_element_type=jnp.float32
    ).astype(jnp.bfloat16)
    out_dot = jnp.sum(grad_rows.astype(jnp.float32) * attended.astype(jnp.float32), axis=-1).T
    grad_prob = jnp.einsum("qhd,khd->hqk", grad_rows, window[1], preferred_element_type=jnp.float32)
    dscore = (chances * (grad_prob - out_dot[..., None])).astype(jnp.bfloat16)
    grad_qn = (
        jnp.einsum("hqk,khd->qhd", dscore, window[0], preferred_element_type=jnp.float32)
        * score_scale
    )
    key_part = (
        jnp.einsum("hqk,qhd->khd", dscore, q_norm, preferred_element_type=jnp.float32) * score_scale
    )
    value_part = jnp.einsum("hqk,qhd->khd", weights, grad_rows, preferred_element_type=jnp.float32)
    blocks = jnp.stack([key_part, value_part]).reshape(
        2, 2 * SPAN + 1, tokens_here, head_count, head_width
    )
    key_grads = blocks[:, SPAN]
    distance = 1
    key_grads = key_grads + from_behind(blocks[:, SPAN - distance], "seq", -distance)
    key_grads = key_grads + from_behind(blocks[:, SPAN + distance], "seq", distance)
    grad_kn = key_grads[0]
    q_grad = norm_grad(grad_qn, q_unit, q_spread, q_gain).astype(jnp.bfloat16)
    k_grad = norm_grad(grad_kn, k_unit, k_spread, k_gain).astype(jnp.bfloat16)
    gain_terms = jnp.stack(
        [jnp.sum(grad_qn * q_unit, axis=(0, 1)), jnp.sum(grad_kn * k_unit, axis=(0, 1))]
    )
    gain_total = lax.psum(gain_terms, ("dp", "seq"))
    flat_shape = (1, tokens_here, head_count * head_width)
    return (
        attended.reshape(flat_shape),
        q_grad.reshape(flat_shape),
        k_grad.reshape(flat_shape),
        key_grads[1].astype(jnp.bfloat16).reshape(flat_shape),
        gain_total[0],
        gain_total[1],
    )


def solution(mesh):
    in_specs = (
        P("dp", "seq", None),
        P("dp", "seq", None),
        P("dp", "seq", None),
        P("dp", "seq", None),
        P(),
        P(),
        P(),
        P(),
    )
    out_specs = (
        P("dp", "seq", None),
        P("dp", "seq", None),
        P("dp", "seq", None),
        P("dp", "seq", None),
        P(),
        P(),
    )
    return jax.shard_map(shards, mesh=mesh, in_specs=in_specs, out_specs=out_specs, check_vma=False)
```

profile of v0, /device:TPU:1, one launch (start us, length us, event | category | flops | bytes accessed | tf_op | source)
XLA Modules:
  0.0 188.9 jit_solution(1837841749778631475)
XLA Ops:
  0.6 1.2 copy.88
  2.1 1.2 copy.86
  5.0 8.8 %collective-permute-start.1 = (bf16[2,128,12,128]{3,1,2,0:T(8,128)(2,1)}, bf16[2,128,12,128]{3,1,2,0:T(8,128)(2,1)}, u32[]{:S(2)}, u32[]{:S(2)}) collective-permute-start(bf16[2,128,12,128]{3,1,2,0:T(8,128)(2,1)} %pad_maximum_fusion.2), channel_id=1, source_target_pairs={{1,0},{2,1},{3,2},{4,3},{5,4},{6,5},{7,6},{8,7},{9,8},{10,9},{11,1... | collective-permute-start | bytes 2359304 | tf_op jit(solution)/shard_map/ppermute | solution.py:13
  13.8 1.9 %collective-permute-start = (bf16[2,128,12,128]{3,1,2,0:T(8,128)(2,1)}, bf16[2,128,12,128]{3,1,2,0:T(8,128)(2,1)}, u32[]{:S(2)}, u32[]{:S(2)}) collective-permute-start(bf16[2,128,12,128]{3,1,2,0:T(8,128)(2,1)} %pad_maximum_fusion.2), channel_id=1, source_target_pairs={{0,1},{1,2},{2,3},{3,4},{4,5},{5,6},{6,7},{7,8},{8,9},{9,10},{10,1... | collective-permute-start | bytes 2359304 | tf_op jit(solution)/shard_map/ppermute | solution.py:13
  18.4 1.5 copy.94
  19.9 1.2 copy.92
  21.2 3.8 %collective-permute-done = bf16[2,128,12,128]{3,1,2,0:T(8,128)(2,1)} collective-permute-done((bf16[2,128,12,128]{3,1,2,0:T(8,128)(2,1)}, bf16[2,128,12,128]{3,1,2,0:T(8,128)(2,1)}, u32[]{:S(2)}, u32[]{:S(2)}) %collective-permute-start) | collective-permute-done | bytes 786464 | tf_op jit(solution)/shard_map/ppermute | solution.py:13
  25.0 1.6 pad_maximum_fusion
  28.2 1.6 multiply_reduce_fusion
  29.8 2.3 %fusion.20 = f32[12,384,128]{2,1,0:T(8,128)} fusion(bf16[128,12,128]{0,2,1:T(8,128)(2,1)S(1)} %bitcast.118, f32[12,128,384]{2,1,0:T(8,128)S(1)} %get-tuple-element.41, f32[12,128]{1,0:T(8,128)S(1)} %log_add_fusion), kind=kOutput, calls=%fused_computation.52 | convolution fusion | flops 152174592 | bytes 5117952 | tf_op jit(solution)/shard_map/hqk,qhd->khd/dot_general | solution.py:100
  34.0 2.0 %multiply_bitcast_fusion = f32[384,12,128]{0,2,1:T(8,128)} fusion(bf16[12,128,384]{2,1,0:T(8,128)(2,1)S(1)} %fusion, f32[128]{0:T(128)S(1)} %copy-done.11, f32[128,12,128]{0,2,1:T(8,128)S(1)} %bitcast.112, f32[128,12]{0,1:T(8,128)S(1)} %add_sqrt_fusion), kind=kOutput, calls=%fused_computation.8 | convolution fusion | flops 152174592 | bytes 4332032 | tf_op jit(solution)/shard_map/hqk,qhd->khd/dot_general | solution.py:98
  36.0 3.1 %copy.100 = f32[384,12,128]{2,0,1:T(8,128)} copy(f32[384,12,128]{0,2,1:T(8,128)} %multiply_bitcast_fusion) | data formatting | bytes 4718592 | tf_op jit(solution)/shard_map/mul | solution.py:98
  39.1 2.0 %copy.103 = f32[1,3,128,12,128]{2,4,3,0,1:T(8,128)S(1)} copy(f32[1,3,128,12,128]{4,2,1,3,0:T(8,128)} %bitcast.116) | data formatting | bytes 4718592 | tf_op jit(solution)/shard_map/stack | solution.py:101
  41.2 3.0 %copy.104 = f32[1,3,128,12,128]{2,4,3,0,1:T(8,128)} copy(f32[1,3,128,12,128]{4,2,1,3,0:T(8,128)} %bitcast.115) | data formatting | bytes 4718592 | tf_op jit(solution)/shard_map/stack | solution.py:101
  44.2 3.4 %fusion.3 = (f32[2,128,12,128]{1,3,2,0:T(8,128)}, f32[2,128,12,128]{1,3,2,0:T(8,128)}) fusion(f32[1,3,128,12,128]{2,4,3,0,1:T(8,128)S(1)} %copy.103, f32[1,3,128,12,128]{2,4,3,0,1:T(8,128)} %copy.104), kind=kLoop, calls=%fused_computation.14 | loop fusion | flops 786432 | bytes 7864320 | tf_op jit(solution)/shard_map/squeeze | solution.py:106
  47.6 4.3 %collective-permute-start.3 = (f32[2,128,12,128]{1,3,2,0:T(8,128)}, f32[2,128,12,128]{1,3,2,0:T(8,128)}, u32[]{:S(2)}, u32[]{:S(2)}) collective-permute-start(f32[2,128,12,128]{1,3,2,0:T(8,128)} %get-tuple-element.35), channel_id=1, source_target_pairs={{0,1},{1,2},{2,3},{3,4},{4,5},{5,6},{6,7},{7,8},{8,9},{9,10},{10,1... | collective-permute-start | bytes 4718600 | tf_op jit(solution)/shard_map/ppermute | solution.py:13
  51.9 1.9 %collective-permute-start.2 = (f32[2,128,12,128]{1,3,2,0:T(8,128)}, f32[2,128,12,128]{1,3,2,0:T(8,128)}, u32[]{:S(2)}, u32[]{:S(2)}) collective-permute-start(f32[2,128,12,128]{1,3,2,0:T(8,128)} %get-tuple-element.34), channel_id=1, source_target_pairs={{1,0},{2,1},{3,2},{4,3},{5,4},{6,5},{7,6},{8,7},{9,8},{10,9},{11,1... | collective-permute-start | bytes 4718600 | tf_op jit(solution)/shard_map/ppermute | solution.py:13
  55.0 1.9 %copy.105 = bf16[1,128,1536]{2,1,0:T(8,128)(2,1)} copy(bf16[1,128,1536]{1,2,0:T(8,128)(2,1)} %bitcast.121) | data formatting | bytes 786432
  56.9 3.2 %fusion.12 = (f32[128]{0:T(128)}, f32[128,12]{0,1:T(8,128)S(1)}, f32[12,128,128]{2,1,0:T(8,128)S(1)}) fusion(f32[128,12,128]{0,2,1:T(8,128)} %bitcast.113, f32[128,12]{0,1:T(8,128)S(1)} %add_sqrt_fusion, f32[128]{0:T(128)} %broadcast_multiply_fusion.2, bf16[12,128,384]{2,1,0:T(8,128)(2,1)} %copy-done.3, bf16[2,384,12,128]{3,1,2,0:T(8,128)(2,1)} %copy-done.2), kind=kOutput, calls=%fused_computation.32 | convolution fusion | flops 152369536 | bytes 3945472 | tf_op jit(solution)/shard_map/hqk,khd->qhd/dot_general | solution.py:94
  61.1 1.9 %copy.106 = bf16[1,128,1536]{2,1,0:T(8,128)(2,1)} copy(bf16[1,128,1536]{1,2,0:T(8,128)(2,1)} %bitcast.124) | data formatting | bytes 786432
  63.0 6.6 %collective-permute-done.3 = f32[2,128,12,128]{1,3,2,0:T(8,128)} collective-permute-done((f32[2,128,12,128]{1,3,2,0:T(8,128)}, f32[2,128,12,128]{1,3,2,0:T(8,128)}, u32[]{:S(2)}, u32[]{:S(2)}) %collective-permute-start.3) | collective-permute-done | bytes 1572896 | tf_op jit(solution)/shard_map/ppermute | solution.py:13
  69.6 4.4 %collective-permute-done.2 = f32[2,128,12,128]{1,3,2,0:T(8,128)} collective-permute-done((f32[2,128,12,128]{1,3,2,0:T(8,128)}, f32[2,128,12,128]{1,3,2,0:T(8,128)}, u32[]{:S(2)}, u32[]{:S(2)}) %collective-permute-start.2) | collective-permute-done | bytes 1572896 | tf_op jit(solution)/shard_map/ppermute | solution.py:13
  74.0 2.4 %fusion.7 = f32[2,128,12,128]{1,3,2,0:T(8,128)S(1)} fusion(f32[2,128,12,128]{1,3,2,0:T(8,128)} %collective-permute-done.3, f32[2,128,12,128]{1,3,2,0:T(8,128)} %collective-permute-done.2, f32[1,3,128,12,128]{2,4,3,0,1:T(8,128)S(1)} %copy.103, f32[1,3,128,12,128]{2,4,3,0,1:T(8,128)} %copy.104), kind=kLoop, calls=%fused_computation.18 | loop fusion | flops 1179648 | bytes 9437184 | tf_op jit(solution)/shard_map/add | solution.py:107
  79.2 109.1 %psum.7 = f32[2,128]{1,0:T(2,128)S(1)} all-reduce(f32[2,128]{1,0:T(2,128)S(1)} %pad_maximum_fusion.3), channel_id=1, replica_groups=mesh['dp'=8,'seq'=64] {'dp','seq'}, use_global_device_ids=true, to_apply=%region_11.12 | all-reduce | flops 256 | bytes 2048 | tf_op jit(solution)/shard_map/psum | solution.py:114
  (76 shorter events, 13.4 us)
Async XLA Ops:
  2.1 1.7 copy-start.8
  3.4 12.4 %copy-start.5 = (bf16[1,128,1536]{2,1,0:T(8,128)(2,1)S(1)}, bf16[1,128,1536]{2,1,0:T(8,128)(2,1)}, u32[]{:S(2)}) copy-start(bf16[1,128,1536]{2,1,0:T(8,128)(2,1)} %param.11) | copy-start | bytes 1179652
  3.7 13.2 %copy-start.7 = (s32[128,12]{0,1:T(8,128)S(1)}, s32[128,12]{0,1:T(8,128)}, u32[]{:S(2)}) copy-start(s32[128,12]{0,1:T(8,128)} %param.15) | copy-start | bytes 18436
  5.0 16.1 %collective-permute-start.1 = (bf16[2,128,12,128]{3,1,2,0:T(8,128)(2,1)}, bf16[2,128,12,128]{3,1,2,0:T(8,128)(2,1)}, u32[]{:S(2)}, u32[]{:S(2)}) collective-permute-start(bf16[2,128,12,128]{3,1,2,0:T(8,128)(2,1)} %pad_maximum_fusion.2), channel_id=1, source_target_pairs={{1,0},{2,1},{3,2},{4,3},{5,4},{6,5},{7,6},{8,7},{9,8},{10,9},{11,1... | collective-permute-start | bytes 2359304 | tf_op jit(solution)/shard_map/ppermute | solution.py:13
  13.8 11.2 %collective-permute-start = (bf16[2,128,12,128]{3,1,2,0:T(8,128)(2,1)}, bf16[2,128,12,128]{3,1,2,0:T(8,128)(2,1)}, u32[]{:S(2)}, u32[]{:S(2)}) collective-permute-start(bf16[2,128,12,128]{3,1,2,0:T(8,128)(2,1)} %pad_maximum_fusion.2), channel_id=1, source_target_pairs={{0,1},{1,2},{2,3},{3,4},{4,5},{5,6},{6,7},{7,8},{8,9},{9,10},{10,1... | collective-permute-start | bytes 2359304 | tf_op jit(solution)/shard_map/ppermute | solution.py:13
  21.0 12.0 %copy-start = (f32[1,128,1536]{1,2,0:T(8,128)}, f32[1,128,1536]{1,2,0:T(8,128)S(1)}, u32[]{:S(2)}) copy-start(f32[1,128,1536]{1,2,0:T(8,128)S(1)} %copy.92) | copy-start | bytes 2359300
  21.1 5.4 %copy-start.4 = (pred[12,128,384]{2,1,0:T(32,128)(4,1)S(1)}, pred[12,128,384]{2,1,0:T(32,128)(4,1)}, u32[]{:S(2)}) copy-start(pred[12,128,384]{2,1,0:T(32,128)(4,1)} %copy.94) | copy-start | bytes 1769476
  21.1 5.4 %copy-start.11 = (f32[128]{0:T(128)S(1)}, f32[128]{0:T(128)}, u32[]{:S(2)}) copy-start(f32[128]{0:T(128)} %param.12) | copy-start | bytes 1540
  26.6 5.6 %copy-start.2 = (bf16[2,384,12,128]{3,1,2,0:T(8,128)(2,1)}, bf16[2,384,12,128]{3,1,2,0:T(8,128)(2,1)S(1)}, u32[]{:S(2)}) copy-start(bf16[2,384,12,128]{3,1,2,0:T(8,128)(2,1)S(1)} %pad_maximum_fusion) | copy-start | bytes 7077892
  33.0 1.0 copy-start.3
  44.2 9.7 %copy-start.12 = (f32[128]{0:T(128)S(1)}, f32[128]{0:T(128)}, u32[]{:S(2)}) copy-start(f32[128]{0:T(128)} %param.12) | copy-start | bytes 1540
  44.2 10.2 %copy-start.9 = (f32[128]{0:T(128)S(1)}, f32[128]{0:T(128)}, u32[]{:S(2)}) copy-start(f32[128]{0:T(128)} %param.13) | copy-start | bytes 1540
  47.6 22.0 %collective-permute-start.3 = (f32[2,128,12,128]{1,3,2,0:T(8,128)}, f32[2,128,12,128]{1,3,2,0:T(8,128)}, u32[]{:S(2)}, u32[]{:S(2)}) collective-permute-start(f32[2,128,12,128]{1,3,2,0:T(8,128)} %get-tuple-element.35), channel_id=1, source_target_pairs={{0,1},{1,2},{2,3},{3,4},{4,5},{5,6},{6,7},{7,8},{8,9},{9,10},{10,1... | collective-permute-start | bytes 4718600 | tf_op jit(solution)/shard_map/ppermute | solution.py:13
  51.9 22.1 %collective-permute-start.2 = (f32[2,128,12,128]{1,3,2,0:T(8,128)}, f32[2,128,12,128]{1,3,2,0:T(8,128)}, u32[]{:S(2)}, u32[]{:S(2)}) collective-permute-start(f32[2,128,12,128]{1,3,2,0:T(8,128)} %get-tuple-element.34), channel_id=1, source_target_pairs={{1,0},{2,1},{3,2},{4,3},{5,4},{6,5},{7,6},{8,7},{9,8},{10,9},{11,1... | collective-permute-start | bytes 4718600 | tf_op jit(solution)/shard_map/ppermute | solution.py:13
  56.9 3.2 %copy-start.1 = (f32[1,128,1536]{1,2,0:T(8,128)S(1)}, f32[1,128,1536]{1,2,0:T(8,128)}, u32[]{:S(2)}) copy-start(f32[1,128,1536]{1,2,0:T(8,128)} %copy-done) | copy-start | bytes 2359300
  56.9 3.2 %copy-start.13 = (f32[128]{0:T(128)S(1)}, f32[128]{0:T(128)}, u32[]{:S(2)}) copy-start(f32[128]{0:T(128)} %broadcast_multiply_fusion.2) | copy-start | bytes 1540
  63.0 13.5 %copy-start.10 = (f32[128]{0:T(128)S(1)}, f32[128]{0:T(128)}, u32[]{:S(2)}) copy-start(f32[128]{0:T(128)} %param.13) | copy-start | bytes 1540
  76.4 0.7 copy-start.6
  76.7 2.5 %copy-start.14 = (f32[128]{0:T(128)S(1)}, f32[128]{0:T(128)}, u32[]{:S(2)}) copy-start(f32[128]{0:T(128)} %get-tuple-element.32) | copy-start | bytes 1540
where the time goes:
time: 190 us; the launch traced here: 189 us
  blocking collectives  109 us (57%)
  local copies, waits for them, and re-layouts  23.5 us (12%)
  starting transfers between devices  16.9 us (9%)
  waiting for transfers between devices  14.8 us (8%)
  other arithmetic  12.7 us (7%)
  matrix products  10.8 us (6%)
    psum x1, blocking collectives, shards(): gain_total = lax.psum(gain_terms, ('dp', 'seq'))  109 us
    ppermute x4, starting transfers between devices, from_behind(): return lax.ppermute(block, axis, route)  16.9 us
    ppermute x4, waiting for transfers between devices, from_behind(): return lax.ppermute(block, axis, route)  14.8 us
    unnamed x38, local copies, waits for them, and re-layouts  9.81 us
    another operation x2, local copies, waits for them, and re-layouts, shards(): jnp.stack([key_part, value_part])  5.06 us
  transfers between devices with their start and end apart: 4, of which 3 were waited for; matrix products, arithmetic and copies ran while one was open for 8% of the time, Pallas kernels for 0%

commit v1 on v0

v1 whole, which is shorter than its diff:
```python
import math

import jax
import jax.numpy as jnp
from jax import lax
from jax.experimental import pallas as pl
from jax.experimental.pallas import tpu as pltpu
from jax.sharding import PartitionSpec as P

TILE = 64
REACH = 2
EPS = 1e-06
HEADS_PER_STEP = 4
NT = (((1,), (1,)), ((), ()))
NN = (((1,), (0,)), ((), ()))


def dot(a, b, dims):
    return lax.dot_general(a, b, dims, preferred_element_type=jnp.float32)


def inverse_spread(rows, axis):
    return lax.rsqrt(jnp.mean(rows * rows, axis=axis, keepdims=True) + EPS)


def shift(block, distance):
    size = lax.axis_size("seq")
    route = [(i, i + distance) for i in range(size) if 0 <= i + distance < size]
    return lax.ppermute(block, "seq", route)


def prepare_kernel(width, q_ref, k_ref, g_ref, qg_ref, kg_ref, qn_ref, qt_ref, gt_ref, kn_ref, kt_ref):
    q_gain = qg_ref[...]
    k_gain = kg_ref[...]
    for h in range(q_ref.shape[1] // width):
        cols = slice(h * width, (h + 1) * width)
        q = q_ref[:, cols].astype(jnp.float32)
        qn = (q * inverse_spread(q, 1) * q_gain).astype(jnp.bfloat16)
        qn_ref[:, cols] = qn
        qt_ref[cols, :] = qn.T
        gt_ref[cols, :] = g_ref[:, cols].T
        k_raw = k_ref[:, cols]
        k = k_raw.astype(jnp.float32)
        kn_ref[:, cols] = (k * inverse_spread(k, 1) * k_gain).astype(jnp.bfloat16)
        kt_ref[cols, :] = k_raw.T


def attend_kernel(
    width,
    q_ref,
    qn_ref,
    qt_ref,
    g_ref,
    gt_ref,
    kn_ref,
    v_ref,
    low_ref,
    high_ref,
    mask_ref,
    qg_ref,
    kg_ref,
    out_ref,
    qgrad_ref,
    own_ref,
    to_low_ref,
    to_high_ref,
    gain_ref,
):
    q_gain = qg_ref[...]
    k_gain = kg_ref[...]
    rows = q_ref.shape[0]
    scale = width ** (-0.5)
    gain_sum = jnp.zeros((rows, width), jnp.float32)
    for h in range(q_ref.shape[1] // width):
        cols = slice(h * width, (h + 1) * width)

        def normal(raw):
            x = raw.astype(jnp.float32)
            return (x * inverse_spread(x, 1) * k_gain).astype(jnp.bfloat16)

        keys = jnp.concatenate(
            [normal(low_ref[0, :, cols]), kn_ref[:, cols], normal(high_ref[0, :, cols])], axis=0
        )
        vals = jnp.concatenate([low_ref[1, :, cols], v_ref[:, cols], high_ref[1, :, cols]], axis=0)
        mask = jnp.concatenate(
            [
                jnp.broadcast_to(mask_ref[h, t : t + 1, :], (TILE, 3 * rows))
                for t in range(rows // TILE)
            ],
            axis=0,
        )
        grads = g_ref[:, cols]
        scores = dot(qn_ref[:, cols], keys, NT)
        terms = jnp.exp2(scores * (scale * math.log2(math.e))) * mask
        probs = terms * (1.0 / jnp.sum(terms, axis=1, keepdims=True))
        weights = probs.astype(jnp.bfloat16)
        dprob = dot(grads, vals, NT)
        delta = jnp.sum(probs * dprob, axis=1, keepdims=True)
        dscore = (probs * (dprob - delta)).astype(jnp.bfloat16)
        out_ref[:, cols] = dot(weights, vals, NN).astype(jnp.bfloat16)
        grad_qn = dot(dscore, keys, NN) * scale
        key_t = dot(qt_ref[cols, :], dscore, NN) * scale
        val_t = dot(gt_ref[cols, :], weights, NN)
        own_ref[0, cols, :] = key_t[:, rows : 2 * rows]
        own_ref[1, cols, :] = val_t[:, rows : 2 * rows]
        to_low_ref[0, cols, :] = key_t[:, :rows].astype(jnp.bfloat16)
        to_low_ref[1, cols, :] = val_t[:, :rows].astype(jnp.bfloat16)
        to_high_ref[0, cols, :] = key_t[:, 2 * rows :].astype(jnp.bfloat16)
        to_high_ref[1, cols, :] = val_t[:, 2 * rows :].astype(jnp.bfloat16)
        q = q_ref[:, cols].astype(jnp.float32)
        inverse = inverse_spread(q, 1)
        unit = q * inverse
        product = grad_qn * unit
        gain_sum = gain_sum + product
        mean = jnp.mean(product * q_gain, axis=1, keepdims=True)
        qgrad_ref[:, cols] = ((grad_qn * q_gain - unit * mean) * inverse).astype(jnp.bfloat16)

    @pl.when(pl.program_id(0) == 0)
    def _():
        gain_ref[...] = jnp.zeros_like(gain_ref)

    gain_ref[...] += jnp.sum(gain_sum, axis=0, keepdims=True)


def finish_kernel(width, kt_ref, own_ref, low_ref, high_ref, kg_ref, kgrad_ref, vgrad_ref):
    gain = kg_ref[...]
    for h in range(kgrad_ref.shape[1] // width):
        cols = slice(h * width, (h + 1) * width)

        def total(i):
            return (
                own_ref[i, cols, :]
                + low_ref[i, cols, :].astype(jnp.float32)
                + high_ref[i, cols, :].astype(jnp.float32)
            )

        k = kt_ref[cols, :].astype(jnp.float32)
        inverse = inverse_spread(k, 0)
        unit = k * inverse
        scaled = total(0) * gain
        mean = jnp.mean(scaled * unit, axis=0, keepdims=True)
        kgrad_ref[:, cols] = ((scaled - unit * mean) * inverse).astype(jnp.bfloat16).T
        vgrad_ref[:, cols] = total(1).astype(jnp.bfloat16).T


def window_mask(offsets, counts, tiles_here):
    heads, slots = offsets.shape
    ntiles = counts.shape[0]
    first = lax.axis_index("seq") * tiles_here
    slot = jnp.arange(slots, dtype=jnp.int32)
    rank = jnp.sum(slot[None, :, None] * (offsets[:, :, None] == slot[None, None, :]), axis=1)
    used = lax.dynamic_slice_in_dim(counts, first, tiles_here, axis=0).T
    query = first + jnp.arange(tiles_here, dtype=jnp.int32)
    key = query[:, None] + slot[None, :] - REACH
    inside = (key >= 0) & (key < ntiles)
    allowed = inside[None] & ((slot == REACH)[None, None] | (rank[:, None, :] < used[:, :, None]))
    allowed = allowed.astype(jnp.float32)
    rows = [
        jnp.pad(allowed[:, t], ((0, 0), (t, tiles_here - 1 - t))) for t in range(tiles_here)
    ]
    return jnp.repeat(jnp.stack(rows, axis=1), TILE, axis=2)


def call(body, grid, in_specs, out_specs, out_shape, flops):
    return pl.pallas_call(
        body,
        grid=grid,
        in_specs=in_specs,
        out_specs=out_specs,
        out_shape=out_shape,
        compiler_params=pltpu.CompilerParams(vmem_limit_bytes=32 * 1024 * 1024),
        cost_estimate=pl.CostEstimate(flops=flops, bytes_accessed=4 << 20, transcendentals=0),
    )


def total_over(axis, vector):
    size = lax.axis_size(axis)
    spread = jnp.broadcast_to(vector[None], (size,) + vector.shape)
    return jnp.sum(lax.all_to_all(spread, axis, 0, 0), axis=0)


def shards(q_raw, k_raw, values, d_out, q_gain, k_gain, offsets, counts):
    rows, columns = q_raw.shape[1:]
    width = q_gain.shape[0]
    heads = offsets.shape[0]
    step = min(HEADS_PER_STEP, heads)
    chunk = step * width
    grid = (heads // step,)
    key_value = jnp.concatenate([k_raw, values], axis=0)
    low = shift(key_value, 1)
    high = shift(key_value, -1)
    q, k, v, g = q_raw[0], k_raw[0], values[0], d_out[0]
    q_row, k_row = q_gain[None], k_gain[None]
    mask = window_mask(offsets, counts, rows // TILE)

    flat = pl.BlockSpec((rows, chunk), lambda j: (0, j))
    turned = pl.BlockSpec((chunk, rows), lambda j: (j, 0))
    pair = pl.BlockSpec((2, rows, chunk), lambda j: (0, 0, j))
    turned_pair = pl.BlockSpec((2, chunk, rows), lambda j: (0, j, 0))
    vector = pl.BlockSpec((1, width), lambda j: (0, 0))
    flat_shape = jax.ShapeDtypeStruct((rows, columns), jnp.bfloat16)
    turned_shape = jax.ShapeDtypeStruct((columns, rows), jnp.bfloat16)
    part_shape = jax.ShapeDtypeStruct((2, columns, rows), jnp.bfloat16)

    def prepare(*refs):
        prepare_kernel(width, *refs)

    def attend(*refs):
        attend_kernel(width, *refs)

    def finish(*refs):
        finish_kernel(width, *refs)

    qn, qt, gt, kn, kt = call(
        prepare,
        grid,
        [flat, flat, flat, vector, vector],
        [flat, turned, turned, flat, turned],
        [flat_shape, turned_shape, turned_shape, flat_shape, turned_shape],
        rows * columns * 40,
    )(q, k, g, q_row, k_row)
    out, q_grad, own, to_low, to_high, gain = call(
        attend,
        grid,
        [flat, flat, turned, flat, turned, flat, flat, pair, pair]
        + [pl.BlockSpec((step, rows // TILE, 3 * rows), lambda j: (j, 0, 0)), vector, vector],
        [flat, flat, turned_pair, turned_pair, turned_pair, vector],
        [
            flat_shape,
            flat_shape,
            jax.ShapeDtypeStruct((2, columns, rows), jnp.float32),
            part_shape,
            part_shape,
            jax.ShapeDtypeStruct((1, width), jnp.float32),
        ],
        rows * rows * columns * 36,
    )(q, qn, qt, g, gt, kn, v, low, high, mask, q_row, k_row)
    from_high = shift(to_low, -1)
    from_low = shift(to_high, 1)
    gain = total_over("dp", total_over("seq", gain))[0]
    k_grad, v_grad = call(
        finish,
        grid,
        [turned, turned_pair, turned_pair, turned_pair, pl.BlockSpec((width, 1), lambda j: (0, 0))],
        [flat, flat],
        [flat_shape, flat_shape],
        rows * columns * 40,
    )(kt, own, from_low, from_high, k_gain[:, None])
    return (
        out[None],
        q_grad[None],
        k_grad[None],
        v_grad[None],
        gain,
        gain * q_gain / k_gain,
    )


def solution(mesh):
    tokens = P("dp", "seq", None)
    return jax.shard_map(
        shards,
        mesh=mesh,
        in_specs=(tokens, tokens, tokens, tokens, P(), P(), P(), P()),
        out_specs=(tokens, tokens, tokens, tokens, P(), P()),
        check_vma=False,
    )
```

time: 190 us -> 81.7 us (0.43)
  blocking collectives: 109 us -> 23.6 us
  local copies, waits for them, and re-layouts: 23.5 us -> 10.1 us
  other arithmetic: 12.7 us -> 0.74 us
  matrix products: 10.8 us -> 0 us
  Pallas kernels: 0 us -> 10.5 us
  starting transfers between devices: 16.9 us -> 24.5 us
  waiting for transfers between devices: 14.8 us -> 11 us
    psum x1 -> x0, blocking collectives: 109 us -> none  [shards(): gain_total = lax.psum(gain_terms, ('dp', 'seq'))]
    all_to_all x0 -> x1, blocking collectives: none -> 23.6 us  [total_over(): return jnp.sum(lax.all_to_all(spread, axis, 0, 0), axis=0)]
    dot_general x6 -> x0, matrix products: 10.8 us -> none  [the longest x1 3.19 us: shards(): jnp.einsum('hqk,khd->qhd', dscore, window[0], preferred_element_type=jnp....]
    pallas_call x0 -> x3, Pallas kernels: none -> 10.5 us  [the longest x1 7.33 us: shards(): call(attend, grid, [flat, flat, turned, flat, turned, flat, flat, pair, p...]
    ppermute x4, waiting for transfers between devices: 14.8 us -> 4.67 us  [shift(): return lax.ppermute(block, 'seq', route)]
    all_to_all x0 -> x1, starting transfers between devices: none -> 10 us  [total_over(): return jnp.sum(lax.all_to_all(spread, axis, 0, 0), axis=0)]
    all_to_all x0 -> x1, waiting for transfers between devices: none -> 6.34 us  [total_over(): return jnp.sum(lax.all_to_all(spread, axis, 0, 0), axis=0)]
    another operation x3 -> x2, local copies, waits for them, and re-layouts: 5.29 us -> 0.11 us  [window_mask(): return jnp.repeat(jnp.stack(rows, axis=1), TILE, axis=2)]
  transfers between devices with their start and end apart: 4 -> 5, of which waited for: 3 -> 3; matrix products, arithmetic and copies ran while one was open for 8% -> 3% of each run, Pallas kernels for 0% -> 1%
where the time goes in v1:
time: 81.7 us; the launch traced here: 81.2 us
  starting transfers between devices  24.5 us (30%)
  blocking collectives  23.6 us (29%)
  waiting for transfers between devices  11 us (13%)
  Pallas kernels  10.5 us (13%)
  local copies, waits for them, and re-layouts  10.1 us (12%)
  between operations  0.82 us (1%)
    all_to_all x1, blocking collectives, total_over(): return jnp.sum(lax.all_to_all(spread, axis, 0, 0), axis=0)  23.6 us
    ppermute x4, starting transfers between devices, shift(): return lax.ppermute(block, 'seq', route)  14.5 us
    all_to_all x1, starting transfers between devices, total_over(): return jnp.sum(lax.all_to_all(spread, axis, 0, 0), axis=0)  10 us
    pallas_call x1, Pallas kernels, shards(): call(attend, grid, [flat, flat, turned, flat, turned, flat, flat, pair, p...  7.33 us
    unnamed x29, local copies, waits for them, and re-layouts  6.47 us
    all_to_all x1, waiting for transfers between devices, total_over(): return jnp.sum(lax.all_to_all(spread, axis, 0, 0), axis=0)  6.34 us
    ppermute x4, waiting for transfers between devices, shift(): return lax.ppermute(block, 'seq', route)  4.67 us
    pallas_call x1, Pallas kernels, shards(): call(finish, grid, [turned, turned_pair, turned_pair, turned_pair, pl.Blo...  2.04 us
  transfers between devices with their start and end apart: 5, of which 3 were waited for; matrix products, arithmetic and copies ran while one was open for 3% of the time, Pallas kernels for 1%

profile of v1, /device:TPU:1, one launch (start us, length us, event | category | flops | bytes accessed | tf_op | source)
XLA Modules:
  0.0 81.2 jit_solution(11352911592406537441)
XLA Ops:
  0.7 1.9 %constant_dynamic-update-slice_fusion.1 = bf16[2,128,1536]{2,1,0:T(8,128)(2,1)} fusion(bf16[1,128,1536]{2,1,0:T(8,128)(2,1)} %param.9), kind=kLoop, calls=%fused_computation.6 | loop fusion | bytes 786432
  2.6 1.8 %constant_dynamic-update-slice_fusion = bf16[2,128,1536]{2,1,0:T(8,128)(2,1)} fusion(bf16[2,128,1536]{2,1,0:T(8,128)(2,1)} %constant_dynamic-update-slice_fusion.1, bf16[1,128,1536]{2,1,0:T(8,128)(2,1)} %param.10), kind=kLoop, calls=%fused_computation.5 | loop fusion | bytes 786432 | tf_op jit(solution)/shard_map/concatenate | solution.py:189
  4.4 4.5 %collective-permute-start = (bf16[2,128,1536]{2,1,0:T(8,128)(2,1)}, bf16[2,128,1536]{2,1,0:T(8,128)(2,1)S(1)}, u32[]{:S(2)}, u32[]{:S(2)}) collective-permute-start(bf16[2,128,1536]{2,1,0:T(8,128)(2,1)} %constant_dynamic-update-slice_fusion), channel_id=1, source_target_pairs={{0,1},{1,2},{2,3},{3,4},{4,5},{5,6},{6,7},{7,8},{8,9},{9,10},{10,1... | collective-permute-start | bytes 2359304 | tf_op jit(solution)/shard_map/ppermute | solution.py:29
  8.9 5.6 %collective-permute-start.1 = (bf16[2,128,1536]{2,1,0:T(8,128)(2,1)}, bf16[2,128,1536]{2,1,0:T(8,128)(2,1)S(1)}, u32[]{:S(2)}, u32[]{:S(2)}) collective-permute-start(bf16[2,128,1536]{2,1,0:T(8,128)(2,1)} %constant_dynamic-update-slice_fusion), channel_id=1, source_target_pairs={{1,0},{2,1},{3,2},{4,3},{5,4},{6,5},{7,6},{8,7},{9,8},{10,9},{11,1... | collective-permute-start | bytes 2359304 | tf_op jit(solution)/shard_map/ppermute | solution.py:29
  14.9 0.1 copy.26
  15.1 0.7 reshape.59.refs_9_
  15.8 1.1 %shard_map.127 = (bf16[128,1536]{1,0:T(8,128)(2,1)S(1)}, bf16[1536,128]{1,0:T(8,128)(2,1)S(1)}, bf16[1536,128]{1,0:T(8,128)(2,1)S(1)}, bf16[128,1536]{1,0:T(8,128)(2,1)S(1)}, bf16[1536,128]{1,0:T(8,128)(2,1)S(1)}) custom-call(bf16[128,1536]{1,0:T(8,128)(2,1)S(1)} %bitcast.26, bf16[128,1536]{1,0:T(8,128)(2,1)S(1)} %bitcast.24, ...), custom_call_target="tpu_custom_call" | custom-call | flops 7864320 | bytes 4194304 | tf_op jit(solution)/shard_map/pallas_call | solution.py:214
  17.0 0.7 copy-done.7
  17.7 0.4 collective-permute-done.refs_7_
  18.1 4.3 %collective-permute-done.1.refs_8_ = bf16[2,128,1536]{2,1,0:T(8,128)(2,1)S(1)} collective-permute-done((bf16[2,128,1536]{2,1,0:T(8,128)(2,1)}, bf16[2,128,1536]{2,1,0:T(8,128)(2,1)S(1)}, u32[]{:S(2)}, u32[]{:S(2)}) %collective-permute-start.1) | collective-permute-done | bytes 786464 | tf_op jit(solution)/shard_map/ppermute | solution.py:29
  22.4 0.9 %copy-done.5 = bf16[2,128,1536]{2,1,0:T(8,128)(2,1)} copy-done((bf16[2,128,1536]{2,1,0:T(8,128)(2,1)}, bf16[2,128,1536]{2,1,0:T(8,128)(2,1)S(1)}, u32[]{:S(2)}) %copy-start.5) | copy-done | bytes 786456
  23.3 1.1 %copy-done.6 = bf16[2,128,1536]{2,1,0:T(8,128)(2,1)S(1)} copy-done((bf16[2,128,1536]{2,1,0:T(8,128)(2,1)S(1)}, bf16[2,128,1536]{2,1,0:T(8,128)(2,1)}, u32[]{:S(2)}) %copy-start.6) | copy-done | bytes 786456
  24.4 0.8 copy-done.9
  25.2 7.3 %shard_map.128 = (bf16[128,1536]{1,0:T(8,128)(2,1)}, bf16[128,1536]{1,0:T(8,128)(2,1)}, f32[2,1536,128]{2,1,0:T(8,128)S(1)}, bf16[2,1536,128]{2,1,0:T(8,128)(2,1...) custom-call(bf16[128,1536]{1,0:T(8,128)(2,1)S(1)} %bitcast.27, bf16[128,1536]{1,0:T(8,128)(2,1)S(1)} %get-tuple-element.19.refs_1_, ...), custom_call_target="tpu_custom_call" | custom-call | flops 905969664 | bytes 4194304 | tf_op jit(solution)/shard_map/pallas_call | solution.py:222
  32.5 1.9 %collective-permute-start.2 = (bf16[2,1536,128]{2,1,0:T(8,128)(2,1)}, bf16[2,1536,128]{2,1,0:T(8,128)(2,1)S(1)}, u32[]{:S(2)}, u32[]{:S(2)}) collective-permute-start(bf16[2,1536,128]{2,1,0:T(8,128)(2,1)} %get-tuple-element.27), channel_id=1, source_target_pairs={{0,1},{1,2},{2,3},{3,4},{4,5},{5,6},{6,7},{7,8},{8,9},{9,10},{10,1... | collective-permute-start | bytes 2359304 | tf_op jit(solution)/shard_map/ppermute | solution.py:29
  34.5 2.5 %collective-permute-start.3 = (bf16[2,1536,128]{2,1,0:T(8,128)(2,1)}, bf16[2,1536,128]{2,1,0:T(8,128)(2,1)S(1)}, u32[]{:S(2)}, u32[]{:S(2)}) collective-permute-start(bf16[2,1536,128]{2,1,0:T(8,128)(2,1)} %get-tuple-element.28), channel_id=1, source_target_pairs={{1,0},{2,1},{3,2},{4,3},{5,4},{6,5},{7,6},{8,7},{9,8},{10,9},{11,1... | collective-permute-start | bytes 2359304 | tf_op jit(solution)/shard_map/ppermute | solution.py:29
  36.9 23.6 %all_to_all.10 = f32[64,1,128]{2,1,0:T(1,128)S(1)} all-to-all(f32[64,1,128]{2,1,0:T(1,128)S(1)} %broadcast_in_dim.56), channel_id=1, replica_groups=mesh['dp'=8,'seq'=64] {'seq'}, dimensions={0} | all-to-all | bytes 65536 | tf_op jit(solution)/shard_map/all_to_all | solution.py:179
  60.5 0.6 broadcast_in_dim.57
  61.1 10.0 %all-to-all-start.1 = ((f32[8,1,128]{2,1,0:T(1,128)}), f32[8,1,128]{2,1,0:T(1,128)S(1)}, u32[]{:S(2)}, u32[]{:S(2)}) async-start(f32[8,1,128]{2,1,0:T(1,128)} %broadcast_in_dim.57), calls=%async_computation.1 | async-start | bytes 8192 | tf_op jit(solution)/shard_map/all_to_all | solution.py:179
  71.2 0.1 copy.27.refs_4_
  71.3 6.3 %all-to-all-done.1 = f32[8,1,128]{2,1,0:T(1,128)S(1)} async-done(((f32[8,1,128]{2,1,0:T(1,128)}), f32[8,1,128]{2,1,0:T(1,128)S(1)}, u32[]{:S(2)}, u32[]{:S(2)}) %all-to-all-start.1) | async-done | bytes 4128 | tf_op jit(solution)/shard_map/all_to_all | solution.py:179
  77.7 0.5 multiply_divide_fusion
  78.2 1.0 %copy-done.8 = bf16[1536,128]{1,0:T(8,128)(2,1)S(1)} copy-done((bf16[1536,128]{1,0:T(8,128)(2,1)S(1)}, bf16[1536,128]{1,0:T(8,128)(2,1)}, u32[]{:S(2)}) %copy-start.8) | copy-done | bytes 393240
  79.2 2.0 %shard_map.129 = (bf16[128,1536]{1,0:T(8,128)(2,1)}, bf16[128,1536]{1,0:T(8,128)(2,1)}) custom-call(bf16[1536,128]{1,0:T(8,128)(2,1)S(1)} %copy-done.8, f32[2,1536,128]{2,1,0:T(8,128)S(1)} %get-tuple-element.26.refs_1_, bf16[2,1536,128]{2,1,0:T(8,128)(2,1)S(1)} %collective-permute-done.2.refs_2_, bf16[2,1536,128]{2,1,0:T(8,128)(2,1)S(1)} %collective-permute-done.3.refs_3_, ...), custom_call_target="tpu_custom_call" | custom-call | flops 7864320 | bytes 4194304 | tf_op jit(solution)/shard_map/pallas_call | solution.py:241
  (39 shorter events, 0.6 us)
Async XLA Ops:
  0.6 13.9 %copy-start = (s32[128,12]{0,1:T(8,128)S(1)}, s32[128,12]{0,1:T(8,128)}, u32[]{:S(2)}) copy-start(s32[128,12]{0,1:T(8,128)} %param.15) | copy-start | bytes 18436
  0.6 15.2 %copy-start.1 = (bf16[1,128,1536]{2,1,0:T(8,128)(2,1)S(1)}, bf16[1,128,1536]{2,1,0:T(8,128)(2,1)}, u32[]{:S(2)}) copy-start(bf16[1,128,1536]{2,1,0:T(8,128)(2,1)} %param.9) | copy-start | bytes 1179652
  0.7 22.7 %copy-start.2 = (bf16[1,128,1536]{2,1,0:T(8,128)(2,1)S(1)}, bf16[1,128,1536]{2,1,0:T(8,128)(2,1)}, u32[]{:S(2)}) copy-start(bf16[1,128,1536]{2,1,0:T(8,128)(2,1)} %param.10) | copy-start | bytes 1179652
  0.7 14.1 %copy-start.12 = (s32[12,5]{0,1:T(8,128)S(1)}, s32[12,5]{0,1:T(8,128)}, u32[]{:S(2)}) copy-start(s32[12,5]{0,1:T(8,128)} %param.14) | copy-start | bytes 724
  0.7 15.1 %copy-start.3 = (bf16[1,128,1536]{2,1,0:T(8,128)(2,1)S(1)}, bf16[1,128,1536]{2,1,0:T(8,128)(2,1)}, u32[]{:S(2)}) copy-start(bf16[1,128,1536]{2,1,0:T(8,128)(2,1)} %param.8) | copy-start | bytes 1179652
  0.7 15.1 %copy-start.4 = (bf16[1,128,1536]{2,1,0:T(8,128)(2,1)S(1)}, bf16[1,128,1536]{2,1,0:T(8,128)(2,1)}, u32[]{:S(2)}) copy-start(bf16[1,128,1536]{2,1,0:T(8,128)(2,1)} %param.11) | copy-start | bytes 1179652
  0.7 15.1 %copy-start.11 = (f32[128]{0:T(128)S(1)}, f32[128]{0:T(128)}, u32[]{:S(2)}) copy-start(f32[128]{0:T(128)} %param.12) | copy-start | bytes 1540
  0.7 15.1 %copy-start.10 = (f32[128]{0:T(128)S(1)}, f32[128]{0:T(128)}, u32[]{:S(2)}) copy-start(f32[128]{0:T(128)} %param.13) | copy-start | bytes 1540
  4.4 13.7 %collective-permute-start = (bf16[2,128,1536]{2,1,0:T(8,128)(2,1)}, bf16[2,128,1536]{2,1,0:T(8,128)(2,1)S(1)}, u32[]{:S(2)}, u32[]{:S(2)}) collective-permute-start(bf16[2,128,1536]{2,1,0:T(8,128)(2,1)} %constant_dynamic-update-slice_fusion), channel_id=1, source_target_pairs={{0,1},{1,2},{2,3},{3,4},{4,5},{5,6},{6,7},{7,8},{8,9},{9,10},{10,1... | collective-permute-start | bytes 2359304 | tf_op jit(solution)/shard_map/ppermute | solution.py:29
  8.9 13.5 %collective-permute-start.1 = (bf16[2,128,1536]{2,1,0:T(8,128)(2,1)}, bf16[2,128,1536]{2,1,0:T(8,128)(2,1)S(1)}, u32[]{:S(2)}, u32[]{:S(2)}) collective-permute-start(bf16[2,128,1536]{2,1,0:T(8,128)(2,1)} %constant_dynamic-update-slice_fusion), channel_id=1, source_target_pairs={{1,0},{2,1},{3,2},{4,3},{5,4},{6,5},{7,6},{8,7},{9,8},{10,9},{11,1... | collective-permute-start | bytes 2359304 | tf_op jit(solution)/shard_map/ppermute | solution.py:29
  17.0 0.7 copy-start.7
  22.4 0.9 %copy-start.5 = (bf16[2,128,1536]{2,1,0:T(8,128)(2,1)}, bf16[2,128,1536]{2,1,0:T(8,128)(2,1)S(1)}, u32[]{:S(2)}) copy-start(bf16[2,128,1536]{2,1,0:T(8,128)(2,1)S(1)} %collective-permute-done.1.refs_8_) | copy-start | bytes 2359300
  23.3 1.1 %copy-start.6 = (bf16[2,128,1536]{2,1,0:T(8,128)(2,1)S(1)}, bf16[2,128,1536]{2,1,0:T(8,128)(2,1)}, u32[]{:S(2)}) copy-start(bf16[2,128,1536]{2,1,0:T(8,128)(2,1)} %copy-done.5) | copy-start | bytes 2359300
  24.4 0.8 copy-start.9
  32.5 45.6 %collective-permute-start.2 = (bf16[2,1536,128]{2,1,0:T(8,128)(2,1)}, bf16[2,1536,128]{2,1,0:T(8,128)(2,1)S(1)}, u32[]{:S(2)}, u32[]{:S(2)}) collective-permute-start(bf16[2,1536,128]{2,1,0:T(8,128)(2,1)} %get-tuple-element.27), channel_id=1, source_target_pairs={{0,1},{1,2},{2,3},{3,4},{4,5},{5,6},{6,7},{7,8},{8,9},{9,10},{10,1... | collective-permute-start | bytes 2359304 | tf_op jit(solution)/shard_map/ppermute | solution.py:29
  34.5 43.7 %collective-permute-start.3 = (bf16[2,1536,128]{2,1,0:T(8,128)(2,1)}, bf16[2,1536,128]{2,1,0:T(8,128)(2,1)S(1)}, u32[]{:S(2)}, u32[]{:S(2)}) collective-permute-start(bf16[2,1536,128]{2,1,0:T(8,128)(2,1)} %get-tuple-element.28), channel_id=1, source_target_pairs={{1,0},{2,1},{3,2},{4,3},{5,4},{6,5},{7,6},{8,7},{9,8},{10,9},{11,1... | collective-permute-start | bytes 2359304 | tf_op jit(solution)/shard_map/ppermute | solution.py:29
  61.1 16.5 %all-to-all-start.1 = ((f32[8,1,128]{2,1,0:T(1,128)}), f32[8,1,128]{2,1,0:T(1,128)S(1)}, u32[]{:S(2)}, u32[]{:S(2)}) async-start(f32[8,1,128]{2,1,0:T(1,128)} %broadcast_in_dim.57), calls=%async_computation.1 | async-start | bytes 8192 | tf_op jit(solution)/shard_map/all_to_all | solution.py:179
  77.7 3.6 %copy-start.13 = (f32[128]{0:T(128)}, f32[128]{0:T(128)S(1)}, u32[]{:S(2)}) copy-start(f32[128]{0:T(128)S(1)} %reduce_sum.29) | copy-start | bytes 1540
  78.2 1.0 %copy-start.8 = (bf16[1536,128]{1,0:T(8,128)(2,1)S(1)}, bf16[1536,128]{1,0:T(8,128)(2,1)}, u32[]{:S(2)}) copy-start(bf16[1536,128]{1,0:T(8,128)(2,1)} %copy-done.7) | copy-start | bytes 1179652

commit v2 on v0

v2 whole, which is shorter than its diff:
```python
import math

import jax
import jax.numpy as jnp
from jax import lax
from jax.experimental import pallas as pl
from jax.experimental.pallas import tpu as pltpu
from jax.sharding import PartitionSpec as P

TILE = 64
REACH = 2
EPS = 1e-06
GROUP = 6
STEP = 3
NT = (((1,), (1,)), ((), ()))
NN = (((1,), (0,)), ((), ()))
F32 = jnp.float32
BF16 = jnp.bfloat16


def dot(a, b, dims):
    return lax.dot_general(a, b, dims, preferred_element_type=F32)


def inverse_spread(rows, axis):
    return lax.rsqrt(jnp.mean(rows * rows, axis=axis, keepdims=True) + EPS)


def swap(block, parity):
    size = lax.axis_size("seq")
    route = [(i, i + 1 if i % 2 == parity else i - 1) for i in range(size)]
    return lax.ppermute(block, "seq", [(i, j) for i, j in route if 0 <= j < size])


def head_columns(ref, width):
    return [slice(h * width, (h + 1) * width) for h in range(ref.shape[-1] // width)]


def window_mask(offsets_t, counts_t, position, t, rows):
    slots, heads = offsets_t.shape
    ntiles = counts_t.shape[1]
    tiles = rows // TILE
    lane = lax.broadcasted_iota(jnp.int32, (heads, 3 * rows), 1)
    side = 1 - 2 * lax.rem(position, 2)
    block = (lax.div(lane, rows) - 1) * side
    slot = block * tiles + lax.div(lax.rem(lane, rows), TILE) - t + REACH
    diagonal = lax.broadcasted_iota(jnp.int32, (heads, heads), 0) == lax.broadcasted_iota(
        jnp.int32, (heads, heads), 1
    )
    rank = jnp.zeros((heads, 3 * rows), F32)
    for s in range(slots):
        row = jnp.broadcast_to(offsets_t[s : s + 1, :], (heads, heads)).astype(F32)
        own = jnp.sum(jnp.where(diagonal, row, 0.0), axis=1, keepdims=True)
        rank = rank + jnp.where(own == slot.astype(F32), float(s), 0.0)
    here = position * tiles + t
    tile = lax.broadcasted_iota(jnp.int32, (heads, ntiles), 1)
    used = jnp.sum(jnp.where(tile == here, counts_t.astype(F32), 0.0), axis=1, keepdims=True)
    key = here + slot - REACH
    inside = (slot >= 0) & (slot < slots) & (key >= 0) & (key < ntiles)
    return jnp.where(inside & ((slot == REACH) | (rank < used)), 1.0, 0.0)


def masked_terms(scores, scale, mask_ref, h, first):
    rows, wide = scores.shape
    mask = jnp.concatenate(
        [
            jnp.broadcast_to(mask_ref[t, h : h + 1, first : first + wide], (TILE, wide))
            for t in range(rows // TILE)
        ],
        axis=0,
    )
    return jnp.exp2(scores * (scale * math.log2(math.e))) * mask


def normal(raw, gain):
    rows = raw.astype(F32)
    return (rows * inverse_spread(rows, 1) * gain).astype(BF16)


def prepare_kernel(
    q_ref, k_ref, v_ref, g_ref, offsets_ref, counts_ref, qgain_ref, kgain_ref,
    qn_ref, qt_ref, gt_ref, kn_ref, kt_ref, unit_ref, inverse_ref, own_ref, mask_ref,
):
    width = qgain_ref.shape[1]
    rows = q_ref.shape[0]
    scale = width ** (-0.5)
    q_gain = qgain_ref[...]
    k_gain = kgain_ref[...]
    position = lax.axis_index("seq")
    for t in range(rows // TILE):
        mask_ref[t] = window_mask(offsets_ref[...], counts_ref[...], position, t, rows)
    for h, cols in enumerate(head_columns(q_ref, width)):
        q = q_ref[:, cols].astype(F32)
        inverse = inverse_spread(q, 1)
        unit = q * inverse
        unit_ref[:, cols] = unit
        inverse_ref[:, cols] = jnp.broadcast_to(inverse, (rows, width))
        qn = (unit * q_gain).astype(BF16)
        qn_ref[:, cols] = qn
        qt_ref[cols, :] = qn.T
        grads = g_ref[:, cols]
        gt_ref[cols, :] = grads.T
        raw = k_ref[:, cols]
        kt_ref[cols, :] = raw.T
        kn = normal(raw, k_gain)
        kn_ref[:, cols] = kn
        own_ref[0, :, cols] = masked_terms(dot(qn, kn, NT), scale, mask_ref, h, rows)
        own_ref[1, :, cols] = dot(grads, v_ref[:, cols], NT)


def attend_kernel(
    qn_ref, g_ref, qt_ref, gt_ref, kn_ref, v_ref, nk_ref, nv_ref, fk_ref, fv_ref,
    mask_ref, unit_ref, inverse_ref, terms_ref, qgain_ref, kgain_ref,
    out_hbm, qgrad_hbm, own_hbm, far_hbm, near_hbm, sum_ref,
    out_ref, qgrad_ref, own_ref, to_far_ref, to_near_ref, sems,
):
    width = qgain_ref.shape[1]
    rows = qn_ref.shape[0]
    scale = width ** (-0.5)
    q_gain = qgain_ref[...]
    k_gain = kgain_ref[...]
    heads = head_columns(qn_ref, width)
    count = len(heads)
    copies = []

    def first_stage(h):
        cols = heads[h]
        k_far, k_near = normal(fk_ref[:, cols], k_gain), normal(nk_ref[:, cols], k_gain)
        v_far, v_near = fv_ref[:, cols], nv_ref[:, cols]
        keys = jnp.concatenate([k_far, kn_ref[:, cols], k_near], axis=0)
        scores = dot(qn_ref[:, cols], jnp.concatenate([k_far, k_near], axis=0), NT)
        dprob = dot(g_ref[:, cols], jnp.concatenate([v_far, v_near], axis=0), NT)
        return keys, scores, dprob

    def middle_stage(h, keys, scores, dprob):
        cols = heads[h]
        terms = [
            masked_terms(scores[:, :rows], scale, mask_ref, h, 0),
            terms_ref[0, :, cols],
            masked_terms(scores[:, rows:], scale, mask_ref, h, 2 * rows),
        ]
        inverse = 1.0 / jnp.sum(terms[0] + terms[1] + terms[2], axis=1, keepdims=True)
        probs = [term * inverse for term in terms]
        dprobs = [dprob[:, :rows], terms_ref[1, :, cols], dprob[:, rows:]]
        delta = jnp.sum(
            probs[0] * dprobs[0] + probs[1] * dprobs[1] + probs[2] * dprobs[2], axis=1, keepdims=True
        )
        dscore = [(p * (d - delta)).astype(BF16) for p, d in zip(probs, dprobs)]
        weights = [p.astype(BF16) for p in probs]
        return keys, jnp.concatenate(dscore, axis=1), jnp.concatenate(weights, axis=1)

    def last_stage(h, keys, dscore, weights, total_gain):
        cols = heads[h]
        vals = jnp.concatenate([fv_ref[:, cols], v_ref[:, cols], nv_ref[:, cols]], axis=0)
        grad_qn = dot(dscore, keys, NN) * scale
        out_ref[:, cols] = dot(weights, vals, NN).astype(BF16)
        key_t = dot(qt_ref[cols, :], dscore, NN) * scale
        val_t = dot(gt_ref[cols, :], weights, NN)
        own_ref[0, cols, :] = key_t[:, rows : 2 * rows]
        own_ref[1, cols, :] = val_t[:, rows : 2 * rows]
        to_far_ref[0, cols, :] = key_t[:, :rows].astype(BF16)
        to_far_ref[1, cols, :] = val_t[:, :rows].astype(BF16)
        to_near_ref[0, cols, :] = key_t[:, 2 * rows :].astype(BF16)
        to_near_ref[1, cols, :] = val_t[:, 2 * rows :].astype(BF16)
        unit = unit_ref[:, cols]
        product = grad_qn * unit
        mean = jnp.mean(product * q_gain, axis=1, keepdims=True)
        qgrad_ref[:, cols] = ((grad_qn * q_gain - unit * mean) * inverse_ref[:, cols]).astype(BF16)
        if h % GROUP == GROUP - 1:
            i = h // GROUP
            span = slice(heads[h - GROUP + 1].start, cols.stop)
            pairs = [
                (to_far_ref.at[:, span, :], far_hbm.at[:, span, :]),
                (to_near_ref.at[:, span, :], near_hbm.at[:, span, :]),
                (own_ref.at[:, span, :], own_hbm.at[:, span, :]),
                (out_ref.at[:, span], out_hbm.at[:, span]),
                (qgrad_ref.at[:, span], qgrad_hbm.at[:, span]),
            ]
            for j, (here, there) in enumerate(pairs):
                copy = pltpu.make_async_copy(here, there, sems.at[i, j])
                copy.start()
                copies.append(copy)
        return total_gain + product

    total_gain = jnp.zeros((rows, width), F32)
    ahead = first_stage(0)
    behind = None
    for h in range(count):
        now = ahead
        if h + 1 < count:
            ahead = first_stage(h + 1)
        now = middle_stage(h, *now)
        if behind is not None:
            total_gain = last_stage(h - 1, *behind, total_gain)
        behind = now
    total_gain = last_stage(count - 1, *behind, total_gain)
    sum_ref[...] = jnp.sum(total_gain, axis=0, keepdims=True)
    for copy in copies:
        copy.wait()


def finish_kernel(kt_ref, own_ref, far_ref, near_ref, gain_ref, kgrad_ref, vgrad_ref, inverse_ref):
    width = gain_ref.shape[1]
    row = gain_ref[...]
    inverse_ref[...] = 1.0 / row
    diagonal = lax.broadcasted_iota(jnp.int32, (width, width), 0) == lax.broadcasted_iota(
        jnp.int32, (width, width), 1
    )
    gain = jnp.sum(jnp.where(diagonal, jnp.broadcast_to(row, (width, width)), 0.0), axis=1, keepdims=True)
    for cols in head_columns(kgrad_ref, width):

        def total(i):
            return own_ref[i, cols, :] + far_ref[i, cols, :].astype(F32) + near_ref[i, cols, :].astype(F32)

        k = kt_ref[cols, :].astype(F32)
        inverse = inverse_spread(k, 0)
        unit = k * inverse
        scaled = total(0) * gain
        mean = jnp.mean(scaled * unit, axis=0, keepdims=True)
        kgrad_ref[:, cols] = ((scaled - unit * mean) * inverse).astype(BF16).T
        vgrad_ref[:, cols] = total(1).astype(BF16).T


def gain_kernel(parts_ref, q_ref, inverse_ref, qgain_ref, kgain_ref):
    total = jnp.sum(parts_ref[...], axis=0)
    qgain_ref[...] = total
    kgain_ref[...] = total * q_ref[...] * inverse_ref[...]


def call(body, out_shape, flops, in_specs=None, out_specs=None, scratch=(), grid=(), vmem=24):
    whole = pl.BlockSpec(memory_space=pltpu.VMEM)

    def run(*args):
        return pl.pallas_call(
            body,
            grid=grid,
            in_specs=in_specs or [whole] * len(args),
            out_specs=out_specs or [whole] * len(out_shape),
            out_shape=out_shape,
            scratch_shapes=scratch,
            compiler_params=pltpu.CompilerParams(vmem_limit_bytes=vmem * 1024 * 1024),
            cost_estimate=pl.CostEstimate(flops=flops, bytes_accessed=4 << 20, transcendentals=0),
        )(*args)

    return run


def spread_over(axis, vector):
    size = lax.axis_size(axis)
    return lax.all_to_all(jnp.broadcast_to(vector[None], (size,) + vector.shape), axis, 0, 0)


def shards(q_raw, k_raw, values, d_out, q_gain, k_gain, offsets, counts):
    rows, columns = q_raw.shape[1:]
    width = q_gain.shape[0]
    heads = offsets.shape[0]
    q, k, v, g = q_raw[0], k_raw[0], values[0], d_out[0]
    q_row, k_row = q_gain[None], k_gain[None]

    def like(*shape, dtype=BF16):
        return jax.ShapeDtypeStruct(shape, dtype)

    hbm = pl.BlockSpec(memory_space=pltpu.HBM)
    vmem = pl.BlockSpec(memory_space=pltpu.VMEM)
    products = 2 * rows * rows * columns
    flat = like(rows, columns)
    turned = like(columns, rows)
    part = like(2, columns, rows)
    own_part = like(2, columns, rows, dtype=F32)

    far_k, far_v = swap(k, 1), swap(v, 1)
    near_k, near_v = swap(k, 0), swap(v, 0)
    wide = like(rows, columns, dtype=F32)
    qn, qt, gt, kn, kt, unit, inverse, terms, mask = call(
        prepare_kernel,
        [flat, turned, turned, flat, turned, wide, wide, like(2, rows, columns, dtype=F32)]
        + [like(rows // TILE, heads, 3 * rows, dtype=F32)],
        2 * products,
    )(q, k, v, g, offsets.T, counts.T, q_row, k_row)
    out, q_grad, own, to_far, to_near, gain = call(
        attend_kernel,
        [flat, flat, own_part, part, part, like(1, width, dtype=F32)],
        16 * products,
        out_specs=[hbm] * 5 + [vmem],
        scratch=[
            pltpu.VMEM((rows, columns), BF16),
            pltpu.VMEM((rows, columns), BF16),
            pltpu.VMEM((2, columns, rows), F32),
            pltpu.VMEM((2, columns, rows), BF16),
            pltpu.VMEM((2, columns, rows), BF16),
            pltpu.SemaphoreType.DMA((heads // GROUP, 5)),
        ],
    )(qn, g, qt, gt, kn, v, near_k, near_v, far_k, far_v, mask, unit, inverse, terms, q_row, k_row)
    from_far = swap(to_far, 1)
    from_near = swap(to_near, 0)
    chunk = STEP * width
    flat_spec = pl.BlockSpec((rows, chunk), lambda j: (0, j))
    turned_spec = pl.BlockSpec((chunk, rows), lambda j: (j, 0))
    part_spec = pl.BlockSpec((2, chunk, rows), lambda j: (0, j, 0))
    row_spec = pl.BlockSpec((1, width), lambda j: (0, 0))
    k_grad, v_grad, inverse_gain = call(
        finish_kernel,
        [flat, flat, like(1, width, dtype=F32)],
        rows * columns * 40,
        in_specs=[turned_spec, part_spec, part_spec, part_spec, row_spec],
        out_specs=[flat_spec, flat_spec, row_spec],
        grid=(heads // STEP,),
    )(kt, own, from_far, from_near, k_row)
    parts = spread_over("seq", jnp.sum(spread_over("dp", gain), axis=0))
    gains = [like(1, width, dtype=F32)] * 2
    q_gain_grad, k_gain_grad = call(gain_kernel, gains, 0)(parts, q_row, inverse_gain)
    return (
        out[None],
        q_grad[None],
        k_grad[None],
        v_grad[None],
        q_gain_grad[0],
        k_gain_grad[0],
    )


def solution(mesh):
    tokens = P("dp", "seq", None)
    return jax.shard_map(
        shards,
        mesh=mesh,
        in_specs=(tokens, tokens, tokens, tokens, P(), P(), P(), P()),
        out_specs=(tokens, tokens, tokens, tokens, P(), P()),
        check_vma=False,
    )
```

time: 190 us -> 71 us (0.37)
  blocking collectives: 109 us -> 14.5 us
  local copies, waits for them, and re-layouts: 23.5 us -> 7.39 us
  starting transfers between devices: 16.9 us -> 32 us
  other arithmetic: 12.7 us -> 0.02 us
  matrix products: 10.8 us -> 0 us
  Pallas kernels: 0 us -> 8.59 us
  waiting for transfers between devices: 14.8 us -> 7.01 us
    psum x1 -> x0, blocking collectives: 109 us -> none  [shards(): gain_total = lax.psum(gain_terms, ('dp', 'seq'))]
    ppermute x4 -> x6, waiting for transfers between devices: 14.8 us -> 0.02 us  [swap(): lax.ppermute(block, 'seq', [(i, j) for i, j in route if 0 <= j < size])]
    all_to_all x0 -> x1, blocking collectives: none -> 14.5 us  [spread_over(): lax.all_to_all(jnp.broadcast_to(vector[None], (size,) + vector.shape), ax...]
    all_to_all x0 -> x1, starting transfers between devices: none -> 13.1 us  [spread_over(): lax.all_to_all(jnp.broadcast_to(vector[None], (size,) + vector.shape), ax...]
    dot_general x6 -> x0, matrix products: 10.8 us -> none  [the longest x1 3.19 us: shards(): jnp.einsum('hqk,khd->qhd', dscore, window[0], preferred_element_type=jnp....]
    pallas_call x0 -> x4, Pallas kernels: none -> 8.59 us  [run(): pl.pallas_call(body, grid=grid, in_specs=in_specs or [whole] * len(args),...]
    all_to_all x0 -> x1, waiting for transfers between devices: none -> 7 us  [spread_over(): lax.all_to_all(jnp.broadcast_to(vector[None], (size,) + vector.shape), ax...]
    another operation x3 -> x0, local copies, waits for them, and re-layouts: 5.29 us -> none  [the longest x2 5.06 us: shards(): jnp.stack([key_part, value_part])]
  transfers between devices with their start and end apart: 4 -> 7, of which waited for: 3 -> 1; matrix products, arithmetic and copies ran while one was open for 8% -> 1% of each run, Pallas kernels for 0% -> 4%
where the time goes in v2:
time: 71 us; the launch traced here: 70.3 us
  starting transfers between devices  32 us (45%)
  blocking collectives  14.5 us (20%)
  Pallas kernels  8.59 us (12%)
  local copies, waits for them, and re-layouts  7.39 us (10%)
  waiting for transfers between devices  7.01 us (10%)
  between operations  0.8 us (1%)
    ppermute x6, starting transfers between devices, swap(): lax.ppermute(block, 'seq', [(i, j) for i, j in route if 0 <= j < size])  18.9 us
    all_to_all x1, blocking collectives, spread_over(): lax.all_to_all(jnp.broadcast_to(vector[None], (size,) + vector.shape), ax...  14.5 us
    all_to_all x1, starting transfers between devices, spread_over(): lax.all_to_all(jnp.broadcast_to(vector[None], (size,) + vector.shape), ax...  13.1 us
    pallas_call x4, Pallas kernels, run(): pl.pallas_call(body, grid=grid, in_specs=in_specs or [whole] * len(args),...  8.59 us
    all_to_all x1, waiting for transfers between devices, spread_over(): lax.all_to_all(jnp.broadcast_to(vector[None], (size,) + vector.shape), ax...  7 us
    unnamed x24, local copies, waits for them, and re-layouts  6.76 us
  transfers between devices with their start and end apart: 7, of which 1 were waited for; matrix products, arithmetic and copies ran while one was open for 1% of the time, Pallas kernels for 4%

profile of v2, /device:TPU:1, one launch (start us, length us, event | category | flops | bytes accessed | tf_op | source)
XLA Modules:
  0.0 70.3 jit_solution(5382416314531183258)
XLA Ops:
  0.6 4.5 %collective-permute-start.2 = (bf16[128,1536]{1,0:T(8,128)(2,1)}, bf16[128,1536]{1,0:T(8,128)(2,1)S(1)}, u32[]{:S(2)}, u32[]{:S(2)}) collective-permute-start(bf16[128,1536]{1,0:T(8,128)(2,1)} %bitcast.23), channel_id=1, source_target_pairs={{1,2},{2,1},{3,4},{4,3},{5,6},{6,5},{7,8},{8,7},{9,10},{10,9},{11,... | collective-permute-start | bytes 1179656 | tf_op jit(solution)/shard_map/ppermute | solution.py:32
  5.2 5.0 %collective-permute-start = (bf16[128,1536]{1,0:T(8,128)(2,1)}, bf16[128,1536]{1,0:T(8,128)(2,1)S(1)}, u32[]{:S(2)}, u32[]{:S(2)}) collective-permute-start(bf16[128,1536]{1,0:T(8,128)(2,1)} %bitcast.24), channel_id=1, source_target_pairs={{0,1},{1,0},{2,3},{3,2},{4,5},{5,4},{6,7},{7,6},{8,9},{9,8},{10,11... | collective-permute-start | bytes 1179656 | tf_op jit(solution)/shard_map/ppermute | solution.py:32
  10.1 1.9 %collective-permute-start.3 = (bf16[128,1536]{1,0:T(8,128)(2,1)}, bf16[128,1536]{1,0:T(8,128)(2,1)S(1)}, u32[]{:S(2)}, u32[]{:S(2)}) collective-permute-start(bf16[128,1536]{1,0:T(8,128)(2,1)} %bitcast.16), channel_id=1, source_target_pairs={{1,2},{2,1},{3,4},{4,3},{5,6},{6,5},{7,8},{8,7},{9,10},{10,9},{11,... | collective-permute-start | bytes 1179656 | tf_op jit(solution)/shard_map/ppermute | solution.py:32
  12.0 1.9 %collective-permute-start.1 = (bf16[128,1536]{1,0:T(8,128)(2,1)}, bf16[128,1536]{1,0:T(8,128)(2,1)S(1)}, u32[]{:S(2)}, u32[]{:S(2)}) collective-permute-start(bf16[128,1536]{1,0:T(8,128)(2,1)} %bitcast.17), channel_id=1, source_target_pairs={{0,1},{1,0},{2,3},{3,2},{4,5},{5,4},{6,7},{7,6},{8,9},{9,8},{10,11... | collective-permute-start | bytes 1179656 | tf_op jit(solution)/shard_map/ppermute | solution.py:32
  14.0 1.0 %copy-done = bf16[1,128,1536]{2,1,0:T(8,128)(2,1)S(1)} copy-done((bf16[1,128,1536]{2,1,0:T(8,128)(2,1)S(1)}, bf16[1,128,1536]{2,1,0:T(8,128)(2,1)}, u32[]{:S(2)}) %copy-start) | copy-done | bytes 393240
  15.0 1.0 %copy-done.2 = bf16[1,128,1536]{2,1,0:T(8,128)(2,1)S(1)} copy-done((bf16[1,128,1536]{2,1,0:T(8,128)(2,1)S(1)}, bf16[1,128,1536]{2,1,0:T(8,128)(2,1)}, u32[]{:S(2)}) %copy-start.2) | copy-done | bytes 393240
  16.0 1.0 %copy-done.4 = bf16[1,128,1536]{2,1,0:T(8,128)(2,1)S(1)} copy-done((bf16[1,128,1536]{2,1,0:T(8,128)(2,1)S(1)}, bf16[1,128,1536]{2,1,0:T(8,128)(2,1)}, u32[]{:S(2)}) %copy-start.4) | copy-done | bytes 393240
  17.0 1.0 %copy-done.5 = bf16[1,128,1536]{2,1,0:T(8,128)(2,1)S(1)} copy-done((bf16[1,128,1536]{2,1,0:T(8,128)(2,1)S(1)}, bf16[1,128,1536]{2,1,0:T(8,128)(2,1)}, u32[]{:S(2)}) %copy-start.5) | copy-done | bytes 393240
  18.0 0.7 copy-done.6
  18.7 0.7 copy-done.7
  19.3 0.7 copy-done.9
  20.0 0.7 copy-done.11
  20.7 1.0 %shard_map.127 = (bf16[128,1536]{1,0:T(8,128)(2,1)S(1)}, bf16[1536,128]{1,0:T(8,128)(2,1)S(1)}, bf16[1536,128]{1,0:T(8,128)(2,1)S(1)}, bf16[128,1536]{1,0:T(8,12...) custom-call(bf16[128,1536]{1,0:T(8,128)(2,1)S(1)} %bitcast.22, ...), custom_call_target="tpu_custom_call" | custom-call | flops 100663296 | bytes 4194304 | tf_op jit(solution)/shard_map/pallas_call | solution.py:234
  21.7 0.1 copy-done.3
  21.8 4.1 %shard_map.128 = (bf16[128,1536]{1,0:T(8,128)(2,1)}, bf16[128,1536]{1,0:T(8,128)(2,1)}, f32[2,1536,128]{2,1,0:T(8,128)S(1)}, bf16[2,1536,128]{2,1,0:T(8,128)(2,1...) custom-call(bf16[128,1536]{1,0:T(8,128)(2,1)S(1)} %get-tuple-element.26.qn_ref, bf16[128,1536]{1,0:T(8,128)(2,1)S(1)} %bitcast.21, ...), custom_call_target="tpu_custom_call" | custom-call | flops 805306368 | bytes 4194304 | tf_op jit(solution)/shard_map/pallas_call | solution.py:234
  25.9 3.6 %collective-permute-start.4 = (bf16[2,1536,128]{2,1,0:T(8,128)(2,1)}, bf16[2,1536,128]{2,1,0:T(8,128)(2,1)S(1)}, u32[]{:S(2)}, u32[]{:S(2)}) collective-permute-start(bf16[2,1536,128]{2,1,0:T(8,128)(2,1)} %get-tuple-element.38), channel_id=1, source_target_pairs={{1,2},{2,1},{3,4},{4,3},{5,6},{6,5},{7,8},{8,7},{9,10},{10,9},{11,... | collective-permute-start | bytes 2359304 | tf_op jit(solution)/shard_map/ppermute | solution.py:32
  29.6 1.9 %collective-permute-start.5 = (bf16[2,1536,128]{2,1,0:T(8,128)(2,1)}, bf16[2,1536,128]{2,1,0:T(8,128)(2,1)S(1)}, u32[]{:S(2)}, u32[]{:S(2)}) collective-permute-start(bf16[2,1536,128]{2,1,0:T(8,128)(2,1)} %get-tuple-element.39), channel_id=1, source_target_pairs={{0,1},{1,0},{2,3},{3,2},{4,5},{5,4},{6,7},{7,6},{8,9},{9,8},{10,11... | collective-permute-start | bytes 2359304 | tf_op jit(solution)/shard_map/ppermute | solution.py:32
  31.5 14.5 %all_to_all.10 = f32[8,1,128]{2,1,0:T(1,128)S(1)} all-to-all(f32[8,1,128]{2,1,0:T(1,128)S(1)} %broadcast_in_dim.39), channel_id=1, replica_groups=mesh['dp'=8,'seq'=64] {'dp'}, dimensions={0} | all-to-all | bytes 8192 | tf_op jit(solution)/shard_map/all_to_all | solution.py:250
  46.0 0.6 broadcast_in_dim.40
  46.6 13.1 %all-to-all-start.1 = ((f32[64,1,128]{2,1,0:T(1,128)}), f32[64,1,128]{2,1,0:T(1,128)}, u32[]{:S(2)}, u32[]{:S(2)}) async-start(f32[64,1,128]{2,1,0:T(1,128)} %broadcast_in_dim.40), calls=%async_computation.1 | async-start | bytes 65536 | tf_op jit(solution)/shard_map/all_to_all | solution.py:250
  59.8 0.0 copy-start.8
  59.8 2.2 %shard_map.129 = (bf16[128,1536]{1,0:T(8,128)(2,1)}, bf16[128,1536]{1,0:T(8,128)(2,1)}, f32[1,128]{1,0:T(1,128)S(1)}) custom-call(bf16[1536,128]{1,0:T(8,128)(2,1)S(1)} %get-tuple-element.36.kt_ref, f32[2,1536,128]{2,1,0:T(8,128)S(1)} %get-tuple-element.37.own_ref, bf16[2,1536,128]{2,1,0:T(8,128)(2,1)S(1)} %collective-permute-done.4.far_ref, ...), custom_call_target="tpu_custom_call" | custom-call | flops 7864320 | bytes 4194304 | tf_op jit(solution)/shard_map/pallas_call | solution.py:234
  61.9 7.0 %all-to-all-done.1.parts_ref = f32[64,1,128]{2,1,0:T(1,128)} async-done(((f32[64,1,128]{2,1,0:T(1,128)}), f32[64,1,128]{2,1,0:T(1,128)}, u32[]{:S(2)}, u32[]{:S(2)}) %all-to-all-start.1) | async-done | bytes 32800 | tf_op jit(solution)/shard_map/all_to_all | solution.py:250
  68.9 1.3 %shard_map.130 = (f32[1,128]{1,0:T(1,128)}, f32[1,128]{1,0:T(1,128)}) custom-call(f32[64,1,128]{2,1,0:T(1,128)} %all-to-all-done.1.parts_ref, f32[1,128]{1,0:T(1,128)S(1)} %bitcast.29, f32[1,128]{1,0:T(1,128)S(1)} %get-tuple-element.43.inverse_ref), custom_call_target="tpu_custom_call" | custom-call | bytes 4194304 | tf_op jit(solution)/shard_map/pallas_call | solution.py:234
  (22 shorter events, 0.1 us)
Async XLA Ops:
  0.6 21.0 %collective-permute-start.2 = (bf16[128,1536]{1,0:T(8,128)(2,1)}, bf16[128,1536]{1,0:T(8,128)(2,1)S(1)}, u32[]{:S(2)}, u32[]{:S(2)}) collective-permute-start(bf16[128,1536]{1,0:T(8,128)(2,1)} %bitcast.23), channel_id=1, source_target_pairs={{1,2},{2,1},{3,4},{4,3},{5,6},{6,5},{7,8},{8,7},{9,10},{10,9},{11,... | collective-permute-start | bytes 1179656 | tf_op jit(solution)/shard_map/ppermute | solution.py:32
  5.2 16.5 %collective-permute-start = (bf16[128,1536]{1,0:T(8,128)(2,1)}, bf16[128,1536]{1,0:T(8,128)(2,1)S(1)}, u32[]{:S(2)}, u32[]{:S(2)}) collective-permute-start(bf16[128,1536]{1,0:T(8,128)(2,1)} %bitcast.24), channel_id=1, source_target_pairs={{0,1},{1,0},{2,3},{3,2},{4,5},{5,4},{6,7},{7,6},{8,9},{9,8},{10,11... | collective-permute-start | bytes 1179656 | tf_op jit(solution)/shard_map/ppermute | solution.py:32
  10.1 11.5 %collective-permute-start.3 = (bf16[128,1536]{1,0:T(8,128)(2,1)}, bf16[128,1536]{1,0:T(8,128)(2,1)S(1)}, u32[]{:S(2)}, u32[]{:S(2)}) collective-permute-start(bf16[128,1536]{1,0:T(8,128)(2,1)} %bitcast.16), channel_id=1, source_target_pairs={{1,2},{2,1},{3,4},{4,3},{5,6},{6,5},{7,8},{8,7},{9,10},{10,9},{11,... | collective-permute-start | bytes 1179656 | tf_op jit(solution)/shard_map/ppermute | solution.py:32
  12.0 9.6 %collective-permute-start.1 = (bf16[128,1536]{1,0:T(8,128)(2,1)}, bf16[128,1536]{1,0:T(8,128)(2,1)S(1)}, u32[]{:S(2)}, u32[]{:S(2)}) collective-permute-start(bf16[128,1536]{1,0:T(8,128)(2,1)} %bitcast.17), channel_id=1, source_target_pairs={{0,1},{1,0},{2,3},{3,2},{4,5},{5,4},{6,7},{7,6},{8,9},{9,8},{10,11... | collective-permute-start | bytes 1179656 | tf_op jit(solution)/shard_map/ppermute | solution.py:32
  14.0 1.0 %copy-start = (bf16[1,128,1536]{2,1,0:T(8,128)(2,1)S(1)}, bf16[1,128,1536]{2,1,0:T(8,128)(2,1)}, u32[]{:S(2)}) copy-start(bf16[1,128,1536]{2,1,0:T(8,128)(2,1)} %param.10) | copy-start | bytes 1179652
  15.0 1.0 %copy-start.2 = (bf16[1,128,1536]{2,1,0:T(8,128)(2,1)S(1)}, bf16[1,128,1536]{2,1,0:T(8,128)(2,1)}, u32[]{:S(2)}) copy-start(bf16[1,128,1536]{2,1,0:T(8,128)(2,1)} %param.11) | copy-start | bytes 1179652
  16.0 1.0 %copy-start.4 = (bf16[1,128,1536]{2,1,0:T(8,128)(2,1)S(1)}, bf16[1,128,1536]{2,1,0:T(8,128)(2,1)}, u32[]{:S(2)}) copy-start(bf16[1,128,1536]{2,1,0:T(8,128)(2,1)} %param.8) | copy-start | bytes 1179652
  17.0 1.0 %copy-start.5 = (bf16[1,128,1536]{2,1,0:T(8,128)(2,1)S(1)}, bf16[1,128,1536]{2,1,0:T(8,128)(2,1)}, u32[]{:S(2)}) copy-start(bf16[1,128,1536]{2,1,0:T(8,128)(2,1)} %param.9) | copy-start | bytes 1179652
  18.0 0.7 copy-start.6
  18.7 0.7 copy-start.7
  19.3 0.7 copy-start.9
  20.0 0.7 copy-start.11
  20.7 1.0 %copy-start.1 = (bf16[1,128,1536]{2,1,0:T(8,128)(2,1)S(1)}, bf16[1,128,1536]{2,1,0:T(8,128)(2,1)}, u32[]{:S(2)}) copy-start(bf16[1,128,1536]{2,1,0:T(8,128)(2,1)} %param.10) | copy-start | bytes 1179652
  20.7 1.1 %copy-start.3 = (bf16[1,128,1536]{2,1,0:T(8,128)(2,1)S(1)}, bf16[1,128,1536]{2,1,0:T(8,128)(2,1)}, u32[]{:S(2)}) copy-start(bf16[1,128,1536]{2,1,0:T(8,128)(2,1)} %param.11) | copy-start | bytes 1179652
  21.8 38.0 %copy-start.10 = (f32[128]{0:T(128)S(1)}, f32[128]{0:T(128)}, u32[]{:S(2)}) copy-start(f32[128]{0:T(128)} %param.13) | copy-start | bytes 1540
  25.9 33.8 %collective-permute-start.4 = (bf16[2,1536,128]{2,1,0:T(8,128)(2,1)}, bf16[2,1536,128]{2,1,0:T(8,128)(2,1)S(1)}, u32[]{:S(2)}, u32[]{:S(2)}) collective-permute-start(bf16[2,1536,128]{2,1,0:T(8,128)(2,1)} %get-tuple-element.38), channel_id=1, source_target_pairs={{1,2},{2,1},{3,4},{4,3},{5,6},{6,5},{7,8},{8,7},{9,10},{10,9},{11,... | collective-permute-start | bytes 2359304 | tf_op jit(solution)/shard_map/ppermute | solution.py:32
  29.6 30.2 %collective-permute-start.5 = (bf16[2,1536,128]{2,1,0:T(8,128)(2,1)}, bf16[2,1536,128]{2,1,0:T(8,128)(2,1)S(1)}, u32[]{:S(2)}, u32[]{:S(2)}) collective-permute-start(bf16[2,1536,128]{2,1,0:T(8,128)(2,1)} %get-tuple-element.39), channel_id=1, source_target_pairs={{0,1},{1,0},{2,3},{3,2},{4,5},{5,4},{6,7},{7,6},{8,9},{9,8},{10,11... | collective-permute-start | bytes 2359304 | tf_op jit(solution)/shard_map/ppermute | solution.py:32
  46.6 22.3 %all-to-all-start.1 = ((f32[64,1,128]{2,1,0:T(1,128)}), f32[64,1,128]{2,1,0:T(1,128)}, u32[]{:S(2)}, u32[]{:S(2)}) async-start(f32[64,1,128]{2,1,0:T(1,128)} %broadcast_in_dim.40), calls=%async_computation.1 | async-start | bytes 65536 | tf_op jit(solution)/shard_map/all_to_all | solution.py:250
  59.8 9.2 %copy-start.8 = (f32[128]{0:T(128)S(1)}, f32[128]{0:T(128)}, u32[]{:S(2)}) copy-start(f32[128]{0:T(128)} %param.12) | copy-start | bytes 1540

commit v3 on v2

--- a/solution.py
+++ b/solution.py
@@ -12,6 +12,8 @@
 EPS = 1e-06
 GROUP = 6
 STEP = 3
+IDLE = 5 * 10**9
+COMBINE = 30 * 10**9
 NT = (((1,), (1,)), ((), ()))
 NN = (((1,), (0,)), ((), ()))
 F32 = jnp.float32
@@ -36,7 +38,7 @@
     return [slice(h * width, (h + 1) * width) for h in range(ref.shape[-1] // width)]
 
 
-def window_mask(offsets_t, counts_t, position, t, rows):
+def window_mask(offsets_t, counts_t, identity, position, t, rows):
     slots, heads = offsets_t.shape
     ntiles = counts_t.shape[1]
     tiles = rows // TILE
@@ -44,13 +46,10 @@
     side = 1 - 2 * lax.rem(position, 2)
     block = (lax.div(lane, rows) - 1) * side
     slot = block * tiles + lax.div(lax.rem(lane, rows), TILE) - t + REACH
-    diagonal = lax.broadcasted_iota(jnp.int32, (heads, heads), 0) == lax.broadcasted_iota(
-        jnp.int32, (heads, heads), 1
-    )
     rank = jnp.zeros((heads, 3 * rows), F32)
     for s in range(slots):
         row = jnp.broadcast_to(offsets_t[s : s + 1, :], (heads, heads)).astype(F32)
-        own = jnp.sum(jnp.where(diagonal, row, 0.0), axis=1, keepdims=True)
+        own = jnp.sum(row * identity, axis=1, keepdims=True)
         rank = rank + jnp.where(own == slot.astype(F32), float(s), 0.0)
     here = position * tiles + t
     tile = lax.broadcasted_iota(jnp.int32, (heads, ntiles), 1)
@@ -77,9 +76,15 @@
     return (rows * inverse_spread(rows, 1) * gain).astype(BF16)
 
 
+def identity_kernel(identity_ref):
+    size = identity_ref.shape[0]
+    line = lax.broadcasted_iota(jnp.int32, (size, size), 0)
+    identity_ref[...] = jnp.where(line == lax.broadcasted_iota(jnp.int32, (size, size), 1), 1.0, 0.0)
+
+
 def prepare_kernel(
-    q_ref, k_ref, v_ref, g_ref, offsets_ref, counts_ref, qgain_ref, kgain_ref,
-    qn_ref, qt_ref, gt_ref, kn_ref, kt_ref, unit_ref, inverse_ref, own_ref, mask_ref,
+    q_ref, k_ref, v_ref, g_ref, offsets_ref, counts_ref, identity_ref, qgain_ref, kgain_ref,
+    qn_ref, qt_ref, gt_ref, kv_ref, kt_ref, unit_ref, inverse_ref, own_ref, mask_ref,
 ):
     width = qgain_ref.shape[1]
     rows = q_ref.shape[0]
@@ -87,8 +92,10 @@
     q_gain = qgain_ref[...]
     k_gain = kgain_ref[...]
     position = lax.axis_index("seq")
+    heads = offsets_ref.shape[1]
+    identity = identity_ref[:heads, :heads]
     for t in range(rows // TILE):
-        mask_ref[t] = window_mask(offsets_ref[...], counts_ref[...], position, t, rows)
+        mask_ref[t] = window_mask(offsets_ref[...], counts_ref[...], identity, position, t, rows)
     for h, cols in enumerate(head_columns(q_ref, width)):
         q = q_ref[:, cols].astype(F32)
         inverse = inverse_spread(q, 1)
@@ -103,14 +110,22 @@
         raw = k_ref[:, cols]
         kt_ref[cols, :] = raw.T
         kn = normal(raw, k_gain)
-        kn_ref[:, cols] = kn
+        vals = v_ref[:, cols]
+        kv_ref[0, :, cols] = kn
+        kv_ref[1, :, cols] = vals
         own_ref[0, :, cols] = masked_terms(dot(qn, kn, NT), scale, mask_ref, h, rows)
-        own_ref[1, :, cols] = dot(grads, v_ref[:, cols], NT)
+        own_ref[1, :, cols] = dot(grads, vals, NT)
+
+
+def far_kernel(k_ref, gain_ref, kn_ref):
+    gain = gain_ref[...]
+    for cols in head_columns(k_ref, gain_ref.shape[1]):
+        kn_ref[:, cols] = normal(k_ref[:, cols], gain)
 
 
 def attend_kernel(
-    qn_ref, g_ref, qt_ref, gt_ref, kn_ref, v_ref, nk_ref, nv_ref, fk_ref, fv_ref,
-    mask_ref, unit_ref, inverse_ref, terms_ref, qgain_ref, kgain_ref,
+    qn_ref, g_ref, qt_ref, gt_ref, kv_ref, near_ref, fk_ref, fv_ref,
+    mask_ref, unit_ref, inverse_ref, terms_ref, qgain_ref,
     out_hbm, qgrad_hbm, own_hbm, far_hbm, near_hbm, sum_ref,
     out_ref, qgrad_ref, own_ref, to_far_ref, to_near_ref, sems,
 ):
@@ -118,16 +133,15 @@
     rows = qn_ref.shape[0]
     scale = width ** (-0.5)
     q_gain = qgain_ref[...]
-    k_gain = kgain_ref[...]
     heads = head_columns(qn_ref, width)
     count = len(heads)
     copies = []
 
     def first_stage(h):
         cols = heads[h]
-        k_far, k_near = normal(fk_ref[:, cols], k_gain), normal(nk_ref[:, cols], k_gain)
-        v_far, v_near = fv_ref[:, cols], nv_ref[:, cols]
-        keys = jnp.concatenate([k_far, kn_ref[:, cols], k_near], axis=0)
+        k_far, k_near = fk_ref[:, cols], near_ref[0, :, cols]
+        v_far, v_near = fv_ref[:, cols], near_ref[1, :, cols]
+        keys = jnp.concatenate([k_far, kv_ref[0, :, cols], k_near], axis=0)
         scores = dot(qn_ref[:, cols], jnp.concatenate([k_far, k_near], axis=0), NT)
         dprob = dot(g_ref[:, cols], jnp.concatenate([v_far, v_near], axis=0), NT)
         return keys, scores, dprob
@@ -151,7 +165,7 @@
 
     def last_stage(h, keys, dscore, weights, total_gain):
         cols = heads[h]
-        vals = jnp.concatenate([fv_ref[:, cols], v_ref[:, cols], nv_ref[:, cols]], axis=0)
+        vals = jnp.concatenate([fv_ref[:, cols], kv_ref[1, :, cols], near_ref[1, :, cols]], axis=0)
         grad_qn = dot(dscore, keys, NN) * scale
         out_ref[:, cols] = dot(weights, vals, NN).astype(BF16)
         key_t = dot(qt_ref[cols, :], dscore, NN) * scale
@@ -199,14 +213,11 @@
         copy.wait()
 
 
-def finish_kernel(kt_ref, own_ref, far_ref, near_ref, gain_ref, kgrad_ref, vgrad_ref, inverse_ref):
+def finish_kernel(kt_ref, own_ref, far_ref, near_ref, identity_ref, gain_ref, kgrad_ref, vgrad_ref, inverse_ref):
     width = gain_ref.shape[1]
     row = gain_ref[...]
     inverse_ref[...] = 1.0 / row
-    diagonal = lax.broadcasted_iota(jnp.int32, (width, width), 0) == lax.broadcasted_iota(
-        jnp.int32, (width, width), 1
-    )
-    gain = jnp.sum(jnp.where(diagonal, jnp.broadcast_to(row, (width, width)), 0.0), axis=1, keepdims=True)
+    gain = jnp.sum(row * identity_ref[...], axis=1, keepdims=True)
     for cols in head_columns(kgrad_ref, width):
 
         def total(i):
@@ -219,6 +230,10 @@
         mean = jnp.mean(scaled * unit, axis=0, keepdims=True)
         kgrad_ref[:, cols] = ((scaled - unit * mean) * inverse).astype(BF16).T
         vgrad_ref[:, cols] = total(1).astype(BF16).T
+
+
+def combine_kernel(parts_ref, spread_ref):
+    spread_ref[...] = jnp.broadcast_to(jnp.sum(parts_ref[...], axis=0, keepdims=True), spread_ref.shape)
 
 
 def gain_kernel(parts_ref, q_ref, inverse_ref, qgain_ref, kgain_ref):
@@ -245,9 +260,12 @@
     return run
 
 
-def spread_over(axis, vector):
-    size = lax.axis_size(axis)
-    return lax.all_to_all(jnp.broadcast_to(vector[None], (size,) + vector.shape), axis, 0, 0)
+def over(axis, vector):
+    return jnp.broadcast_to(vector[None], (lax.axis_size(axis),) + vector.shape)
+
+
+def exchange(parts, axis):
+    return lax.all_to_all(parts, axis, 0, 0)
 
 
 def shards(q_raw, k_raw, values, d_out, q_gain, k_gain, offsets, counts):
@@ -269,14 +287,16 @@
     own_part = like(2, columns, rows, dtype=F32)
 
     far_k, far_v = swap(k, 1), swap(v, 1)
-    near_k, near_v = swap(k, 0), swap(v, 0)
+    (identity,) = call(identity_kernel, [like(width, width, dtype=F32)], IDLE)()
     wide = like(rows, columns, dtype=F32)
-    qn, qt, gt, kn, kt, unit, inverse, terms, mask = call(
+    qn, qt, gt, kv, kt, unit, inverse, terms, mask = call(
         prepare_kernel,
-        [flat, turned, turned, flat, turned, wide, wide, like(2, rows, columns, dtype=F32)]
-        + [like(rows // TILE, heads, 3 * rows, dtype=F32)],
+        [flat, turned, turned, like(2, rows, columns), turned, wide, wide]
+        + [like(2, rows, columns, dtype=F32), like(rows // TILE, heads, 3 * rows, dtype=F32)],
         2 * products,
-    )(q, k, v, g, offsets.T, counts.T, q_row, k_row)
+    )(q, k, v, g, offsets.T, counts.T, identity, q_row, k_row)
+    near = swap(kv, 0)
+    (far_k,) = call(far_kernel, [flat], 2 * IDLE)(far_k, k_row)
     out, q_grad, own, to_far, to_near, gain = call(
         attend_kernel,
         [flat, flat, own_part, part, part, like(1, width, dtype=F32)],
@@ -290,7 +310,7 @@
             pltpu.VMEM((2, columns, rows), BF16),
             pltpu.SemaphoreType.DMA((heads // GROUP, 5)),
         ],
-    )(qn, g, qt, gt, kn, v, near_k, near_v, far_k, far_v, mask, unit, inverse, terms, q_row, k_row)
+    )(qn, g, qt, gt, kv, near, far_k, far_v, mask, unit, inverse, terms, q_row)
     from_far = swap(to_far, 1)
     from_near = swap(to_near, 0)
     chunk = STEP * width
@@ -298,15 +318,18 @@
     turned_spec = pl.BlockSpec((chunk, rows), lambda j: (j, 0))
     part_spec = pl.BlockSpec((2, chunk, rows), lambda j: (0, j, 0))
     row_spec = pl.BlockSpec((1, width), lambda j: (0, 0))
+    square_spec = pl.BlockSpec((width, width), lambda j: (0, 0))
     k_grad, v_grad, inverse_gain = call(
         finish_kernel,
         [flat, flat, like(1, width, dtype=F32)],
         rows * columns * 40,
-        in_specs=[turned_spec, part_spec, part_spec, part_spec, row_spec],
+        in_specs=[turned_spec, part_spec, part_spec, part_spec, square_spec, row_spec],
         out_specs=[flat_spec, flat_spec, row_spec],
         grid=(heads // STEP,),
-    )(kt, own, from_far, from_near, k_row)
-    parts = spread_over("seq", jnp.sum(spread_over("dp", gain), axis=0))
+    )(kt, own, from_far, from_near, identity, k_row)
+    spread = [like(lax.axis_size("seq"), 1, width, dtype=F32)]
+    (spread,) = call(combine_kernel, spread, COMBINE)(exchange(over("dp", gain), "dp"))
+    parts = exchange(spread, "seq")
     gains = [like(1, width, dtype=F32)] * 2
     q_gain_grad, k_gain_grad = call(gain_kernel, gains, 0)(parts, q_row, inverse_gain)
     return (

time: 71 us -> 61.8 us (0.87)
  blocking collectives: 14.5 us -> 0 us
  starting transfers between devices: 32 us -> 39.7 us
  local copies, waits for them, and re-layouts: 7.39 us -> 2.99 us
  waiting for transfers between devices: 7.01 us -> 8.99 us
    all_to_all x1 -> x0, blocking collectives: 14.5 us -> none  [spread_over(): lax.all_to_all(jnp.broadcast_to(vector[None], (size,) + vector.shape), ax...]
    all_to_all x1 -> x2, starting transfers between devices: 13.1 us -> 23.3 us  [exchange(): return lax.all_to_all(parts, axis, 0, 0)]
    unnamed x24, local copies, waits for them, and re-layouts: 6.76 us -> 2.39 us
    ppermute x6 -> x5, starting transfers between devices: 18.9 us -> 16.5 us  [swap(): lax.ppermute(block, 'seq', [(i, j) for i, j in route if 0 <= j < size])]
    ppermute x6 -> x5, waiting for transfers between devices: 0.02 us -> 2.2 us  [swap(): lax.ppermute(block, 'seq', [(i, j) for i, j in route if 0 <= j < size])]
    all_to_all x1 -> x2, waiting for transfers between devices: 7 us -> 6.79 us  [exchange(): return lax.all_to_all(parts, axis, 0, 0)]
    pallas_call x4 -> x7, Pallas kernels: 8.59 us -> 8.78 us  [run(): pl.pallas_call(body, grid=grid, in_specs=in_specs or [whole] * len(args),...]
  transfers between devices with their start and end apart: 7 -> 7, of which waited for: 1 -> 3; matrix products, arithmetic and copies ran while one was open for 1% -> 0% of each run, Pallas kernels for 4% -> 6%
where the time goes in v3:
time: 61.8 us; the launch traced here: 61.4 us
  starting transfers between devices  39.7 us (64%)
  waiting for transfers between devices  8.99 us (15%)
  Pallas kernels  8.78 us (14%)
  local copies, waits for them, and re-layouts  2.99 us (5%)
  between operations  0.91 us (1%)
    all_to_all x2, starting transfers between devices, exchange(): return lax.all_to_all(parts, axis, 0, 0)  23.3 us
    ppermute x5, starting transfers between devices, swap(): lax.ppermute(block, 'seq', [(i, j) for i, j in route if 0 <= j < size])  16.5 us
    pallas_call x7, Pallas kernels, run(): pl.pallas_call(body, grid=grid, in_specs=in_specs or [whole] * len(args),...  8.78 us
    all_to_all x2, waiting for transfers between devices, exchange(): return lax.all_to_all(parts, axis, 0, 0)  6.79 us
    unnamed x24, local copies, waits for them, and re-layouts  2.39 us
    ppermute x5, waiting for transfers between devices, swap(): lax.ppermute(block, 'seq', [(i, j) for i, j in route if 0 <= j < size])  2.2 us
  transfers between devices with their start and end apart: 7, of which 3 were waited for; matrix products, arithmetic and copies ran while one was open for 0% of the time, Pallas kernels for 6%

profile of v3, /device:TPU:1, one launch (start us, length us, event | category | flops | bytes accessed | tf_op | source)
XLA Modules:
  0.0 61.4 jit_solution(10268510991499411781)
XLA Ops:
  0.6 4.5 %collective-permute-start.1 = (bf16[128,1536]{1,0:T(8,128)(2,1)}, bf16[128,1536]{1,0:T(8,128)(2,1)S(1)}, u32[]{:S(2)}, u32[]{:S(2)}) collective-permute-start(bf16[128,1536]{1,0:T(8,128)(2,1)} %bitcast.18), channel_id=1, source_target_pairs={{1,2},{2,1},{3,4},{4,3},{5,6},{6,5},{7,8},{8,7},{9,10},{10,9},{11,... | collective-permute-start | bytes 1179656 | tf_op jit(solution)/shard_map/ppermute | solution.py:34
  5.2 2.1 %collective-permute-start.2 = (bf16[128,1536]{1,0:T(8,128)(2,1)}, bf16[128,1536]{1,0:T(8,128)(2,1)S(1)}, u32[]{:S(2)}, u32[]{:S(2)}) collective-permute-start(bf16[128,1536]{1,0:T(8,128)(2,1)} %bitcast.20), channel_id=1, source_target_pairs={{1,2},{2,1},{3,4},{4,3},{5,6},{6,5},{7,8},{8,7},{9,10},{10,9},{11,... | collective-permute-start | bytes 1179656 | tf_op jit(solution)/shard_map/ppermute | solution.py:34
  7.3 0.0 copy-start.4
  7.4 1.0 %shard_map.128 = (bf16[128,1536]{1,0:T(8,128)(2,1)S(1)}, bf16[1536,128]{1,0:T(8,128)(2,1)S(1)}, bf16[1536,128]{1,0:T(8,128)(2,1)S(1)}, bf16[2,128,1536]{2,1,0:T(...) custom-call(bf16[128,1536]{1,0:T(8,128)(2,1)S(1)} %bitcast.17, ...), custom_call_target="tpu_custom_call" | custom-call | flops 100663296 | bytes 4194304 | tf_op jit(solution)/shard_map/pallas_call | solution.py:249
  8.4 4.1 %collective-permute-start = (bf16[2,128,1536]{2,1,0:T(8,128)(2,1)S(1)}, bf16[2,128,1536]{2,1,0:T(8,128)(2,1)S(1)}, u32[]{:S(2)}, u32[]{:S(2)}) collective-permute-start(bf16[2,128,1536]{2,1,0:T(8,128)(2,1)S(1)} %get-tuple-element.29.kv_ref), channel_id=1, source_target_pairs={{0,1},{1,0},{2,3},{3,2},{4,5},{5,4},{6,7},{7,6},{8,9},{9,8},{10,11... | collective-permute-start | bytes 2359304 | tf_op jit(solution)/shard_map/ppermute | solution.py:34
  12.5 0.0 collective-permute-done.1.k_ref
  12.5 0.3 shard_map.129.fk_ref
  12.8 2.2 %collective-permute-done.2.fv_ref = bf16[128,1536]{1,0:T(8,128)(2,1)S(1)} collective-permute-done((bf16[128,1536]{1,0:T(8,128)(2,1)}, bf16[128,1536]{1,0:T(8,128)(2,1)S(1)}, u32[]{:S(2)}, u32[]{:S(2)}) %collective-permute-start.2) | collective-permute-done | bytes 393248 | tf_op jit(solution)/shard_map/ppermute | solution.py:34
  15.0 3.9 %shard_map.130 = (bf16[128,1536]{1,0:T(8,128)(2,1)}, bf16[128,1536]{1,0:T(8,128)(2,1)}, f32[2,1536,128]{2,1,0:T(8,128)S(1)}, bf16[2,1536,128]{2,1,0:T(8,128)(2,1...) custom-call(bf16[128,1536]{1,0:T(8,128)(2,1)S(1)} %get-tuple-element.26.qn_ref, ...), custom_call_target="tpu_custom_call" | custom-call | flops 805306368 | bytes 4194304 | tf_op jit(solution)/shard_map/pallas_call | solution.py:249
  19.0 0.9 %copy-done.11 = bf16[2,1536,128]{2,1,0:T(8,128)(2,1)} copy-done((bf16[2,1536,128]{2,1,0:T(8,128)(2,1)}, bf16[2,1536,128]{2,1,0:T(8,128)(2,1)S(1)}, u32[]{:S(2)}) %copy-start.11) | copy-done | bytes 786456
  19.9 0.6 broadcast_in_dim.33
  20.5 10.0 %all-to-all-start = ((f32[8,1,128]{2,1,0:T(1,128)}), f32[8,1,128]{2,1,0:T(1,128)S(1)}, u32[]{:S(2)}, u32[]{:S(2)}) async-start(f32[8,1,128]{2,1,0:T(1,128)} %broadcast_in_dim.33), calls=%async_computation | async-start | bytes 8192 | tf_op jit(solution)/shard_map/all_to_all | solution.py:268
  30.5 3.9 %collective-permute-start.3 = (bf16[2,1536,128]{2,1,0:T(8,128)(2,1)}, bf16[2,1536,128]{2,1,0:T(8,128)(2,1)S(1)}, u32[]{:S(2)}, u32[]{:S(2)}) collective-permute-start(bf16[2,1536,128]{2,1,0:T(8,128)(2,1)} %get-tuple-element.38), channel_id=1, source_target_pairs={{1,2},{2,1},{3,4},{4,3},{5,6},{6,5},{7,8},{8,7},{9,10},{10,9},{11,... | collective-permute-start | bytes 2359304 | tf_op jit(solution)/shard_map/ppermute | solution.py:34
  34.5 1.9 %collective-permute-start.4 = (bf16[2,1536,128]{2,1,0:T(8,128)(2,1)}, bf16[2,1536,128]{2,1,0:T(8,128)(2,1)S(1)}, u32[]{:S(2)}, u32[]{:S(2)}) collective-permute-start(bf16[2,1536,128]{2,1,0:T(8,128)(2,1)} %copy-done.11), channel_id=1, source_target_pairs={{0,1},{1,0},{2,3},{3,2},{4,5},{5,4},{6,7},{7,6},{8,9},{9,8},{10,11... | collective-permute-start | bytes 2359304 | tf_op jit(solution)/shard_map/ppermute | solution.py:34
  36.4 0.6 all-to-all-done.parts_ref
  37.0 0.6 copy-done.6
  37.6 13.2 %all-to-all-start.1 = ((f32[64,1,128]{2,1,0:T(1,128)}), f32[64,1,128]{2,1,0:T(1,128)}, u32[]{:S(2)}, u32[]{:S(2)}) async-start(f32[64,1,128]{2,1,0:T(1,128)} %copy-done.6), calls=%async_computation.1 | async-start | bytes 65536 | tf_op jit(solution)/shard_map/all_to_all | solution.py:268
  50.9 0.0 collective-permute-done.3.far_ref
  50.9 0.0 collective-permute-done.4.near_ref
  50.9 0.0 copy-start.5
  50.9 0.8 %copy-done.5 = f32[128,128]{1,0:T(8,128)S(1)} copy-done((f32[128,128]{1,0:T(8,128)S(1)}, f32[128,128]{1,0:T(8,128)}, u32[]{:S(2)}) %copy-start.5) | copy-done | bytes 65560
  51.7 2.1 %shard_map.131 = (bf16[128,1536]{1,0:T(8,128)(2,1)}, bf16[128,1536]{1,0:T(8,128)(2,1)}, f32[1,128]{1,0:T(1,128)S(1)}) custom-call(bf16[1536,128]{1,0:T(8,128)(2,1)S(1)} %get-tuple-element.36.kt_ref, f32[2,1536,128]{2,1,0:T(8,128)S(1)} %get-tuple-element.37.own_ref, bf16[2,1536,128]{2,1,0:T(8,128)(2,1)S(1)} %collective-permute-done.3.far_ref, ...), custom_call_target="tpu_custom_call" | custom-call | flops 7864320 | bytes 4194304 | tf_op jit(solution)/shard_map/pallas_call | solution.py:249
  53.9 6.2 %all-to-all-done.1.parts_ref = f32[64,1,128]{2,1,0:T(1,128)} async-done(((f32[64,1,128]{2,1,0:T(1,128)}), f32[64,1,128]{2,1,0:T(1,128)}, u32[]{:S(2)}, u32[]{:S(2)}) %all-to-all-start.1) | async-done | bytes 32800 | tf_op jit(solution)/shard_map/all_to_all | solution.py:268
  60.1 1.3 %shard_map.133 = (f32[1,128]{1,0:T(1,128)}, f32[1,128]{1,0:T(1,128)}) custom-call(f32[64,1,128]{2,1,0:T(1,128)} %all-to-all-done.1.parts_ref, f32[1,128]{1,0:T(1,128)S(1)} %bitcast.25, f32[1,128]{1,0:T(1,128)S(1)} %get-tuple-element.43.inverse_ref), custom_call_target="tpu_custom_call" | custom-call | bytes 4194304 | tf_op jit(solution)/shard_map/pallas_call | solution.py:249
  (22 shorter events, 0.1 us)
Async XLA Ops:
  0.6 11.9 %collective-permute-start.1 = (bf16[128,1536]{1,0:T(8,128)(2,1)}, bf16[128,1536]{1,0:T(8,128)(2,1)S(1)}, u32[]{:S(2)}, u32[]{:S(2)}) collective-permute-start(bf16[128,1536]{1,0:T(8,128)(2,1)} %bitcast.18), channel_id=1, source_target_pairs={{1,2},{2,1},{3,4},{4,3},{5,6},{6,5},{7,8},{8,7},{9,10},{10,9},{11,... | collective-permute-start | bytes 1179656 | tf_op jit(solution)/shard_map/ppermute | solution.py:34
  5.2 2.2 %copy-start = (bf16[1,128,1536]{2,1,0:T(8,128)(2,1)S(1)}, bf16[1,128,1536]{2,1,0:T(8,128)(2,1)}, u32[]{:S(2)}) copy-start(bf16[1,128,1536]{2,1,0:T(8,128)(2,1)} %param.11) | copy-start | bytes 1179652
  5.2 2.2 %copy-start.1 = (bf16[1,128,1536]{2,1,0:T(8,128)(2,1)S(1)}, bf16[1,128,1536]{2,1,0:T(8,128)(2,1)}, u32[]{:S(2)}) copy-start(bf16[1,128,1536]{2,1,0:T(8,128)(2,1)} %param.8) | copy-start | bytes 1179652
  5.2 2.2 %copy-start.2 = (bf16[1,128,1536]{2,1,0:T(8,128)(2,1)S(1)}, bf16[1,128,1536]{2,1,0:T(8,128)(2,1)}, u32[]{:S(2)}) copy-start(bf16[1,128,1536]{2,1,0:T(8,128)(2,1)} %param.9) | copy-start | bytes 1179652
  5.2 2.2 %copy-start.3 = (bf16[1,128,1536]{2,1,0:T(8,128)(2,1)S(1)}, bf16[1,128,1536]{2,1,0:T(8,128)(2,1)}, u32[]{:S(2)}) copy-start(bf16[1,128,1536]{2,1,0:T(8,128)(2,1)} %param.10) | copy-start | bytes 1179652
  5.2 2.2 %copy-start.7 = (s32[128,12]{0,1:T(8,128)S(1)}, s32[128,12]{0,1:T(8,128)}, u32[]{:S(2)}) copy-start(s32[128,12]{0,1:T(8,128)} %param.15) | copy-start | bytes 18436
  5.2 2.2 %copy-start.8 = (f32[128]{0:T(128)S(1)}, f32[128]{0:T(128)}, u32[]{:S(2)}) copy-start(f32[128]{0:T(128)} %param.12) | copy-start | bytes 1540
  5.2 2.2 %copy-start.9 = (s32[12,5]{0,1:T(8,128)S(1)}, s32[12,5]{0,1:T(8,128)}, u32[]{:S(2)}) copy-start(s32[12,5]{0,1:T(8,128)} %param.14) | copy-start | bytes 724
  5.2 2.2 %copy-start.10 = (f32[128]{0:T(128)S(1)}, f32[128]{0:T(128)}, u32[]{:S(2)}) copy-start(f32[128]{0:T(128)} %param.13) | copy-start | bytes 1540
  5.2 9.8 %collective-permute-start.2 = (bf16[128,1536]{1,0:T(8,128)(2,1)}, bf16[128,1536]{1,0:T(8,128)(2,1)S(1)}, u32[]{:S(2)}, u32[]{:S(2)}) collective-permute-start(bf16[128,1536]{1,0:T(8,128)(2,1)} %bitcast.20), channel_id=1, source_target_pairs={{1,2},{2,1},{3,4},{4,3},{5,6},{6,5},{7,8},{8,7},{9,10},{10,9},{11,... | collective-permute-start | bytes 1179656 | tf_op jit(solution)/shard_map/ppermute | solution.py:34
  7.3 5.2 %copy-start.4 = (f32[128,128]{1,0:T(8,128)}, f32[128,128]{1,0:T(8,128)S(1)}, u32[]{:S(2)}) copy-start(f32[128,128]{1,0:T(8,128)S(1)} %shard_map.127.identity_ref) | copy-start | bytes 196612
  8.4 6.6 %collective-permute-start = (bf16[2,128,1536]{2,1,0:T(8,128)(2,1)S(1)}, bf16[2,128,1536]{2,1,0:T(8,128)(2,1)S(1)}, u32[]{:S(2)}, u32[]{:S(2)}) collective-permute-start(bf16[2,128,1536]{2,1,0:T(8,128)(2,1)S(1)} %get-tuple-element.29.kv_ref), channel_id=1, source_target_pairs={{0,1},{1,0},{2,3},{3,2},{4,5},{5,4},{6,7},{7,6},{8,9},{9,8},{10,11... | collective-permute-start | bytes 2359304 | tf_op jit(solution)/shard_map/ppermute | solution.py:34
  19.0 0.9 %copy-start.11 = (bf16[2,1536,128]{2,1,0:T(8,128)(2,1)}, bf16[2,1536,128]{2,1,0:T(8,128)(2,1)S(1)}, u32[]{:S(2)}) copy-start(bf16[2,1536,128]{2,1,0:T(8,128)(2,1)S(1)} %get-tuple-element.39) | copy-start | bytes 2359300
  20.5 16.5 %all-to-all-start = ((f32[8,1,128]{2,1,0:T(1,128)}), f32[8,1,128]{2,1,0:T(1,128)S(1)}, u32[]{:S(2)}, u32[]{:S(2)}) async-start(f32[8,1,128]{2,1,0:T(1,128)} %broadcast_in_dim.33), calls=%async_computation | async-start | bytes 8192 | tf_op jit(solution)/shard_map/all_to_all | solution.py:268
  30.5 20.3 %collective-permute-start.3 = (bf16[2,1536,128]{2,1,0:T(8,128)(2,1)}, bf16[2,1536,128]{2,1,0:T(8,128)(2,1)S(1)}, u32[]{:S(2)}, u32[]{:S(2)}) collective-permute-start(bf16[2,1536,128]{2,1,0:T(8,128)(2,1)} %get-tuple-element.38), channel_id=1, source_target_pairs={{1,2},{2,1},{3,4},{4,3},{5,6},{6,5},{7,8},{8,7},{9,10},{10,9},{11,... | collective-permute-start | bytes 2359304 | tf_op jit(solution)/shard_map/ppermute | solution.py:34
  34.5 16.4 %collective-permute-start.4 = (bf16[2,1536,128]{2,1,0:T(8,128)(2,1)}, bf16[2,1536,128]{2,1,0:T(8,128)(2,1)S(1)}, u32[]{:S(2)}, u32[]{:S(2)}) collective-permute-start(bf16[2,1536,128]{2,1,0:T(8,128)(2,1)} %copy-done.11), channel_id=1, source_target_pairs={{0,1},{1,0},{2,3},{3,2},{4,5},{5,4},{6,7},{7,6},{8,9},{9,8},{10,11... | collective-permute-start | bytes 2359304 | tf_op jit(solution)/shard_map/ppermute | solution.py:34
  37.0 0.6 %copy-start.6 = (f32[64,1,128]{2,1,0:T(1,128)}, f32[64,1,128]{2,1,0:T(1,128)S(1)}, u32[]{:S(2)}) copy-start(f32[64,1,128]{2,1,0:T(1,128)S(1)} %shard_map.132) | copy-start | bytes 98308
  37.6 22.4 %all-to-all-start.1 = ((f32[64,1,128]{2,1,0:T(1,128)}), f32[64,1,128]{2,1,0:T(1,128)}, u32[]{:S(2)}, u32[]{:S(2)}) async-start(f32[64,1,128]{2,1,0:T(1,128)} %copy-done.6), calls=%async_computation.1 | async-start | bytes 65536 | tf_op jit(solution)/shard_map/all_to_all | solution.py:268
  50.9 0.8 %copy-start.5 = (f32[128,128]{1,0:T(8,128)S(1)}, f32[128,128]{1,0:T(8,128)}, u32[]{:S(2)}) copy-start(f32[128,128]{1,0:T(8,128)} %copy-done.4) | copy-start | bytes 196612

commit v4 on v3

--- a/solution.py
+++ b/solution.py
@@ -11,7 +11,7 @@
 REACH = 2
 EPS = 1e-06
 GROUP = 6
-STEP = 3
+STEP = 6
 IDLE = 5 * 10**9
 COMBINE = 30 * 10**9
 NT = (((1,), (1,)), ((), ()))
@@ -123,11 +123,22 @@
         kn_ref[:, cols] = normal(k_ref[:, cols], gain)
 
 
+def side_kernel(qn_ref, g_ref, near_ref, fk_ref, mask_ref, gain_ref, terms_ref):
+    width = gain_ref.shape[1]
+    rows = qn_ref.shape[0]
+    scale = width ** (-0.5)
+    for h, cols in enumerate(head_columns(qn_ref, width)):
+        scores = dot(qn_ref[:, cols], jnp.concatenate([fk_ref[:, cols], near_ref[0, :, cols]], axis=0), NT)
+        terms_ref[0, :, cols] = masked_terms(scores[:, :rows], scale, mask_ref, h, 0)
+        terms_ref[1, :, cols] = masked_terms(scores[:, rows:], scale, mask_ref, h, 2 * rows)
+        terms_ref[2, :, cols] = dot(g_ref[:, cols], near_ref[1, :, cols], NT)
+
+
 def attend_kernel(
     qn_ref, g_ref, qt_ref, gt_ref, kv_ref, near_ref, fk_ref, fv_ref,
-    mask_ref, unit_ref, inverse_ref, terms_ref, qgain_ref,
-    out_hbm, qgrad_hbm, own_hbm, far_hbm, near_hbm, sum_ref,
-    out_ref, qgrad_ref, own_ref, to_far_ref, to_near_ref, sems,
+    side_ref, unit_ref, inverse_ref, terms_ref, qgain_ref,
+    out_hbm, qgrad_hbm, own_ref, far_hbm, near_hbm, spread_hbm,
+    out_ref, qgrad_ref, to_far_ref, to_near_ref, spread_ref, sems,
 ):
     width = qgain_ref.shape[1]
     rows = qn_ref.shape[0]
@@ -138,40 +149,31 @@
     copies = []
 
     def first_stage(h):
+        return (dot(g_ref[:, heads[h]], fv_ref[:, heads[h]], NT),)
+
+    def middle_stage(h, dprob):
         cols = heads[h]
-        k_far, k_near = fk_ref[:, cols], near_ref[0, :, cols]
-        v_far, v_near = fv_ref[:, cols], near_ref[1, :, cols]
-        keys = jnp.concatenate([k_far, kv_ref[0, :, cols], k_near], axis=0)
-        scores = dot(qn_ref[:, cols], jnp.concatenate([k_far, k_near], axis=0), NT)
-        dprob = dot(g_ref[:, cols], jnp.concatenate([v_far, v_near], axis=0), NT)
-        return keys, scores, dprob
-
-    def middle_stage(h, keys, scores, dprob):
-        cols = heads[h]
-        terms = [
-            masked_terms(scores[:, :rows], scale, mask_ref, h, 0),
-            terms_ref[0, :, cols],
-            masked_terms(scores[:, rows:], scale, mask_ref, h, 2 * rows),
-        ]
+        terms = [side_ref[0, :, cols], terms_ref[0, :, cols], side_ref[1, :, cols]]
         inverse = 1.0 / jnp.sum(terms[0] + terms[1] + terms[2], axis=1, keepdims=True)
         probs = [term * inverse for term in terms]
-        dprobs = [dprob[:, :rows], terms_ref[1, :, cols], dprob[:, rows:]]
+        dprobs = [dprob, terms_ref[1, :, cols], side_ref[2, :, cols]]
         delta = jnp.sum(
             probs[0] * dprobs[0] + probs[1] * dprobs[1] + probs[2] * dprobs[2], axis=1, keepdims=True
         )
         dscore = [(p * (d - delta)).astype(BF16) for p, d in zip(probs, dprobs)]
         weights = [p.astype(BF16) for p in probs]
-        return keys, jnp.concatenate(dscore, axis=1), jnp.concatenate(weights, axis=1)
-
-    def last_stage(h, keys, dscore, weights, total_gain):
+        return jnp.concatenate(dscore, axis=1), jnp.concatenate(weights, axis=1)
+
+    def last_stage(h, dscore, weights, total_gain):
         cols = heads[h]
+        keys = jnp.concatenate([fk_ref[:, cols], kv_ref[0, :, cols], near_ref[0, :, cols]], axis=0)
         vals = jnp.concatenate([fv_ref[:, cols], kv_ref[1, :, cols], near_ref[1, :, cols]], axis=0)
         grad_qn = dot(dscore, keys, NN) * scale
         out_ref[:, cols] = dot(weights, vals, NN).astype(BF16)
         key_t = dot(qt_ref[cols, :], dscore, NN) * scale
         val_t = dot(gt_ref[cols, :], weights, NN)
-        own_ref[0, cols, :] = key_t[:, rows : 2 * rows]
-        own_ref[1, cols, :] = val_t[:, rows : 2 * rows]
+        own_ref[0, cols, :] = key_t[:, rows : 2 * rows].astype(BF16)
+        own_ref[1, cols, :] = val_t[:, rows : 2 * rows].astype(BF16)
         to_far_ref[0, cols, :] = key_t[:, :rows].astype(BF16)
         to_far_ref[1, cols, :] = val_t[:, :rows].astype(BF16)
         to_near_ref[0, cols, :] = key_t[:, 2 * rows :].astype(BF16)
@@ -186,7 +188,6 @@
             pairs = [
                 (to_far_ref.at[:, span, :], far_hbm.at[:, span, :]),
                 (to_near_ref.at[:, span, :], near_hbm.at[:, span, :]),
-                (own_ref.at[:, span, :], own_hbm.at[:, span, :]),
                 (out_ref.at[:, span], out_hbm.at[:, span]),
                 (qgrad_ref.at[:, span], qgrad_hbm.at[:, span]),
             ]
@@ -208,20 +209,29 @@
             total_gain = last_stage(h - 1, *behind, total_gain)
         behind = now
     total_gain = last_stage(count - 1, *behind, total_gain)
-    sum_ref[...] = jnp.sum(total_gain, axis=0, keepdims=True)
+    sums = jnp.sum(total_gain, axis=0, keepdims=True)
+    spread_ref[...] = jnp.broadcast_to(sums[None], spread_ref.shape)
+    copies.append(pltpu.make_async_copy(spread_ref, spread_hbm, sems.at[count // GROUP, 0]))
+    copies[-1].start()
     for copy in copies:
         copy.wait()
 
 
-def finish_kernel(kt_ref, own_ref, far_ref, near_ref, identity_ref, gain_ref, kgrad_ref, vgrad_ref, inverse_ref):
+def finish_kernel(
+    kt_ref, own_ref, far_ref, near_ref, gain_ref, kgrad_hbm, vgrad_hbm, inverse_ref, kgrad_ref, vgrad_ref, sems
+):
     width = gain_ref.shape[1]
     row = gain_ref[...]
     inverse_ref[...] = 1.0 / row
-    gain = jnp.sum(row * identity_ref[...], axis=1, keepdims=True)
-    for cols in head_columns(kgrad_ref, width):
+    line = lax.broadcasted_iota(jnp.int32, (width, width), 0)
+    diagonal = line == lax.broadcasted_iota(jnp.int32, (width, width), 1)
+    gain = jnp.sum(jnp.where(diagonal, jnp.broadcast_to(row, (width, width)), 0.0), axis=1, keepdims=True)
+    heads = head_columns(kgrad_ref, width)
+    copies = []
+    for h, cols in enumerate(heads):
 
         def total(i):
-            return own_ref[i, cols, :] + far_ref[i, cols, :].astype(F32) + near_ref[i, cols, :].astype(F32)
+            return own_ref[i, cols, :].astype(F32) + far_ref[i, cols, :].astype(F32) + near_ref[i, cols, :].astype(F32)
 
         k = kt_ref[cols, :].astype(F32)
         inverse = inverse_spread(k, 0)
@@ -230,6 +240,14 @@
         mean = jnp.mean(scaled * unit, axis=0, keepdims=True)
         kgrad_ref[:, cols] = ((scaled - unit * mean) * inverse).astype(BF16).T
         vgrad_ref[:, cols] = total(1).astype(BF16).T
+        if h % STEP == STEP - 1:
+            i = h // STEP
+            span = slice(heads[h - STEP + 1].start, cols.stop)
+            for j, (here, there) in enumerate([(kgrad_ref, kgrad_hbm), (vgrad_ref, vgrad_hbm)]):
+                copies.append(pltpu.make_async_copy(here.at[:, span], there.at[:, span], sems.at[i, j]))
+                copies[-1].start()
+    for copy in copies:
+        copy.wait()
 
 
 def combine_kernel(parts_ref, spread_ref):
@@ -242,13 +260,12 @@
     kgain_ref[...] = total * q_ref[...] * inverse_ref[...]
 
 
-def call(body, out_shape, flops, in_specs=None, out_specs=None, scratch=(), grid=(), vmem=24):
+def call(body, out_shape, flops, in_specs=None, out_specs=None, scratch=(), vmem=24):
     whole = pl.BlockSpec(memory_space=pltpu.VMEM)
 
     def run(*args):
         return pl.pallas_call(
             body,
-            grid=grid,
             in_specs=in_specs or [whole] * len(args),
             out_specs=out_specs or [whole] * len(out_shape),
             out_shape=out_shape,
@@ -260,10 +277,6 @@
     return run
 
 
-def over(axis, vector):
-    return jnp.broadcast_to(vector[None], (lax.axis_size(axis),) + vector.shape)
-
-
 def exchange(parts, axis):
     return lax.all_to_all(parts, axis, 0, 0)
 
@@ -278,13 +291,15 @@
     def like(*shape, dtype=BF16):
         return jax.ShapeDtypeStruct(shape, dtype)
 
+    def far_away(shape):
+        return pltpu.HBM(shape.shape, shape.dtype)
+
     hbm = pl.BlockSpec(memory_space=pltpu.HBM)
     vmem = pl.BlockSpec(memory_space=pltpu.VMEM)
     products = 2 * rows * rows * columns
     flat = like(rows, columns)
     turned = like(columns, rows)
     part = like(2, columns, rows)
-    own_part = like(2, columns, rows, dtype=F32)
 
     far_k, far_v = swap(k, 1), swap(v, 1)
     (identity,) = call(identity_kernel, [like(width, width, dtype=F32)], IDLE)()
@@ -297,38 +312,39 @@
     )(q, k, v, g, offsets.T, counts.T, identity, q_row, k_row)
     near = swap(kv, 0)
     (far_k,) = call(far_kernel, [flat], 2 * IDLE)(far_k, k_row)
-    out, q_grad, own, to_far, to_near, gain = call(
+    (side,) = call(side_kernel, [like(3, rows, columns, dtype=F32)], 3 * products)(
+        qn, g, near, far_k, mask, k_row
+    )
+    spread_dp = like(lax.axis_size("dp"), 1, width, dtype=F32)
+    out, q_grad, own, to_far, to_near, spread = call(
         attend_kernel,
-        [flat, flat, own_part, part, part, like(1, width, dtype=F32)],
+        [far_away(flat), far_away(flat), part, far_away(part), far_away(part), far_away(spread_dp)],
         16 * products,
-        out_specs=[hbm] * 5 + [vmem],
+        out_specs=[hbm, hbm, vmem, hbm, hbm, hbm],
         scratch=[
             pltpu.VMEM((rows, columns), BF16),
             pltpu.VMEM((rows, columns), BF16),
-            pltpu.VMEM((2, columns, rows), F32),
             pltpu.VMEM((2, columns, rows), BF16),
             pltpu.VMEM((2, columns, rows), BF16),
-            pltpu.SemaphoreType.DMA((heads // GROUP, 5)),
+            pltpu.VMEM(spread_dp.shape, F32),
+            pltpu.SemaphoreType.DMA((heads // GROUP + 1, 4)),
         ],
-    )(qn, g, qt, gt, kv, near, far_k, far_v, mask, unit, inverse, terms, q_row)
+    )(qn, g, qt, gt, kv, near, far_k, far_v, side, unit, inverse, terms, q_row)
     from_far = swap(to_far, 1)
     from_near = swap(to_near, 0)
-    chunk = STEP * width
-    flat_spec = pl.BlockSpec((rows, chunk), lambda j: (0, j))
-    turned_spec = pl.BlockSpec((chunk, rows), lambda j: (j, 0))
-    part_spec = pl.BlockSpec((2, chunk, rows), lambda j: (0, j, 0))
-    row_spec = pl.BlockSpec((1, width), lambda j: (0, 0))
-    square_spec = pl.BlockSpec((width, width), lambda j: (0, 0))
     k_grad, v_grad, inverse_gain = call(
         finish_kernel,
-        [flat, flat, like(1, width, dtype=F32)],
+        [far_away(flat), far_away(flat), like(1, width, dtype=F32)],
         rows * columns * 40,
-        in_specs=[turned_spec, part_spec, part_spec, part_spec, square_spec, row_spec],
-        out_specs=[flat_spec, flat_spec, row_spec],
-        grid=(heads // STEP,),
-    )(kt, own, from_far, from_near, identity, k_row)
-    spread = [like(lax.axis_size("seq"), 1, width, dtype=F32)]
-    (spread,) = call(combine_kernel, spread, COMBINE)(exchange(over("dp", gain), "dp"))
+        out_specs=[hbm, hbm, vmem],
+        scratch=[
+            pltpu.VMEM((rows, columns), BF16),
+            pltpu.VMEM((rows, columns), BF16),
+            pltpu.SemaphoreType.DMA((heads // STEP, 2)),
+        ],
+    )(kt, own, from_far, from_near, k_row)
+    spread_seq = like(lax.axis_size("seq"), 1, width, dtype=F32)
+    (spread,) = call(combine_kernel, [spread_seq], COMBINE)(exchange(spread, "dp"))
     parts = exchange(spread, "seq")
     gains = [like(1, width, dtype=F32)] * 2
     q_gain_grad, k_gain_grad = call(gain_kernel, gains, 0)(parts, q_row, inverse_gain)

time: 61.8 us -> 59.2 us (0.958)
  local copies, waits for them, and re-layouts: 2.99 us -> 0.03 us
  waiting for transfers between devices: 8.99 us -> 10.1 us
    unnamed x24 -> x16, local copies, waits for them, and re-layouts: 2.39 us -> 0.03 us
    all_to_all x2, waiting for transfers between devices: 6.79 us -> 8.48 us  [exchange(): return lax.all_to_all(parts, axis, 0, 0)]
    pallas_call x7 -> x8, Pallas kernels: 8.78 us -> 8.36 us  [run(): pl.pallas_call(body, in_specs=in_specs or [whole] * len(args), out_specs=...]
  transfers between devices with their start and end apart: 7 -> 7, of which waited for: 3 -> 3; matrix products, arithmetic and copies ran while one was open for 0% -> 0% of each run, Pallas kernels for 6% -> 7%
where the time goes in v4:
time: 59.2 us; the launch traced here: 58.8 us
  starting transfers between devices  39.5 us (67%)
  waiting for transfers between devices  10.1 us (17%)
  Pallas kernels  8.36 us (14%)
  between operations  0.89 us (2%)
    all_to_all x2, starting transfers between devices, exchange(): return lax.all_to_all(parts, axis, 0, 0)  23 us
    ppermute x5, starting transfers between devices, swap(): lax.ppermute(block, 'seq', [(i, j) for i, j in route if 0 <= j < size])  16.5 us
    all_to_all x2, waiting for transfers between devices, exchange(): return lax.all_to_all(parts, axis, 0, 0)  8.48 us
    pallas_call x8, Pallas kernels, run(): pl.pallas_call(body, in_specs=in_specs or [whole] * len(args), out_specs=...  8.36 us
    ppermute x5, waiting for transfers between devices, swap(): lax.ppermute(block, 'seq', [(i, j) for i, j in route if 0 <= j < size])  1.59 us
  transfers between devices with their start and end apart: 7, of which 3 were waited for; matrix products, arithmetic and copies ran while one was open for 0% of the time, Pallas kernels for 7%

profile of v4, /device:TPU:1, one launch (start us, length us, event | category | flops | bytes accessed | tf_op | source)
XLA Modules:
  0.0 58.8 jit_solution(5490897758886263901)
XLA Ops:
  0.6 4.5 %collective-permute-start.1 = (bf16[128,1536]{1,0:T(8,128)(2,1)}, bf16[128,1536]{1,0:T(8,128)(2,1)S(1)}, u32[]{:S(2)}, u32[]{:S(2)}) collective-permute-start(bf16[128,1536]{1,0:T(8,128)(2,1)} %bitcast.18), channel_id=1, source_target_pairs={{1,2},{2,1},{3,4},{4,3},{5,6},{6,5},{7,8},{8,7},{9,10},{10,9},{11,... | collective-permute-start | bytes 1179656 | tf_op jit(solution)/shard_map/ppermute | solution.py:34
  5.2 0.0 copy-start
  5.2 0.0 copy-start.1
  5.2 0.0 copy-start.2
  5.2 2.1 %collective-permute-start.2 = (bf16[128,1536]{1,0:T(8,128)(2,1)}, bf16[128,1536]{1,0:T(8,128)(2,1)S(1)}, u32[]{:S(2)}, u32[]{:S(2)}) collective-permute-start(bf16[128,1536]{1,0:T(8,128)(2,1)} %bitcast.20), channel_id=1, source_target_pairs={{1,2},{2,1},{3,4},{4,3},{5,6},{6,5},{7,8},{8,7},{9,10},{10,9},{11,... | collective-permute-start | bytes 1179656 | tf_op jit(solution)/shard_map/ppermute | solution.py:34
  7.4 1.0 %shard_map.128 = (bf16[128,1536]{1,0:T(8,128)(2,1)S(1)}, bf16[1536,128]{1,0:T(8,128)(2,1)S(1)}, bf16[1536,128]{1,0:T(8,128)(2,1)S(1)}, bf16[2,128,1536]{2,1,0:T(...) custom-call(bf16[128,1536]{1,0:T(8,128)(2,1)S(1)} %bitcast.17, ...), custom_call_target="tpu_custom_call" | custom-call | flops 100663296 | bytes 4194304 | tf_op jit(solution)/shard_map/pallas_call | solution.py:267
  8.4 4.1 %collective-permute-start = (bf16[2,128,1536]{2,1,0:T(8,128)(2,1)S(1)}, bf16[2,128,1536]{2,1,0:T(8,128)(2,1)S(1)}, u32[]{:S(2)}, u32[]{:S(2)}) collective-permute-start(bf16[2,128,1536]{2,1,0:T(8,128)(2,1)S(1)} %get-tuple-element.29.kv_ref), channel_id=1, source_target_pairs={{0,1},{1,0},{2,3},{3,2},{4,5},{5,4},{6,7},{7,6},{8,9},{9,8},{10,11... | collective-permute-start | bytes 2359304 | tf_op jit(solution)/shard_map/ppermute | solution.py:34
  12.5 0.0 collective-permute-done.1.k_ref
  12.6 0.3 shard_map.129.fk_ref
  12.9 1.6 %collective-permute-done.near_ref = bf16[2,128,1536]{2,1,0:T(8,128)(2,1)S(1)} collective-permute-done((bf16[2,128,1536]{2,1,0:T(8,128)(2,1)S(1)}, bf16[2,128,1536]{2,1,0:T(8,128)(2,1)S(1)}, u32[]{:S(2)}, u32[]{:S(2)}) %collective-permute-start) | collective-permute-done | bytes 786464 | tf_op jit(solution)/shard_map/ppermute | solution.py:34
  14.4 0.7 %shard_map.130.side_ref = f32[3,128,1536]{2,1,0:T(8,128)S(1)} custom-call(bf16[128,1536]{1,0:T(8,128)(2,1)S(1)} %get-tuple-element.26.qn_ref, bf16[128,1536]{1,0:T(8,128)(2,1)S(1)} %bitcast.15, bf16[2,128,1536]{2,1,0:T(8,128)(2,1)S(1)} %collective-permute-done.near_ref, bf16[128,1536]{1,0:T(8,128)(2,1)S(1)} %shard_map.129.fk_ref, ...), custom_call_target="tpu_custom_call" | custom-call | flops 150994944 | bytes 4194304 | tf_op jit(solution)/shard_map/pallas_call | solution.py:267
  15.1 0.0 collective-permute-done.2.fv_ref
  15.1 3.6 %shard_map.131 = (bf16[128,1536]{1,0:T(8,128)(2,1)}, bf16[128,1536]{1,0:T(8,128)(2,1)}, bf16[2,1536,128]{2,1,0:T(8,128)(2,1)S(1)}, bf16[2,1536,128]{2,1,0:T(8,12...) custom-call(bf16[128,1536]{1,0:T(8,128)(2,1)S(1)} %get-tuple-element.26.qn_ref, ...), custom_call_target="tpu_custom_call" | custom-call | flops 805306368 | bytes 4194304 | tf_op jit(solution)/shard_map/pallas_call | solution.py:267
  18.8 9.9 %all-to-all-start = ((f32[8,1,128]{2,1,0:T(1,128)}), f32[8,1,128]{2,1,0:T(1,128)S(1)}, u32[]{:S(2)}, u32[]{:S(2)}) async-start(f32[8,1,128]{2,1,0:T(1,128)} %get-tuple-element.42), calls=%async_computation | async-start | bytes 8192 | tf_op jit(solution)/shard_map/all_to_all | solution.py:281
  28.7 3.9 %collective-permute-start.3 = (bf16[2,1536,128]{2,1,0:T(8,128)(2,1)}, bf16[2,1536,128]{2,1,0:T(8,128)(2,1)S(1)}, u32[]{:S(2)}, u32[]{:S(2)}) collective-permute-start(bf16[2,1536,128]{2,1,0:T(8,128)(2,1)} %get-tuple-element.38), channel_id=1, source_target_pairs={{1,2},{2,1},{3,4},{4,3},{5,6},{6,5},{7,8},{8,7},{9,10},{10,9},{11,... | collective-permute-start | bytes 2359304 | tf_op jit(solution)/shard_map/ppermute | solution.py:34
  32.6 1.9 %collective-permute-start.4 = (bf16[2,1536,128]{2,1,0:T(8,128)(2,1)}, bf16[2,1536,128]{2,1,0:T(8,128)(2,1)S(1)}, u32[]{:S(2)}, u32[]{:S(2)}) collective-permute-start(bf16[2,1536,128]{2,1,0:T(8,128)(2,1)} %get-tuple-element.39), channel_id=1, source_target_pairs={{0,1},{1,0},{2,3},{3,2},{4,5},{5,4},{6,7},{7,6},{8,9},{9,8},{10,11... | collective-permute-start | bytes 2359304 | tf_op jit(solution)/shard_map/ppermute | solution.py:34
  34.6 0.6 %all-to-all-done.parts_ref = f32[8,1,128]{2,1,0:T(1,128)S(1)} async-done(((f32[8,1,128]{2,1,0:T(1,128)}), f32[8,1,128]{2,1,0:T(1,128)S(1)}, u32[]{:S(2)}, u32[]{:S(2)}) %all-to-all-start) | async-done | bytes 4128 | tf_op jit(solution)/shard_map/all_to_all | solution.py:281
  35.2 0.6 %shard_map.133 = f32[64,1,128]{2,1,0:T(1,128)} custom-call(f32[8,1,128]{2,1,0:T(1,128)S(1)} %all-to-all-done.parts_ref), custom_call_target="tpu_custom_call" | custom-call | flops 30000001024 | bytes 4194304 | tf_op jit(solution)/shard_map/pallas_call | solution.py:267
  35.8 13.0 %all-to-all-start.1 = ((f32[64,1,128]{2,1,0:T(1,128)}), f32[64,1,128]{2,1,0:T(1,128)S(1)}, u32[]{:S(2)}, u32[]{:S(2)}) async-start(f32[64,1,128]{2,1,0:T(1,128)} %shard_map.133), calls=%async_computation.1 | async-start | bytes 65536 | tf_op jit(solution)/shard_map/all_to_all | solution.py:281
  48.9 0.0 collective-permute-done.3.far_ref
  48.9 0.0 collective-permute-done.4.near_ref
  48.9 1.5 %shard_map.132 = (bf16[128,1536]{1,0:T(8,128)(2,1)}, bf16[128,1536]{1,0:T(8,128)(2,1)}, f32[1,128]{1,0:T(1,128)S(1)}) custom-call(bf16[1536,128]{1,0:T(8,128)(2,1)S(1)} %get-tuple-element.36.kt_ref, bf16[2,1536,128]{2,1,0:T(8,128)(2,1)S(1)} %get-tuple-element.37.own_ref, bf16[2,1536,128]{2,1,0:T(8,128)(2,1)S(1)} %collective-permute-done.3.far_ref, ...), custom_call_target="tpu_custom_call" | custom-call | flops 7864320 | bytes 4194304 | tf_op jit(solution)/shard_map/pallas_call | solution.py:267
  50.4 7.9 %all-to-all-done.1.parts_ref = f32[64,1,128]{2,1,0:T(1,128)S(1)} async-done(((f32[64,1,128]{2,1,0:T(1,128)}), f32[64,1,128]{2,1,0:T(1,128)S(1)}, u32[]{:S(2)}, u32[]{:S(2)}) %all-to-all-start.1) | async-done | bytes 32800 | tf_op jit(solution)/shard_map/all_to_all | solution.py:281
  58.2 0.6 shard_map.134
  (14 shorter events, 0.0 us)
Async XLA Ops:
  0.6 11.9 %collective-permute-start.1 = (bf16[128,1536]{1,0:T(8,128)(2,1)}, bf16[128,1536]{1,0:T(8,128)(2,1)S(1)}, u32[]{:S(2)}, u32[]{:S(2)}) collective-permute-start(bf16[128,1536]{1,0:T(8,128)(2,1)} %bitcast.18), channel_id=1, source_target_pairs={{1,2},{2,1},{3,4},{4,3},{5,6},{6,5},{7,8},{8,7},{9,10},{10,9},{11,... | collective-permute-start | bytes 1179656 | tf_op jit(solution)/shard_map/ppermute | solution.py:34
  5.2 2.2 %copy-start = (bf16[1,128,1536]{2,1,0:T(8,128)(2,1)S(1)}, bf16[1,128,1536]{2,1,0:T(8,128)(2,1)}, u32[]{:S(2)}) copy-start(bf16[1,128,1536]{2,1,0:T(8,128)(2,1)} %param.11) | copy-start | bytes 1179652
  5.2 2.2 %copy-start.1 = (bf16[1,128,1536]{2,1,0:T(8,128)(2,1)S(1)}, bf16[1,128,1536]{2,1,0:T(8,128)(2,1)}, u32[]{:S(2)}) copy-start(bf16[1,128,1536]{2,1,0:T(8,128)(2,1)} %param.8) | copy-start | bytes 1179652
  5.2 2.2 %copy-start.2 = (bf16[1,128,1536]{2,1,0:T(8,128)(2,1)S(1)}, bf16[1,128,1536]{2,1,0:T(8,128)(2,1)}, u32[]{:S(2)}) copy-start(bf16[1,128,1536]{2,1,0:T(8,128)(2,1)} %param.9) | copy-start | bytes 1179652
  5.2 2.2 %copy-start.3 = (bf16[1,128,1536]{2,1,0:T(8,128)(2,1)S(1)}, bf16[1,128,1536]{2,1,0:T(8,128)(2,1)}, u32[]{:S(2)}) copy-start(bf16[1,128,1536]{2,1,0:T(8,128)(2,1)} %param.10) | copy-start | bytes 1179652
  5.2 2.2 %copy-start.4 = (s32[128,12]{0,1:T(8,128)S(1)}, s32[128,12]{0,1:T(8,128)}, u32[]{:S(2)}) copy-start(s32[128,12]{0,1:T(8,128)} %param.15) | copy-start | bytes 18436
  5.2 2.2 %copy-start.5 = (f32[128]{0:T(128)S(1)}, f32[128]{0:T(128)}, u32[]{:S(2)}) copy-start(f32[128]{0:T(128)} %param.13) | copy-start | bytes 1540
  5.2 2.2 %copy-start.6 = (f32[128]{0:T(128)S(1)}, f32[128]{0:T(128)}, u32[]{:S(2)}) copy-start(f32[128]{0:T(128)} %param.12) | copy-start | bytes 1540
  5.2 2.2 %copy-start.7 = (s32[12,5]{0,1:T(8,128)S(1)}, s32[12,5]{0,1:T(8,128)}, u32[]{:S(2)}) copy-start(s32[12,5]{0,1:T(8,128)} %param.14) | copy-start | bytes 724
  5.2 9.9 %collective-permute-start.2 = (bf16[128,1536]{1,0:T(8,128)(2,1)}, bf16[128,1536]{1,0:T(8,128)(2,1)S(1)}, u32[]{:S(2)}, u32[]{:S(2)}) collective-permute-start(bf16[128,1536]{1,0:T(8,128)(2,1)} %bitcast.20), channel_id=1, source_target_pairs={{1,2},{2,1},{3,4},{4,3},{5,6},{6,5},{7,8},{8,7},{9,10},{10,9},{11,... | collective-permute-start | bytes 1179656 | tf_op jit(solution)/shard_map/ppermute | solution.py:34
  8.4 6.0 %collective-permute-start = (bf16[2,128,1536]{2,1,0:T(8,128)(2,1)S(1)}, bf16[2,128,1536]{2,1,0:T(8,128)(2,1)S(1)}, u32[]{:S(2)}, u32[]{:S(2)}) collective-permute-start(bf16[2,128,1536]{2,1,0:T(8,128)(2,1)S(1)} %get-tuple-element.29.kv_ref), channel_id=1, source_target_pairs={{0,1},{1,0},{2,3},{3,2},{4,5},{5,4},{6,7},{7,6},{8,9},{9,8},{10,11... | collective-permute-start | bytes 2359304 | tf_op jit(solution)/shard_map/ppermute | solution.py:34
  18.8 16.4 %all-to-all-start = ((f32[8,1,128]{2,1,0:T(1,128)}), f32[8,1,128]{2,1,0:T(1,128)S(1)}, u32[]{:S(2)}, u32[]{:S(2)}) async-start(f32[8,1,128]{2,1,0:T(1,128)} %get-tuple-element.42), calls=%async_computation | async-start | bytes 8192 | tf_op jit(solution)/shard_map/all_to_all | solution.py:281
  28.7 20.2 %collective-permute-start.3 = (bf16[2,1536,128]{2,1,0:T(8,128)(2,1)}, bf16[2,1536,128]{2,1,0:T(8,128)(2,1)S(1)}, u32[]{:S(2)}, u32[]{:S(2)}) collective-permute-start(bf16[2,1536,128]{2,1,0:T(8,128)(2,1)} %get-tuple-element.38), channel_id=1, source_target_pairs={{1,2},{2,1},{3,4},{4,3},{5,6},{6,5},{7,8},{8,7},{9,10},{10,9},{11,... | collective-permute-start | bytes 2359304 | tf_op jit(solution)/shard_map/ppermute | solution.py:34
  32.6 16.2 %collective-permute-start.4 = (bf16[2,1536,128]{2,1,0:T(8,128)(2,1)}, bf16[2,1536,128]{2,1,0:T(8,128)(2,1)S(1)}, u32[]{:S(2)}, u32[]{:S(2)}) collective-permute-start(bf16[2,1536,128]{2,1,0:T(8,128)(2,1)} %get-tuple-element.39), channel_id=1, source_target_pairs={{0,1},{1,0},{2,3},{3,2},{4,5},{5,4},{6,7},{7,6},{8,9},{9,8},{10,11... | collective-permute-start | bytes 2359304 | tf_op jit(solution)/shard_map/ppermute | solution.py:34
  35.8 22.4 %all-to-all-start.1 = ((f32[64,1,128]{2,1,0:T(1,128)}), f32[64,1,128]{2,1,0:T(1,128)S(1)}, u32[]{:S(2)}, u32[]{:S(2)}) async-start(f32[64,1,128]{2,1,0:T(1,128)} %shard_map.133), calls=%async_computation.1 | async-start | bytes 65536 | tf_op jit(solution)/shard_map/all_to_all | solution.py:281

commit v5 on v4

--- a/solution.py
+++ b/solution.py
@@ -123,40 +123,56 @@
         kn_ref[:, cols] = normal(k_ref[:, cols], gain)
 
 
-def side_kernel(qn_ref, g_ref, near_ref, fk_ref, mask_ref, gain_ref, terms_ref):
-    width = gain_ref.shape[1]
+def side_kernel(
+    qn_ref, g_ref, gt_ref, near_ref, fk_ref, mask_ref, own_ref, probs_ref, dprob_ref, far_v_ref, own_v_ref, near_v_ref
+):
     rows = qn_ref.shape[0]
+    width = gt_ref.shape[0] // mask_ref.shape[1]
     scale = width ** (-0.5)
     for h, cols in enumerate(head_columns(qn_ref, width)):
         scores = dot(qn_ref[:, cols], jnp.concatenate([fk_ref[:, cols], near_ref[0, :, cols]], axis=0), NT)
-        terms_ref[0, :, cols] = masked_terms(scores[:, :rows], scale, mask_ref, h, 0)
-        terms_ref[1, :, cols] = masked_terms(scores[:, rows:], scale, mask_ref, h, 2 * rows)
-        terms_ref[2, :, cols] = dot(g_ref[:, cols], near_ref[1, :, cols], NT)
+        dprob_ref[:, cols] = dot(g_ref[:, cols], near_ref[1, :, cols], NT)
+        terms = [
+            masked_terms(scores[:, :rows], scale, mask_ref, h, 0),
+            own_ref[0, :, cols],
+            masked_terms(scores[:, rows:], scale, mask_ref, h, 2 * rows),
+        ]
+        inverse = 1.0 / jnp.sum(terms[0] + terms[1] + terms[2], axis=1, keepdims=True)
+        probs = [term * inverse for term in terms]
+        for i, p in enumerate(probs):
+            probs_ref[i, :, cols] = p
+        weights = jnp.concatenate([p.astype(BF16) for p in probs], axis=1)
+        val_t = dot(gt_ref[cols, :], weights, NN).astype(BF16)
+        for i, ref in enumerate([far_v_ref, own_v_ref, near_v_ref]):
+            ref[cols, :] = val_t[:, i * rows : (i + 1) * rows]
 
 
 def attend_kernel(
-    qn_ref, g_ref, qt_ref, gt_ref, kv_ref, near_ref, fk_ref, fv_ref,
-    side_ref, unit_ref, inverse_ref, terms_ref, qgain_ref,
+    g_ref, qt_ref, kv_ref, near_ref, fk_ref, fv_ref, probs_ref, dprob_ref, far_v_ref, near_v_ref,
+    unit_ref, inverse_ref, terms_ref, qgain_ref,
     out_hbm, qgrad_hbm, own_ref, far_hbm, near_hbm, spread_hbm,
     out_ref, qgrad_ref, to_far_ref, to_near_ref, spread_ref, sems,
 ):
     width = qgain_ref.shape[1]
-    rows = qn_ref.shape[0]
+    rows = g_ref.shape[0]
     scale = width ** (-0.5)
     q_gain = qgain_ref[...]
-    heads = head_columns(qn_ref, width)
+    heads = head_columns(g_ref, width)
     count = len(heads)
-    copies = []
+    copies = [
+        pltpu.make_async_copy(far_v_ref, far_hbm.at[1], sems.at[count // GROUP, 1]),
+        pltpu.make_async_copy(near_v_ref, near_hbm.at[1], sems.at[count // GROUP, 2]),
+    ]
+    for copy in copies:
+        copy.start()
 
     def first_stage(h):
         return (dot(g_ref[:, heads[h]], fv_ref[:, heads[h]], NT),)
 
     def middle_stage(h, dprob):
         cols = heads[h]
-        terms = [side_ref[0, :, cols], terms_ref[0, :, cols], side_ref[1, :, cols]]
-        inverse = 1.0 / jnp.sum(terms[0] + terms[1] + terms[2], axis=1, keepdims=True)
-        probs = [term * inverse for term in terms]
-        dprobs = [dprob, terms_ref[1, :, cols], side_ref[2, :, cols]]
+        probs = [probs_ref[i, :, cols] for i in range(3)]
+        dprobs = [dprob, terms_ref[1, :, cols], dprob_ref[:, cols]]
         delta = jnp.sum(
             probs[0] * dprobs[0] + probs[1] * dprobs[1] + probs[2] * dprobs[2], axis=1, keepdims=True
         )
@@ -171,13 +187,9 @@
         grad_qn = dot(dscore, keys, NN) * scale
         out_ref[:, cols] = dot(weights, vals, NN).astype(BF16)
         key_t = dot(qt_ref[cols, :], dscore, NN) * scale
-        val_t = dot(gt_ref[cols, :], weights, NN)
-        own_ref[0, cols, :] = key_t[:, rows : 2 * rows].astype(BF16)
-        own_ref[1, cols, :] = val_t[:, rows : 2 * rows].astype(BF16)
-        to_far_ref[0, cols, :] = key_t[:, :rows].astype(BF16)
-        to_far_ref[1, cols, :] = val_t[:, :rows].astype(BF16)
-        to_near_ref[0, cols, :] = key_t[:, 2 * rows :].astype(BF16)
-        to_near_ref[1, cols, :] = val_t[:, 2 * rows :].astype(BF16)
+        own_ref[cols, :] = key_t[:, rows : 2 * rows].astype(BF16)
+        to_far_ref[cols, :] = key_t[:, :rows].astype(BF16)
+        to_near_ref[cols, :] = key_t[:, 2 * rows :].astype(BF16)
         unit = unit_ref[:, cols]
         product = grad_qn * unit
         mean = jnp.mean(product * q_gain, axis=1, keepdims=True)
@@ -186,8 +198,8 @@
             i = h // GROUP
             span = slice(heads[h - GROUP + 1].start, cols.stop)
             pairs = [
-                (to_far_ref.at[:, span, :], far_hbm.at[:, span, :]),
-                (to_near_ref.at[:, span, :], near_hbm.at[:, span, :]),
+                (to_far_ref.at[span, :], far_hbm.at[0, span, :]),
+                (to_near_ref.at[span, :], near_hbm.at[0, span, :]),
                 (out_ref.at[:, span], out_hbm.at[:, span]),
                 (qgrad_ref.at[:, span], qgrad_hbm.at[:, span]),
             ]
@@ -218,7 +230,7 @@
 
 
 def finish_kernel(
-    kt_ref, own_ref, far_ref, near_ref, gain_ref, kgrad_hbm, vgrad_hbm, inverse_ref, kgrad_ref, vgrad_ref, sems
+    kt_ref, own_k_ref, own_v_ref, far_ref, near_ref, gain_ref, kgrad_hbm, vgrad_hbm, inverse_ref, kgrad_ref, vgrad_ref, sems
 ):
     width = gain_ref.shape[1]
     row = gain_ref[...]
@@ -231,7 +243,8 @@
     for h, cols in enumerate(heads):
 
         def total(i):
-            return own_ref[i, cols, :].astype(F32) + far_ref[i, cols, :].astype(F32) + near_ref[i, cols, :].astype(F32)
+            own = (own_k_ref, own_v_ref)[i][cols, :].astype(F32)
+            return own + far_ref[i, cols, :].astype(F32) + near_ref[i, cols, :].astype(F32)
 
         k = kt_ref[cols, :].astype(F32)
         inverse = inverse_spread(k, 0)
@@ -312,24 +325,26 @@
     )(q, k, v, g, offsets.T, counts.T, identity, q_row, k_row)
     near = swap(kv, 0)
     (far_k,) = call(far_kernel, [flat], 2 * IDLE)(far_k, k_row)
-    (side,) = call(side_kernel, [like(3, rows, columns, dtype=F32)], 3 * products)(
-        qn, g, near, far_k, mask, k_row
-    )
+    probs, dprob, far_v_part, own_v_part, near_v_part = call(
+        side_kernel,
+        [like(3, rows, columns, dtype=F32), wide, turned, turned, turned],
+        6 * products,
+    )(qn, g, gt, near, far_k, mask, terms)
     spread_dp = like(lax.axis_size("dp"), 1, width, dtype=F32)
-    out, q_grad, own, to_far, to_near, spread = call(
+    out, q_grad, own_k_part, to_far, to_near, spread = call(
         attend_kernel,
-        [far_away(flat), far_away(flat), part, far_away(part), far_away(part), far_away(spread_dp)],
-        16 * products,
+        [far_away(flat), far_away(flat), turned, far_away(part), far_away(part), far_away(spread_dp)],
+        11 * products,
         out_specs=[hbm, hbm, vmem, hbm, hbm, hbm],
         scratch=[
             pltpu.VMEM((rows, columns), BF16),
             pltpu.VMEM((rows, columns), BF16),
-            pltpu.VMEM((2, columns, rows), BF16),
-            pltpu.VMEM((2, columns, rows), BF16),
+            pltpu.VMEM((columns, rows), BF16),
+            pltpu.VMEM((columns, rows), BF16),
             pltpu.VMEM(spread_dp.shape, F32),
             pltpu.SemaphoreType.DMA((heads // GROUP + 1, 4)),
         ],
-    )(qn, g, qt, gt, kv, near, far_k, far_v, side, unit, inverse, terms, q_row)
+    )(g, qt, kv, near, far_k, far_v, probs, dprob, far_v_part, near_v_part, unit, inverse, terms, q_row)
     from_far = swap(to_far, 1)
     from_near = swap(to_near, 0)
     k_grad, v_grad, inverse_gain = call(
@@ -342,7 +357,7 @@
             pltpu.VMEM((rows, columns), BF16),
             pltpu.SemaphoreType.DMA((heads // STEP, 2)),
         ],
-    )(kt, own, from_far, from_near, k_row)
+    )(kt, own_k_part, own_v_part, from_far, from_near, k_row)
     spread_seq = like(lax.axis_size("seq"), 1, width, dtype=F32)
     (spread,) = call(combine_kernel, [spread_seq], COMBINE)(exchange(spread, "dp"))
     parts = exchange(spread, "seq")

time: 59.2 us -> 60.1 us (1.015)
  Pallas kernels: 8.36 us -> 10.6 us
  starting transfers between devices: 39.5 us -> 38.2 us
    pallas_call x8, Pallas kernels: 8.36 us -> 10.6 us  [run(): pl.pallas_call(body, in_specs=in_specs or [whole] * len(args), out_specs=...]
    all_to_all x2, starting transfers between devices: 23 us -> 21.7 us  [exchange(): return lax.all_to_all(parts, axis, 0, 0)]
  transfers between devices with their start and end apart: 7 -> 7, of which waited for: 3 -> 3; matrix products, arithmetic and copies ran while one was open for 0% -> 0% of each run, Pallas kernels for 7% -> 12%
where the time goes in v5:
time: 60.1 us; the launch traced here: 59.8 us
  starting transfers between devices  38.2 us (64%)
  Pallas kernels  10.6 us (18%)
  waiting for transfers between devices  10.1 us (17%)
  between operations  0.89 us (1%)
    all_to_all x2, starting transfers between devices, exchange(): return lax.all_to_all(parts, axis, 0, 0)  21.7 us
    ppermute x5, starting transfers between devices, swap(): lax.ppermute(block, 'seq', [(i, j) for i, j in route if 0 <= j < size])  16.5 us
    pallas_call x8, Pallas kernels, run(): pl.pallas_call(body, in_specs=in_specs or [whole] * len(args), out_specs=...  10.6 us
    all_to_all x2, waiting for transfers between devices, exchange(): return lax.all_to_all(parts, axis, 0, 0)  8.49 us
    ppermute x5, waiting for transfers between devices, swap(): lax.ppermute(block, 'seq', [(i, j) for i, j in route if 0 <= j < size])  1.59 us
  transfers between devices with their start and end apart: 7, of which 3 were waited for; matrix products, arithmetic and copies ran while one was open for 0% of the time, Pallas kernels for 12%

profile of v5, /device:TPU:1, one launch (start us, length us, event | category | flops | bytes accessed | tf_op | source)
XLA Modules:
  0.0 59.8 jit_solution(9380377237223797758)
XLA Ops:
  0.6 4.5 %collective-permute-start.1 = (bf16[128,1536]{1,0:T(8,128)(2,1)}, bf16[128,1536]{1,0:T(8,128)(2,1)S(1)}, u32[]{:S(2)}, u32[]{:S(2)}) collective-permute-start(bf16[128,1536]{1,0:T(8,128)(2,1)} %bitcast.18), channel_id=1, source_target_pairs={{1,2},{2,1},{3,4},{4,3},{5,6},{6,5},{7,8},{8,7},{9,10},{10,9},{11,... | collective-permute-start | bytes 1179656 | tf_op jit(solution)/shard_map/ppermute | solution.py:34
  5.2 0.0 copy-start
  5.2 0.0 copy-start.1
  5.2 0.0 copy-start.2
  5.2 2.1 %collective-permute-start.2 = (bf16[128,1536]{1,0:T(8,128)(2,1)}, bf16[128,1536]{1,0:T(8,128)(2,1)S(1)}, u32[]{:S(2)}, u32[]{:S(2)}) collective-permute-start(bf16[128,1536]{1,0:T(8,128)(2,1)} %bitcast.20), channel_id=1, source_target_pairs={{1,2},{2,1},{3,4},{4,3},{5,6},{6,5},{7,8},{8,7},{9,10},{10,9},{11,... | collective-permute-start | bytes 1179656 | tf_op jit(solution)/shard_map/ppermute | solution.py:34
  7.4 1.0 %shard_map.128 = (bf16[128,1536]{1,0:T(8,128)(2,1)S(1)}, bf16[1536,128]{1,0:T(8,128)(2,1)S(1)}, bf16[1536,128]{1,0:T(8,128)(2,1)S(1)}, bf16[2,128,1536]{2,1,0:T(...) custom-call(bf16[128,1536]{1,0:T(8,128)(2,1)S(1)} %bitcast.17, ...), custom_call_target="tpu_custom_call" | custom-call | flops 100663296 | bytes 4194304 | tf_op jit(solution)/shard_map/pallas_call | solution.py:280
  8.4 4.1 %collective-permute-start = (bf16[2,128,1536]{2,1,0:T(8,128)(2,1)S(1)}, bf16[2,128,1536]{2,1,0:T(8,128)(2,1)S(1)}, u32[]{:S(2)}, u32[]{:S(2)}) collective-permute-start(bf16[2,128,1536]{2,1,0:T(8,128)(2,1)S(1)} %get-tuple-element.32.kv_ref), channel_id=1, source_target_pairs={{0,1},{1,0},{2,3},{3,2},{4,5},{5,4},{6,7},{7,6},{8,9},{9,8},{10,11... | collective-permute-start | bytes 2359304 | tf_op jit(solution)/shard_map/ppermute | solution.py:34
  12.5 0.0 collective-permute-done.1.k_ref
  12.5 0.3 shard_map.129.fk_ref
  12.8 1.6 %collective-permute-done.near_ref = bf16[2,128,1536]{2,1,0:T(8,128)(2,1)S(1)} collective-permute-done((bf16[2,128,1536]{2,1,0:T(8,128)(2,1)S(1)}, bf16[2,128,1536]{2,1,0:T(8,128)(2,1)S(1)}, u32[]{:S(2)}, u32[]{:S(2)}) %collective-permute-start) | collective-permute-done | bytes 786464 | tf_op jit(solution)/shard_map/ppermute | solution.py:34
  14.4 3.6 %shard_map.130 = (f32[3,128,1536]{2,1,0:T(8,128)S(1)}, f32[128,1536]{1,0:T(8,128)S(1)}, bf16[1536,128]{1,0:T(8,128)(2,1)S(1)}, bf16[1536,128]{1,0:T(8,128)(2,1)S(1)}, bf16[1536,128]{1,0:T(8,128)(2,1)S(1)}) custom-call(bf16[128,1536]{1,0:T(8,128)(2,1)S(1)} %get-tuple-element.33.qn_ref, bf16[128,1536]{1,0:T(8,128)(2,1)S(1)} %bitcast.15, ...), custom_call_target="tpu_custom_call" | custom-call | flops 301989888 | bytes 4194304 | tf_op jit(solution)/shard_map/pallas_call | solution.py:280
  18.0 0.0 collective-permute-done.2.fv_ref
  18.0 3.0 %shard_map.131 = (bf16[128,1536]{1,0:T(8,128)(2,1)}, bf16[128,1536]{1,0:T(8,128)(2,1)}, bf16[1536,128]{1,0:T(8,128)(2,1)S(1)}, bf16[2,1536,128]{2,1,0:T(8,128)(2...) custom-call(bf16[128,1536]{1,0:T(8,128)(2,1)S(1)} %bitcast.16, bf16[1536,128]{1,0:T(8,128)(2,1)S(1)} %get-tuple-element.31.qt_ref, ...), custom_call_target="tpu_custom_call" | custom-call | flops 553648128 | bytes 4194304 | tf_op jit(solution)/shard_map/pallas_call | solution.py:280
  21.0 8.2 %all-to-all-start = ((f32[8,1,128]{2,1,0:T(1,128)}), f32[8,1,128]{2,1,0:T(1,128)S(1)}, u32[]{:S(2)}, u32[]{:S(2)}) async-start(f32[8,1,128]{2,1,0:T(1,128)} %get-tuple-element.52), calls=%async_computation | async-start | bytes 8192 | tf_op jit(solution)/shard_map/all_to_all | solution.py:294
  29.2 3.9 %collective-permute-start.3 = (bf16[2,1536,128]{2,1,0:T(8,128)(2,1)}, bf16[2,1536,128]{2,1,0:T(8,128)(2,1)S(1)}, u32[]{:S(2)}, u32[]{:S(2)}) collective-permute-start(bf16[2,1536,128]{2,1,0:T(8,128)(2,1)} %get-tuple-element.48), channel_id=1, source_target_pairs={{1,2},{2,1},{3,4},{4,3},{5,6},{6,5},{7,8},{8,7},{9,10},{10,9},{11,... | collective-permute-start | bytes 2359304 | tf_op jit(solution)/shard_map/ppermute | solution.py:34
  33.2 1.9 %collective-permute-start.4 = (bf16[2,1536,128]{2,1,0:T(8,128)(2,1)}, bf16[2,1536,128]{2,1,0:T(8,128)(2,1)S(1)}, u32[]{:S(2)}, u32[]{:S(2)}) collective-permute-start(bf16[2,1536,128]{2,1,0:T(8,128)(2,1)} %get-tuple-element.49), channel_id=1, source_target_pairs={{0,1},{1,0},{2,3},{3,2},{4,5},{5,4},{6,7},{7,6},{8,9},{9,8},{10,11... | collective-permute-start | bytes 2359304 | tf_op jit(solution)/shard_map/ppermute | solution.py:34
  35.1 0.6 %all-to-all-done.parts_ref = f32[8,1,128]{2,1,0:T(1,128)S(1)} async-done(((f32[8,1,128]{2,1,0:T(1,128)}), f32[8,1,128]{2,1,0:T(1,128)S(1)}, u32[]{:S(2)}, u32[]{:S(2)}) %all-to-all-start) | async-done | bytes 4128 | tf_op jit(solution)/shard_map/all_to_all | solution.py:294
  35.7 0.6 %shard_map.133 = f32[64,1,128]{2,1,0:T(1,128)} custom-call(f32[8,1,128]{2,1,0:T(1,128)S(1)} %all-to-all-done.parts_ref), custom_call_target="tpu_custom_call" | custom-call | flops 30000001024 | bytes 4194304 | tf_op jit(solution)/shard_map/pallas_call | solution.py:280
  36.3 13.5 %all-to-all-start.1 = ((f32[64,1,128]{2,1,0:T(1,128)}), f32[64,1,128]{2,1,0:T(1,128)S(1)}, u32[]{:S(2)}, u32[]{:S(2)}) async-start(f32[64,1,128]{2,1,0:T(1,128)} %shard_map.133), calls=%async_computation.1 | async-start | bytes 65536 | tf_op jit(solution)/shard_map/all_to_all | solution.py:294
  49.8 0.0 collective-permute-done.3.far_ref
  49.8 0.0 collective-permute-done.4.near_ref
  49.8 1.5 %shard_map.132 = (bf16[128,1536]{1,0:T(8,128)(2,1)}, bf16[128,1536]{1,0:T(8,128)(2,1)}, f32[1,128]{1,0:T(1,128)S(1)}) custom-call(bf16[1536,128]{1,0:T(8,128)(2,1)S(1)} %get-tuple-element.45.kt_ref, bf16[1536,128]{1,0:T(8,128)(2,1)S(1)} %get-tuple-element.46.own_k_ref, bf16[1536,128]{1,0:T(8,128)(2,1)S(1)} %get-tuple-element.47.own_v_ref, ...), custom_call_target="tpu_custom_call" | custom-call | flops 7864320 | bytes 4194304 | tf_op jit(solution)/shard_map/pallas_call | solution.py:280
  51.3 7.9 %all-to-all-done.1.parts_ref = f32[64,1,128]{2,1,0:T(1,128)S(1)} async-done(((f32[64,1,128]{2,1,0:T(1,128)}), f32[64,1,128]{2,1,0:T(1,128)S(1)}, u32[]{:S(2)}, u32[]{:S(2)}) %all-to-all-start.1) | async-done | bytes 32800 | tf_op jit(solution)/shard_map/all_to_all | solution.py:294
  59.2 0.6 shard_map.134
  (14 shorter events, 0.0 us)
Async XLA Ops:
  0.6 11.9 %collective-permute-start.1 = (bf16[128,1536]{1,0:T(8,128)(2,1)}, bf16[128,1536]{1,0:T(8,128)(2,1)S(1)}, u32[]{:S(2)}, u32[]{:S(2)}) collective-permute-start(bf16[128,1536]{1,0:T(8,128)(2,1)} %bitcast.18), channel_id=1, source_target_pairs={{1,2},{2,1},{3,4},{4,3},{5,6},{6,5},{7,8},{8,7},{9,10},{10,9},{11,... | collective-permute-start | bytes 1179656 | tf_op jit(solution)/shard_map/ppermute | solution.py:34
  5.2 2.2 %copy-start = (bf16[1,128,1536]{2,1,0:T(8,128)(2,1)S(1)}, bf16[1,128,1536]{2,1,0:T(8,128)(2,1)}, u32[]{:S(2)}) copy-start(bf16[1,128,1536]{2,1,0:T(8,128)(2,1)} %param.11) | copy-start | bytes 1179652
  5.2 2.2 %copy-start.1 = (bf16[1,128,1536]{2,1,0:T(8,128)(2,1)S(1)}, bf16[1,128,1536]{2,1,0:T(8,128)(2,1)}, u32[]{:S(2)}) copy-start(bf16[1,128,1536]{2,1,0:T(8,128)(2,1)} %param.8) | copy-start | bytes 1179652
  5.2 2.2 %copy-start.2 = (bf16[1,128,1536]{2,1,0:T(8,128)(2,1)S(1)}, bf16[1,128,1536]{2,1,0:T(8,128)(2,1)}, u32[]{:S(2)}) copy-start(bf16[1,128,1536]{2,1,0:T(8,128)(2,1)} %param.9) | copy-start | bytes 1179652
  5.2 2.2 %copy-start.3 = (bf16[1,128,1536]{2,1,0:T(8,128)(2,1)S(1)}, bf16[1,128,1536]{2,1,0:T(8,128)(2,1)}, u32[]{:S(2)}) copy-start(bf16[1,128,1536]{2,1,0:T(8,128)(2,1)} %param.10) | copy-start | bytes 1179652
  5.2 2.2 %copy-start.4 = (s32[128,12]{0,1:T(8,128)S(1)}, s32[128,12]{0,1:T(8,128)}, u32[]{:S(2)}) copy-start(s32[128,12]{0,1:T(8,128)} %param.15) | copy-start | bytes 18436
  5.2 2.2 %copy-start.5 = (f32[128]{0:T(128)S(1)}, f32[128]{0:T(128)}, u32[]{:S(2)}) copy-start(f32[128]{0:T(128)} %param.12) | copy-start | bytes 1540
  5.2 2.2 %copy-start.6 = (s32[12,5]{0,1:T(8,128)S(1)}, s32[12,5]{0,1:T(8,128)}, u32[]{:S(2)}) copy-start(s32[12,5]{0,1:T(8,128)} %param.14) | copy-start | bytes 724
  5.2 2.2 %copy-start.7 = (f32[128]{0:T(128)S(1)}, f32[128]{0:T(128)}, u32[]{:S(2)}) copy-start(f32[128]{0:T(128)} %param.13) | copy-start | bytes 1540
  5.2 12.8 %collective-permute-start.2 = (bf16[128,1536]{1,0:T(8,128)(2,1)}, bf16[128,1536]{1,0:T(8,128)(2,1)S(1)}, u32[]{:S(2)}, u32[]{:S(2)}) collective-permute-start(bf16[128,1536]{1,0:T(8,128)(2,1)} %bitcast.20), channel_id=1, source_target_pairs={{1,2},{2,1},{3,4},{4,3},{5,6},{6,5},{7,8},{8,7},{9,10},{10,9},{11,... | collective-permute-start | bytes 1179656 | tf_op jit(solution)/shard_map/ppermute | solution.py:34
  8.4 6.0 %collective-permute-start = (bf16[2,128,1536]{2,1,0:T(8,128)(2,1)S(1)}, bf16[2,128,1536]{2,1,0:T(8,128)(2,1)S(1)}, u32[]{:S(2)}, u32[]{:S(2)}) collective-permute-start(bf16[2,128,1536]{2,1,0:T(8,128)(2,1)S(1)} %get-tuple-element.32.kv_ref), channel_id=1, source_target_pairs={{0,1},{1,0},{2,3},{3,2},{4,5},{5,4},{6,7},{7,6},{8,9},{9,8},{10,11... | collective-permute-start | bytes 2359304 | tf_op jit(solution)/shard_map/ppermute | solution.py:34
  21.0 14.7 %all-to-all-start = ((f32[8,1,128]{2,1,0:T(1,128)}), f32[8,1,128]{2,1,0:T(1,128)S(1)}, u32[]{:S(2)}, u32[]{:S(2)}) async-start(f32[8,1,128]{2,1,0:T(1,128)} %get-tuple-element.52), calls=%async_computation | async-start | bytes 8192 | tf_op jit(solution)/shard_map/all_to_all | solution.py:294
  29.2 20.6 %collective-permute-start.3 = (bf16[2,1536,128]{2,1,0:T(8,128)(2,1)}, bf16[2,1536,128]{2,1,0:T(8,128)(2,1)S(1)}, u32[]{:S(2)}, u32[]{:S(2)}) collective-permute-start(bf16[2,1536,128]{2,1,0:T(8,128)(2,1)} %get-tuple-element.48), channel_id=1, source_target_pairs={{1,2},{2,1},{3,4},{4,3},{5,6},{6,5},{7,8},{8,7},{9,10},{10,9},{11,... | collective-permute-start | bytes 2359304 | tf_op jit(solution)/shard_map/ppermute | solution.py:34
  33.2 16.7 %collective-permute-start.4 = (bf16[2,1536,128]{2,1,0:T(8,128)(2,1)}, bf16[2,1536,128]{2,1,0:T(8,128)(2,1)S(1)}, u32[]{:S(2)}, u32[]{:S(2)}) collective-permute-start(bf16[2,1536,128]{2,1,0:T(8,128)(2,1)} %get-tuple-element.49), channel_id=1, source_target_pairs={{0,1},{1,0},{2,3},{3,2},{4,5},{5,4},{6,7},{7,6},{8,9},{9,8},{10,11... | collective-permute-start | bytes 2359304 | tf_op jit(solution)/shard_map/ppermute | solution.py:34
  36.3 22.9 %all-to-all-start.1 = ((f32[64,1,128]{2,1,0:T(1,128)}), f32[64,1,128]{2,1,0:T(1,128)S(1)}, u32[]{:S(2)}, u32[]{:S(2)}) async-start(f32[64,1,128]{2,1,0:T(1,128)} %shard_map.133), calls=%async_computation.1 | async-start | bytes 65536 | tf_op jit(solution)/shard_map/all_to_all | solution.py:294

commit v6 on v5

--- a/solution.py
+++ b/solution.py
@@ -129,9 +129,15 @@
     rows = qn_ref.shape[0]
     width = gt_ref.shape[0] // mask_ref.shape[1]
     scale = width ** (-0.5)
-    for h, cols in enumerate(head_columns(qn_ref, width)):
-        scores = dot(qn_ref[:, cols], jnp.concatenate([fk_ref[:, cols], near_ref[0, :, cols]], axis=0), NT)
-        dprob_ref[:, cols] = dot(g_ref[:, cols], near_ref[1, :, cols], NT)
+    heads = head_columns(qn_ref, width)
+    count = len(heads)
+
+    def first_stage(h):
+        cols = heads[h]
+        return dot(qn_ref[:, cols], jnp.concatenate([fk_ref[:, cols], near_ref[0, :, cols]], axis=0), NT)
+
+    def middle_stage(h, scores):
+        cols = heads[h]
         terms = [
             masked_terms(scores[:, :rows], scale, mask_ref, h, 0),
             own_ref[0, :, cols],
@@ -141,10 +147,26 @@
         probs = [term * inverse for term in terms]
         for i, p in enumerate(probs):
             probs_ref[i, :, cols] = p
-        weights = jnp.concatenate([p.astype(BF16) for p in probs], axis=1)
+        return jnp.concatenate([p.astype(BF16) for p in probs], axis=1)
+
+    def last_stage(h, weights):
+        cols = heads[h]
+        dprob_ref[:, cols] = dot(g_ref[:, cols], near_ref[1, :, cols], NT)
         val_t = dot(gt_ref[cols, :], weights, NN).astype(BF16)
         for i, ref in enumerate([far_v_ref, own_v_ref, near_v_ref]):
             ref[cols, :] = val_t[:, i * rows : (i + 1) * rows]
+
+    ahead = first_stage(0)
+    behind = None
+    for h in range(count):
+        now = ahead
+        if h + 1 < count:
+            ahead = first_stage(h + 1)
+        now = middle_stage(h, now)
+        if behind is not None:
+            last_stage(h - 1, behind)
+        behind = now
+    last_stage(count - 1, behind)
 
 
 def attend_kernel(

time: 60.1 us -> 58.5 us (0.973)
  Pallas kernels: 10.6 us -> 8.49 us
    pallas_call x8, Pallas kernels: 10.6 us -> 8.49 us  [run(): pl.pallas_call(body, in_specs=in_specs or [whole] * len(args), out_specs=...]
  transfers between devices with their start and end apart: 7 -> 7, of which waited for: 3 -> 3; matrix products, arithmetic and copies ran while one was open for 0% -> 0% of each run, Pallas kernels for 12% -> 8%
where the time goes in v6:
time: 58.5 us; the launch traced here: 58.1 us
  starting transfers between devices  38.6 us (66%)
  waiting for transfers between devices  10.1 us (17%)
  Pallas kernels  8.49 us (15%)
  between operations  0.89 us (2%)
    all_to_all x2, starting transfers between devices, exchange(): return lax.all_to_all(parts, axis, 0, 0)  22.2 us
    ppermute x5, starting transfers between devices, swap(): lax.ppermute(block, 'seq', [(i, j) for i, j in route if 0 <= j < size])  16.5 us
    all_to_all x2, waiting for transfers between devices, exchange(): return lax.all_to_all(parts, axis, 0, 0)  8.5 us
    pallas_call x8, Pallas kernels, run(): pl.pallas_call(body, in_specs=in_specs or [whole] * len(args), out_specs=...  8.49 us
    ppermute x5, waiting for transfers between devices, swap(): lax.ppermute(block, 'seq', [(i, j) for i, j in route if 0 <= j < size])  1.59 us
  transfers between devices with their start and end apart: 7, of which 3 were waited for; matrix products, arithmetic and copies ran while one was open for 0% of the time, Pallas kernels for 8%

profile of v6, /device:TPU:1, one launch (start us, length us, event | category | flops | bytes accessed | tf_op | source)
XLA Modules:
  0.0 58.1 jit_solution(17894451012373999830)
XLA Ops:
  0.6 4.5 %collective-permute-start.1 = (bf16[128,1536]{1,0:T(8,128)(2,1)}, bf16[128,1536]{1,0:T(8,128)(2,1)S(1)}, u32[]{:S(2)}, u32[]{:S(2)}) collective-permute-start(bf16[128,1536]{1,0:T(8,128)(2,1)} %bitcast.18), channel_id=1, source_target_pairs={{1,2},{2,1},{3,4},{4,3},{5,6},{6,5},{7,8},{8,7},{9,10},{10,9},{11,... | collective-permute-start | bytes 1179656 | tf_op jit(solution)/shard_map/ppermute | solution.py:34
  5.2 0.0 copy-start
  5.2 0.0 copy-start.1
  5.2 0.0 copy-start.2
  5.2 2.1 %collective-permute-start.2 = (bf16[128,1536]{1,0:T(8,128)(2,1)}, bf16[128,1536]{1,0:T(8,128)(2,1)S(1)}, u32[]{:S(2)}, u32[]{:S(2)}) collective-permute-start(bf16[128,1536]{1,0:T(8,128)(2,1)} %bitcast.20), channel_id=1, source_target_pairs={{1,2},{2,1},{3,4},{4,3},{5,6},{6,5},{7,8},{8,7},{9,10},{10,9},{11,... | collective-permute-start | bytes 1179656 | tf_op jit(solution)/shard_map/ppermute | solution.py:34
  7.4 1.0 %shard_map.128 = (bf16[128,1536]{1,0:T(8,128)(2,1)S(1)}, bf16[1536,128]{1,0:T(8,128)(2,1)S(1)}, bf16[1536,128]{1,0:T(8,128)(2,1)S(1)}, bf16[2,128,1536]{2,1,0:T(...) custom-call(bf16[128,1536]{1,0:T(8,128)(2,1)S(1)} %bitcast.17, ...), custom_call_target="tpu_custom_call" | custom-call | flops 100663296 | bytes 4194304 | tf_op jit(solution)/shard_map/pallas_call | solution.py:302
  8.4 4.1 %collective-permute-start = (bf16[2,128,1536]{2,1,0:T(8,128)(2,1)S(1)}, bf16[2,128,1536]{2,1,0:T(8,128)(2,1)S(1)}, u32[]{:S(2)}, u32[]{:S(2)}) collective-permute-start(bf16[2,128,1536]{2,1,0:T(8,128)(2,1)S(1)} %get-tuple-element.32.kv_ref), channel_id=1, source_target_pairs={{0,1},{1,0},{2,3},{3,2},{4,5},{5,4},{6,7},{7,6},{8,9},{9,8},{10,11... | collective-permute-start | bytes 2359304 | tf_op jit(solution)/shard_map/ppermute | solution.py:34
  12.5 0.0 collective-permute-done.1.k_ref
  12.5 0.3 shard_map.129.fk_ref
  12.8 1.6 %collective-permute-done.near_ref = bf16[2,128,1536]{2,1,0:T(8,128)(2,1)S(1)} collective-permute-done((bf16[2,128,1536]{2,1,0:T(8,128)(2,1)S(1)}, bf16[2,128,1536]{2,1,0:T(8,128)(2,1)S(1)}, u32[]{:S(2)}, u32[]{:S(2)}) %collective-permute-start) | collective-permute-done | bytes 786464 | tf_op jit(solution)/shard_map/ppermute | solution.py:34
  14.4 1.5 %shard_map.130 = (f32[3,128,1536]{2,1,0:T(8,128)S(1)}, f32[128,1536]{1,0:T(8,128)S(1)}, bf16[1536,128]{1,0:T(8,128)(2,1)S(1)}, bf16[1536,128]{1,0:T(8,128)(2,1)S(1)}, bf16[1536,128]{1,0:T(8,128)(2,1)S(1)}) custom-call(bf16[128,1536]{1,0:T(8,128)(2,1)S(1)} %get-tuple-element.33.qn_ref, bf16[128,1536]{1,0:T(8,128)(2,1)S(1)} %bitcast.15, ...), custom_call_target="tpu_custom_call" | custom-call | flops 301989888 | bytes 4194304 | tf_op jit(solution)/shard_map/pallas_call | solution.py:302
  15.9 0.0 collective-permute-done.2.fv_ref
  15.9 3.0 %shard_map.131 = (bf16[128,1536]{1,0:T(8,128)(2,1)}, bf16[128,1536]{1,0:T(8,128)(2,1)}, bf16[1536,128]{1,0:T(8,128)(2,1)S(1)}, bf16[2,1536,128]{2,1,0:T(8,128)(2...) custom-call(bf16[128,1536]{1,0:T(8,128)(2,1)S(1)} %bitcast.16, bf16[1536,128]{1,0:T(8,128)(2,1)S(1)} %get-tuple-element.31.qt_ref, ...), custom_call_target="tpu_custom_call" | custom-call | flops 553648128 | bytes 4194304 | tf_op jit(solution)/shard_map/pallas_call | solution.py:302
  18.9 9.1 %all-to-all-start = ((f32[8,1,128]{2,1,0:T(1,128)}), f32[8,1,128]{2,1,0:T(1,128)S(1)}, u32[]{:S(2)}, u32[]{:S(2)}) async-start(f32[8,1,128]{2,1,0:T(1,128)} %get-tuple-element.52), calls=%async_computation | async-start | bytes 8192 | tf_op jit(solution)/shard_map/all_to_all | solution.py:316
  28.0 3.9 %collective-permute-start.3 = (bf16[2,1536,128]{2,1,0:T(8,128)(2,1)}, bf16[2,1536,128]{2,1,0:T(8,128)(2,1)S(1)}, u32[]{:S(2)}, u32[]{:S(2)}) collective-permute-start(bf16[2,1536,128]{2,1,0:T(8,128)(2,1)} %get-tuple-element.48), channel_id=1, source_target_pairs={{1,2},{2,1},{3,4},{4,3},{5,6},{6,5},{7,8},{8,7},{9,10},{10,9},{11,... | collective-permute-start | bytes 2359304 | tf_op jit(solution)/shard_map/ppermute | solution.py:34
  32.0 1.9 %collective-permute-start.4 = (bf16[2,1536,128]{2,1,0:T(8,128)(2,1)}, bf16[2,1536,128]{2,1,0:T(8,128)(2,1)S(1)}, u32[]{:S(2)}, u32[]{:S(2)}) collective-permute-start(bf16[2,1536,128]{2,1,0:T(8,128)(2,1)} %get-tuple-element.49), channel_id=1, source_target_pairs={{0,1},{1,0},{2,3},{3,2},{4,5},{5,4},{6,7},{7,6},{8,9},{9,8},{10,11... | collective-permute-start | bytes 2359304 | tf_op jit(solution)/shard_map/ppermute | solution.py:34
  33.9 0.6 %all-to-all-done.parts_ref = f32[8,1,128]{2,1,0:T(1,128)S(1)} async-done(((f32[8,1,128]{2,1,0:T(1,128)}), f32[8,1,128]{2,1,0:T(1,128)S(1)}, u32[]{:S(2)}, u32[]{:S(2)}) %all-to-all-start) | async-done | bytes 4128 | tf_op jit(solution)/shard_map/all_to_all | solution.py:316
  34.5 0.6 %shard_map.133 = f32[64,1,128]{2,1,0:T(1,128)} custom-call(f32[8,1,128]{2,1,0:T(1,128)S(1)} %all-to-all-done.parts_ref), custom_call_target="tpu_custom_call" | custom-call | flops 30000001024 | bytes 4194304 | tf_op jit(solution)/shard_map/pallas_call | solution.py:302
  35.1 13.0 %all-to-all-start.1 = ((f32[64,1,128]{2,1,0:T(1,128)}), f32[64,1,128]{2,1,0:T(1,128)S(1)}, u32[]{:S(2)}, u32[]{:S(2)}) async-start(f32[64,1,128]{2,1,0:T(1,128)} %shard_map.133), calls=%async_computation.1 | async-start | bytes 65536 | tf_op jit(solution)/shard_map/all_to_all | solution.py:316
  48.2 0.0 collective-permute-done.3.far_ref
  48.2 0.0 collective-permute-done.4.near_ref
  48.2 1.5 %shard_map.132 = (bf16[128,1536]{1,0:T(8,128)(2,1)}, bf16[128,1536]{1,0:T(8,128)(2,1)}, f32[1,128]{1,0:T(1,128)S(1)}) custom-call(bf16[1536,128]{1,0:T(8,128)(2,1)S(1)} %get-tuple-element.45.kt_ref, bf16[1536,128]{1,0:T(8,128)(2,1)S(1)} %get-tuple-element.46.own_k_ref, bf16[1536,128]{1,0:T(8,128)(2,1)S(1)} %get-tuple-element.47.own_v_ref, ...), custom_call_target="tpu_custom_call" | custom-call | flops 7864320 | bytes 4194304 | tf_op jit(solution)/shard_map/pallas_call | solution.py:302
  49.7 7.9 %all-to-all-done.1.parts_ref = f32[64,1,128]{2,1,0:T(1,128)S(1)} async-done(((f32[64,1,128]{2,1,0:T(1,128)}), f32[64,1,128]{2,1,0:T(1,128)S(1)}, u32[]{:S(2)}, u32[]{:S(2)}) %all-to-all-start.1) | async-done | bytes 32800 | tf_op jit(solution)/shard_map/all_to_all | solution.py:316
  57.6 0.6 %shard_map.134 = (f32[1,128]{1,0:T(1,128)}, f32[1,128]{1,0:T(1,128)}) custom-call(f32[64,1,128]{2,1,0:T(1,128)S(1)} %all-to-all-done.1.parts_ref, f32[1,128]{1,0:T(1,128)S(1)} %bitcast.25, f32[1,128]{1,0:T(1,128)S(1)} %get-tuple-element.53.inverse_ref), custom_call_target="tpu_custom_call" | custom-call | bytes 4194304 | tf_op jit(solution)/shard_map/pallas_call | solution.py:302
  (14 shorter events, 0.0 us)
Async XLA Ops:
  0.6 11.9 %collective-permute-start.1 = (bf16[128,1536]{1,0:T(8,128)(2,1)}, bf16[128,1536]{1,0:T(8,128)(2,1)S(1)}, u32[]{:S(2)}, u32[]{:S(2)}) collective-permute-start(bf16[128,1536]{1,0:T(8,128)(2,1)} %bitcast.18), channel_id=1, source_target_pairs={{1,2},{2,1},{3,4},{4,3},{5,6},{6,5},{7,8},{8,7},{9,10},{10,9},{11,... | collective-permute-start | bytes 1179656 | tf_op jit(solution)/shard_map/ppermute | solution.py:34
  5.2 2.2 %copy-start = (bf16[1,128,1536]{2,1,0:T(8,128)(2,1)S(1)}, bf16[1,128,1536]{2,1,0:T(8,128)(2,1)}, u32[]{:S(2)}) copy-start(bf16[1,128,1536]{2,1,0:T(8,128)(2,1)} %param.11) | copy-start | bytes 1179652
  5.2 2.2 %copy-start.1 = (bf16[1,128,1536]{2,1,0:T(8,128)(2,1)S(1)}, bf16[1,128,1536]{2,1,0:T(8,128)(2,1)}, u32[]{:S(2)}) copy-start(bf16[1,128,1536]{2,1,0:T(8,128)(2,1)} %param.8) | copy-start | bytes 1179652
  5.2 2.2 %copy-start.2 = (bf16[1,128,1536]{2,1,0:T(8,128)(2,1)S(1)}, bf16[1,128,1536]{2,1,0:T(8,128)(2,1)}, u32[]{:S(2)}) copy-start(bf16[1,128,1536]{2,1,0:T(8,128)(2,1)} %param.9) | copy-start | bytes 1179652
  5.2 2.2 %copy-start.3 = (bf16[1,128,1536]{2,1,0:T(8,128)(2,1)S(1)}, bf16[1,128,1536]{2,1,0:T(8,128)(2,1)}, u32[]{:S(2)}) copy-start(bf16[1,128,1536]{2,1,0:T(8,128)(2,1)} %param.10) | copy-start | bytes 1179652
  5.2 2.2 %copy-start.4 = (s32[128,12]{0,1:T(8,128)S(1)}, s32[128,12]{0,1:T(8,128)}, u32[]{:S(2)}) copy-start(s32[128,12]{0,1:T(8,128)} %param.15) | copy-start | bytes 18436
  5.2 2.2 %copy-start.5 = (f32[128]{0:T(128)S(1)}, f32[128]{0:T(128)}, u32[]{:S(2)}) copy-start(f32[128]{0:T(128)} %param.12) | copy-start | bytes 1540
  5.2 2.2 %copy-start.6 = (s32[12,5]{0,1:T(8,128)S(1)}, s32[12,5]{0,1:T(8,128)}, u32[]{:S(2)}) copy-start(s32[12,5]{0,1:T(8,128)} %param.14) | copy-start | bytes 724
  5.2 2.2 %copy-start.7 = (f32[128]{0:T(128)S(1)}, f32[128]{0:T(128)}, u32[]{:S(2)}) copy-start(f32[128]{0:T(128)} %param.13) | copy-start | bytes 1540
  5.2 10.7 %collective-permute-start.2 = (bf16[128,1536]{1,0:T(8,128)(2,1)}, bf16[128,1536]{1,0:T(8,128)(2,1)S(1)}, u32[]{:S(2)}, u32[]{:S(2)}) collective-permute-start(bf16[128,1536]{1,0:T(8,128)(2,1)} %bitcast.20), channel_id=1, source_target_pairs={{1,2},{2,1},{3,4},{4,3},{5,6},{6,5},{7,8},{8,7},{9,10},{10,9},{11,... | collective-permute-start | bytes 1179656 | tf_op jit(solution)/shard_map/ppermute | solution.py:34
  8.4 6.0 %collective-permute-start = (bf16[2,128,1536]{2,1,0:T(8,128)(2,1)S(1)}, bf16[2,128,1536]{2,1,0:T(8,128)(2,1)S(1)}, u32[]{:S(2)}, u32[]{:S(2)}) collective-permute-start(bf16[2,128,1536]{2,1,0:T(8,128)(2,1)S(1)} %get-tuple-element.32.kv_ref), channel_id=1, source_target_pairs={{0,1},{1,0},{2,3},{3,2},{4,5},{5,4},{6,7},{7,6},{8,9},{9,8},{10,11... | collective-permute-start | bytes 2359304 | tf_op jit(solution)/shard_map/ppermute | solution.py:34
  18.9 15.6 %all-to-all-start = ((f32[8,1,128]{2,1,0:T(1,128)}), f32[8,1,128]{2,1,0:T(1,128)S(1)}, u32[]{:S(2)}, u32[]{:S(2)}) async-start(f32[8,1,128]{2,1,0:T(1,128)} %get-tuple-element.52), calls=%async_computation | async-start | bytes 8192 | tf_op jit(solution)/shard_map/all_to_all | solution.py:316
  28.0 20.1 %collective-permute-start.3 = (bf16[2,1536,128]{2,1,0:T(8,128)(2,1)}, bf16[2,1536,128]{2,1,0:T(8,128)(2,1)S(1)}, u32[]{:S(2)}, u32[]{:S(2)}) collective-permute-start(bf16[2,1536,128]{2,1,0:T(8,128)(2,1)} %get-tuple-element.48), channel_id=1, source_target_pairs={{1,2},{2,1},{3,4},{4,3},{5,6},{6,5},{7,8},{8,7},{9,10},{10,9},{11,... | collective-permute-start | bytes 2359304 | tf_op jit(solution)/shard_map/ppermute | solution.py:34
  32.0 16.2 %collective-permute-start.4 = (bf16[2,1536,128]{2,1,0:T(8,128)(2,1)}, bf16[2,1536,128]{2,1,0:T(8,128)(2,1)S(1)}, u32[]{:S(2)}, u32[]{:S(2)}) collective-permute-start(bf16[2,1536,128]{2,1,0:T(8,128)(2,1)} %get-tuple-element.49), channel_id=1, source_target_pairs={{0,1},{1,0},{2,3},{3,2},{4,5},{5,4},{6,7},{7,6},{8,9},{9,8},{10,11... | collective-permute-start | bytes 2359304 | tf_op jit(solution)/shard_map/ppermute | solution.py:34
  35.1 22.4 %all-to-all-start.1 = ((f32[64,1,128]{2,1,0:T(1,128)}), f32[64,1,128]{2,1,0:T(1,128)S(1)}, u32[]{:S(2)}, u32[]{:S(2)}) async-start(f32[64,1,128]{2,1,0:T(1,128)} %shard_map.133), calls=%async_computation.1 | async-start | bytes 65536 | tf_op jit(solution)/shard_map/all_to_all | solution.py:316

commit v7 on v6

--- a/solution.py
+++ b/solution.py
@@ -352,10 +352,10 @@
         [like(3, rows, columns, dtype=F32), wide, turned, turned, turned],
         6 * products,
     )(qn, g, gt, near, far_k, mask, terms)
-    spread_dp = like(lax.axis_size("dp"), 1, width, dtype=F32)
+    spread_one = like(lax.axis_size("seq"), 1, width, dtype=F32)
     out, q_grad, own_k_part, to_far, to_near, spread = call(
         attend_kernel,
-        [far_away(flat), far_away(flat), turned, far_away(part), far_away(part), far_away(spread_dp)],
+        [far_away(flat), far_away(flat), turned, far_away(part), far_away(part), far_away(spread_one)],
         11 * products,
         out_specs=[hbm, hbm, vmem, hbm, hbm, hbm],
         scratch=[
@@ -363,7 +363,7 @@
             pltpu.VMEM((rows, columns), BF16),
             pltpu.VMEM((columns, rows), BF16),
             pltpu.VMEM((columns, rows), BF16),
-            pltpu.VMEM(spread_dp.shape, F32),
+            pltpu.VMEM(spread_one.shape, F32),
             pltpu.SemaphoreType.DMA((heads // GROUP + 1, 4)),
         ],
     )(g, qt, kv, near, far_k, far_v, probs, dprob, far_v_part, near_v_part, unit, inverse, terms, q_row)
@@ -380,9 +380,9 @@
             pltpu.SemaphoreType.DMA((heads // STEP, 2)),
         ],
     )(kt, own_k_part, own_v_part, from_far, from_near, k_row)
-    spread_seq = like(lax.axis_size("seq"), 1, width, dtype=F32)
-    (spread,) = call(combine_kernel, [spread_seq], COMBINE)(exchange(spread, "dp"))
-    parts = exchange(spread, "seq")
+    spread_two = like(lax.axis_size("dp"), 1, width, dtype=F32)
+    (spread,) = call(combine_kernel, [spread_two], COMBINE)(exchange(spread, "seq"))
+    parts = exchange(spread, "dp")
     gains = [like(1, width, dtype=F32)] * 2
     q_gain_grad, k_gain_grad = call(gain_kernel, gains, 0)(parts, q_row, inverse_gain)
     return (

time: 58.5 us -> 57.4 us (0.981)
  starting transfers between devices: 38.6 us -> 37.3 us
    all_to_all x2, starting transfers between devices: 22.2 us -> 21.2 us  [exchange(): return lax.all_to_all(parts, axis, 0, 0)]
  transfers between devices with their start and end apart: 7 -> 7, of which waited for: 3 -> 3; matrix products, arithmetic and copies ran while one was open for 0% -> 0% of each run, Pallas kernels for 8% -> 9%
where the time goes in v7:
time: 57.4 us; the launch traced here: 57.1 us
  starting transfers between devices  37.3 us (65%)
  waiting for transfers between devices  10.4 us (18%)
  Pallas kernels  8.48 us (15%)
  between operations  0.88 us (2%)
    all_to_all x2, starting transfers between devices, exchange(): return lax.all_to_all(parts, axis, 0, 0)  21.2 us
    ppermute x5, starting transfers between devices, swap(): lax.ppermute(block, 'seq', [(i, j) for i, j in route if 0 <= j < size])  16.1 us
    all_to_all x2, waiting for transfers between devices, exchange(): return lax.all_to_all(parts, axis, 0, 0)  8.85 us
    pallas_call x8, Pallas kernels, run(): pl.pallas_call(body, in_specs=in_specs or [whole] * len(args), out_specs=...  8.48 us
    ppermute x5, waiting for transfers between devices, swap(): lax.ppermute(block, 'seq', [(i, j) for i, j in route if 0 <= j < size])  1.59 us
  transfers between devices with their start and end apart: 7, of which 3 were waited for; matrix products, arithmetic and copies ran while one was open for 0% of the time, Pallas kernels for 9%

profile of v7, /device:TPU:1, one launch (start us, length us, event | category | flops | bytes accessed | tf_op | source)
XLA Modules:
  0.0 57.1 jit_solution(16288943305831797054)
XLA Ops:
  0.6 4.5 %collective-permute-start.1 = (bf16[128,1536]{1,0:T(8,128)(2,1)}, bf16[128,1536]{1,0:T(8,128)(2,1)S(1)}, u32[]{:S(2)}, u32[]{:S(2)}) collective-permute-start(bf16[128,1536]{1,0:T(8,128)(2,1)} %bitcast.18), channel_id=1, source_target_pairs={{1,2},{2,1},{3,4},{4,3},{5,6},{6,5},{7,8},{8,7},{9,10},{10,9},{11,... | collective-permute-start | bytes 1179656 | tf_op jit(solution)/shard_map/ppermute | solution.py:34
  5.2 0.0 copy-start
  5.2 0.0 copy-start.1
  5.2 0.0 copy-start.2
  5.2 2.1 %collective-permute-start.2 = (bf16[128,1536]{1,0:T(8,128)(2,1)}, bf16[128,1536]{1,0:T(8,128)(2,1)S(1)}, u32[]{:S(2)}, u32[]{:S(2)}) collective-permute-start(bf16[128,1536]{1,0:T(8,128)(2,1)} %bitcast.20), channel_id=1, source_target_pairs={{1,2},{2,1},{3,4},{4,3},{5,6},{6,5},{7,8},{8,7},{9,10},{10,9},{11,... | collective-permute-start | bytes 1179656 | tf_op jit(solution)/shard_map/ppermute | solution.py:34
  7.4 1.0 %shard_map.128 = (bf16[128,1536]{1,0:T(8,128)(2,1)S(1)}, bf16[1536,128]{1,0:T(8,128)(2,1)S(1)}, bf16[1536,128]{1,0:T(8,128)(2,1)S(1)}, bf16[2,128,1536]{2,1,0:T(...) custom-call(bf16[128,1536]{1,0:T(8,128)(2,1)S(1)} %bitcast.17, ...), custom_call_target="tpu_custom_call" | custom-call | flops 100663296 | bytes 4194304 | tf_op jit(solution)/shard_map/pallas_call | solution.py:302
  8.4 4.1 %collective-permute-start = (bf16[2,128,1536]{2,1,0:T(8,128)(2,1)S(1)}, bf16[2,128,1536]{2,1,0:T(8,128)(2,1)S(1)}, u32[]{:S(2)}, u32[]{:S(2)}) collective-permute-start(bf16[2,128,1536]{2,1,0:T(8,128)(2,1)S(1)} %get-tuple-element.32.kv_ref), channel_id=1, source_target_pairs={{0,1},{1,0},{2,3},{3,2},{4,5},{5,4},{6,7},{7,6},{8,9},{9,8},{10,11... | collective-permute-start | bytes 2359304 | tf_op jit(solution)/shard_map/ppermute | solution.py:34
  12.5 0.0 collective-permute-done.1.k_ref
  12.5 0.3 shard_map.129.fk_ref
  12.8 1.6 %collective-permute-done.near_ref = bf16[2,128,1536]{2,1,0:T(8,128)(2,1)S(1)} collective-permute-done((bf16[2,128,1536]{2,1,0:T(8,128)(2,1)S(1)}, bf16[2,128,1536]{2,1,0:T(8,128)(2,1)S(1)}, u32[]{:S(2)}, u32[]{:S(2)}) %collective-permute-start) | collective-permute-done | bytes 786464 | tf_op jit(solution)/shard_map/ppermute | solution.py:34
  14.4 1.5 %shard_map.130 = (f32[3,128,1536]{2,1,0:T(8,128)S(1)}, f32[128,1536]{1,0:T(8,128)S(1)}, bf16[1536,128]{1,0:T(8,128)(2,1)S(1)}, bf16[1536,128]{1,0:T(8,128)(2,1)S(1)}, bf16[1536,128]{1,0:T(8,128)(2,1)S(1)}) custom-call(bf16[128,1536]{1,0:T(8,128)(2,1)S(1)} %get-tuple-element.33.qn_ref, bf16[128,1536]{1,0:T(8,128)(2,1)S(1)} %bitcast.15, ...), custom_call_target="tpu_custom_call" | custom-call | flops 301989888 | bytes 4194304 | tf_op jit(solution)/shard_map/pallas_call | solution.py:302
  15.9 0.0 collective-permute-done.2.fv_ref
  15.9 3.0 %shard_map.131 = (bf16[128,1536]{1,0:T(8,128)(2,1)}, bf16[128,1536]{1,0:T(8,128)(2,1)}, bf16[1536,128]{1,0:T(8,128)(2,1)S(1)}, bf16[2,1536,128]{2,1,0:T(8,128)(2...) custom-call(bf16[128,1536]{1,0:T(8,128)(2,1)S(1)} %bitcast.16, ...), custom_call_target="tpu_custom_call" | custom-call | flops 553648128 | bytes 4194304 | tf_op jit(solution)/shard_map/pallas_call | solution.py:302
  18.9 11.1 %all-to-all-start = ((f32[64,1,128]{2,1,0:T(1,128)}), f32[64,1,128]{2,1,0:T(1,128)S(1)}, u32[]{:S(2)}, u32[]{:S(2)}) async-start(f32[64,1,128]{2,1,0:T(1,128)} %get-tuple-element.52), calls=%async_computation | async-start | bytes 65536 | tf_op jit(solution)/shard_map/all_to_all | solution.py:316
  30.1 3.5 %collective-permute-start.3 = (bf16[2,1536,128]{2,1,0:T(8,128)(2,1)}, bf16[2,1536,128]{2,1,0:T(8,128)(2,1)S(1)}, u32[]{:S(2)}, u32[]{:S(2)}) collective-permute-start(bf16[2,1536,128]{2,1,0:T(8,128)(2,1)} %get-tuple-element.48), channel_id=1, source_target_pairs={{1,2},{2,1},{3,4},{4,3},{5,6},{6,5},{7,8},{8,7},{9,10},{10,9},{11,... | collective-permute-start | bytes 2359304 | tf_op jit(solution)/shard_map/ppermute | solution.py:34
  33.6 1.9 %collective-permute-start.4 = (bf16[2,1536,128]{2,1,0:T(8,128)(2,1)}, bf16[2,1536,128]{2,1,0:T(8,128)(2,1)S(1)}, u32[]{:S(2)}, u32[]{:S(2)}) collective-permute-start(bf16[2,1536,128]{2,1,0:T(8,128)(2,1)} %get-tuple-element.49), channel_id=1, source_target_pairs={{0,1},{1,0},{2,3},{3,2},{4,5},{5,4},{6,7},{7,6},{8,9},{9,8},{10,11... | collective-permute-start | bytes 2359304 | tf_op jit(solution)/shard_map/ppermute | solution.py:34
  35.6 3.8 %all-to-all-done.parts_ref = f32[64,1,128]{2,1,0:T(1,128)S(1)} async-done(((f32[64,1,128]{2,1,0:T(1,128)}), f32[64,1,128]{2,1,0:T(1,128)S(1)}, u32[]{:S(2)}, u32[]{:S(2)}) %all-to-all-start) | async-done | bytes 32800 | tf_op jit(solution)/shard_map/all_to_all | solution.py:316
  39.4 0.7 %shard_map.133 = f32[8,1,128]{2,1,0:T(1,128)} custom-call(f32[64,1,128]{2,1,0:T(1,128)S(1)} %all-to-all-done.parts_ref), custom_call_target="tpu_custom_call" | custom-call | flops 30000001024 | bytes 4194304 | tf_op jit(solution)/shard_map/pallas_call | solution.py:302
  40.0 10.0 %all-to-all-start.1 = ((f32[8,1,128]{2,1,0:T(1,128)}), f32[8,1,128]{2,1,0:T(1,128)S(1)}, u32[]{:S(2)}, u32[]{:S(2)}) async-start(f32[8,1,128]{2,1,0:T(1,128)} %shard_map.133), calls=%async_computation.1 | async-start | bytes 8192 | tf_op jit(solution)/shard_map/all_to_all | solution.py:316
  50.1 0.0 collective-permute-done.3.far_ref
  50.1 0.0 collective-permute-done.4.near_ref
  50.1 1.5 %shard_map.132 = (bf16[128,1536]{1,0:T(8,128)(2,1)}, bf16[128,1536]{1,0:T(8,128)(2,1)}, f32[1,128]{1,0:T(1,128)S(1)}) custom-call(bf16[1536,128]{1,0:T(8,128)(2,1)S(1)} %get-tuple-element.45.kt_ref, bf16[1536,128]{1,0:T(8,128)(2,1)S(1)} %get-tuple-element.46.own_k_ref, bf16[1536,128]{1,0:T(8,128)(2,1)S(1)} %get-tuple-element.47.own_v_ref, ...), custom_call_target="tpu_custom_call" | custom-call | flops 7864320 | bytes 4194304 | tf_op jit(solution)/shard_map/pallas_call | solution.py:302
  51.6 5.0 %all-to-all-done.1.parts_ref = f32[8,1,128]{2,1,0:T(1,128)S(1)} async-done(((f32[8,1,128]{2,1,0:T(1,128)}), f32[8,1,128]{2,1,0:T(1,128)S(1)}, u32[]{:S(2)}, u32[]{:S(2)}) %all-to-all-start.1) | async-done | bytes 4128 | tf_op jit(solution)/shard_map/all_to_all | solution.py:316
  56.6 0.5 shard_map.134
  (14 shorter events, 0.0 us)
Async XLA Ops:
  0.6 11.9 %collective-permute-start.1 = (bf16[128,1536]{1,0:T(8,128)(2,1)}, bf16[128,1536]{1,0:T(8,128)(2,1)S(1)}, u32[]{:S(2)}, u32[]{:S(2)}) collective-permute-start(bf16[128,1536]{1,0:T(8,128)(2,1)} %bitcast.18), channel_id=1, source_target_pairs={{1,2},{2,1},{3,4},{4,3},{5,6},{6,5},{7,8},{8,7},{9,10},{10,9},{11,... | collective-permute-start | bytes 1179656 | tf_op jit(solution)/shard_map/ppermute | solution.py:34
  5.2 2.2 %copy-start = (bf16[1,128,1536]{2,1,0:T(8,128)(2,1)S(1)}, bf16[1,128,1536]{2,1,0:T(8,128)(2,1)}, u32[]{:S(2)}) copy-start(bf16[1,128,1536]{2,1,0:T(8,128)(2,1)} %param.11) | copy-start | bytes 1179652
  5.2 2.2 %copy-start.1 = (bf16[1,128,1536]{2,1,0:T(8,128)(2,1)S(1)}, bf16[1,128,1536]{2,1,0:T(8,128)(2,1)}, u32[]{:S(2)}) copy-start(bf16[1,128,1536]{2,1,0:T(8,128)(2,1)} %param.8) | copy-start | bytes 1179652
  5.2 2.2 %copy-start.2 = (bf16[1,128,1536]{2,1,0:T(8,128)(2,1)S(1)}, bf16[1,128,1536]{2,1,0:T(8,128)(2,1)}, u32[]{:S(2)}) copy-start(bf16[1,128,1536]{2,1,0:T(8,128)(2,1)} %param.9) | copy-start | bytes 1179652
  5.2 2.2 %copy-start.3 = (bf16[1,128,1536]{2,1,0:T(8,128)(2,1)S(1)}, bf16[1,128,1536]{2,1,0:T(8,128)(2,1)}, u32[]{:S(2)}) copy-start(bf16[1,128,1536]{2,1,0:T(8,128)(2,1)} %param.10) | copy-start | bytes 1179652
  5.2 2.2 %copy-start.4 = (s32[128,12]{0,1:T(8,128)S(1)}, s32[128,12]{0,1:T(8,128)}, u32[]{:S(2)}) copy-start(s32[128,12]{0,1:T(8,128)} %param.15) | copy-start | bytes 18436
  5.2 2.2 %copy-start.5 = (f32[128]{0:T(128)S(1)}, f32[128]{0:T(128)}, u32[]{:S(2)}) copy-start(f32[128]{0:T(128)} %param.12) | copy-start | bytes 1540
  5.2 2.2 %copy-start.6 = (s32[12,5]{0,1:T(8,128)S(1)}, s32[12,5]{0,1:T(8,128)}, u32[]{:S(2)}) copy-start(s32[12,5]{0,1:T(8,128)} %param.14) | copy-start | bytes 724
  5.2 2.2 %copy-start.7 = (f32[128]{0:T(128)S(1)}, f32[128]{0:T(128)}, u32[]{:S(2)}) copy-start(f32[128]{0:T(128)} %param.13) | copy-start | bytes 1540
  5.2 10.7 %collective-permute-start.2 = (bf16[128,1536]{1,0:T(8,128)(2,1)}, bf16[128,1536]{1,0:T(8,128)(2,1)S(1)}, u32[]{:S(2)}, u32[]{:S(2)}) collective-permute-start(bf16[128,1536]{1,0:T(8,128)(2,1)} %bitcast.20), channel_id=1, source_target_pairs={{1,2},{2,1},{3,4},{4,3},{5,6},{6,5},{7,8},{8,7},{9,10},{10,9},{11,... | collective-permute-start | bytes 1179656 | tf_op jit(solution)/shard_map/ppermute | solution.py:34
  8.4 6.0 %collective-permute-start = (bf16[2,128,1536]{2,1,0:T(8,128)(2,1)S(1)}, bf16[2,128,1536]{2,1,0:T(8,128)(2,1)S(1)}, u32[]{:S(2)}, u32[]{:S(2)}) collective-permute-start(bf16[2,128,1536]{2,1,0:T(8,128)(2,1)S(1)} %get-tuple-element.32.kv_ref), channel_id=1, source_target_pairs={{0,1},{1,0},{2,3},{3,2},{4,5},{5,4},{6,7},{7,6},{8,9},{9,8},{10,11... | collective-permute-start | bytes 2359304 | tf_op jit(solution)/shard_map/ppermute | solution.py:34
  18.9 20.4 %all-to-all-start = ((f32[64,1,128]{2,1,0:T(1,128)}), f32[64,1,128]{2,1,0:T(1,128)S(1)}, u32[]{:S(2)}, u32[]{:S(2)}) async-start(f32[64,1,128]{2,1,0:T(1,128)} %get-tuple-element.52), calls=%async_computation | async-start | bytes 65536 | tf_op jit(solution)/shard_map/all_to_all | solution.py:316
  30.1 20.0 %collective-permute-start.3 = (bf16[2,1536,128]{2,1,0:T(8,128)(2,1)}, bf16[2,1536,128]{2,1,0:T(8,128)(2,1)S(1)}, u32[]{:S(2)}, u32[]{:S(2)}) collective-permute-start(bf16[2,1536,128]{2,1,0:T(8,128)(2,1)} %get-tuple-element.48), channel_id=1, source_target_pairs={{1,2},{2,1},{3,4},{4,3},{5,6},{6,5},{7,8},{8,7},{9,10},{10,9},{11,... | collective-permute-start | bytes 2359304 | tf_op jit(solution)/shard_map/ppermute | solution.py:34
  33.6 16.5 %collective-permute-start.4 = (bf16[2,1536,128]{2,1,0:T(8,128)(2,1)}, bf16[2,1536,128]{2,1,0:T(8,128)(2,1)S(1)}, u32[]{:S(2)}, u32[]{:S(2)}) collective-permute-start(bf16[2,1536,128]{2,1,0:T(8,128)(2,1)} %get-tuple-element.49), channel_id=1, source_target_pairs={{0,1},{1,0},{2,3},{3,2},{4,5},{5,4},{6,7},{7,6},{8,9},{9,8},{10,11... | collective-permute-start | bytes 2359304 | tf_op jit(solution)/shard_map/ppermute | solution.py:34
  40.0 16.6 %all-to-all-start.1 = ((f32[8,1,128]{2,1,0:T(1,128)}), f32[8,1,128]{2,1,0:T(1,128)S(1)}, u32[]{:S(2)}, u32[]{:S(2)}) async-start(f32[8,1,128]{2,1,0:T(1,128)} %shard_map.133), calls=%async_computation.1 | async-start | bytes 8192 | tf_op jit(solution)/shard_map/all_to_all | solution.py:316

commit v8 on v7

--- a/solution.py
+++ b/solution.py
@@ -124,7 +124,8 @@
 
 
 def side_kernel(
-    qn_ref, g_ref, gt_ref, near_ref, fk_ref, mask_ref, own_ref, probs_ref, dprob_ref, far_v_ref, own_v_ref, near_v_ref
+    qn_ref, g_ref, gt_ref, near_ref, fk_ref, kv_ref, mask_ref, own_ref,
+    probs_ref, dprob_ref, sum_ref, far_v_ref, own_v_ref, near_v_ref,
 ):
     rows = qn_ref.shape[0]
     width = gt_ref.shape[0] // mask_ref.shape[1]
@@ -152,6 +153,8 @@
     def last_stage(h, weights):
         cols = heads[h]
         dprob_ref[:, cols] = dot(g_ref[:, cols], near_ref[1, :, cols], NT)
+        vals = jnp.concatenate([kv_ref[1, :, cols], near_ref[1, :, cols]], axis=0)
+        sum_ref[:, cols] = dot(weights[:, rows:], vals, NN)
         val_t = dot(gt_ref[cols, :], weights, NN).astype(BF16)
         for i, ref in enumerate([far_v_ref, own_v_ref, near_v_ref]):
             ref[cols, :] = val_t[:, i * rows : (i + 1) * rows]
@@ -170,7 +173,7 @@
 
 
 def attend_kernel(
-    g_ref, qt_ref, kv_ref, near_ref, fk_ref, fv_ref, probs_ref, dprob_ref, far_v_ref, near_v_ref,
+    g_ref, qt_ref, kv_ref, near_ref, fk_ref, fv_ref, probs_ref, dprob_ref, sum_ref, far_v_ref, near_v_ref,
     unit_ref, inverse_ref, terms_ref, qgain_ref,
     out_hbm, qgrad_hbm, own_ref, far_hbm, near_hbm, spread_hbm,
     out_ref, qgrad_ref, to_far_ref, to_near_ref, spread_ref, sems,
@@ -199,15 +202,13 @@
             probs[0] * dprobs[0] + probs[1] * dprobs[1] + probs[2] * dprobs[2], axis=1, keepdims=True
         )
         dscore = [(p * (d - delta)).astype(BF16) for p, d in zip(probs, dprobs)]
-        weights = [p.astype(BF16) for p in probs]
-        return jnp.concatenate(dscore, axis=1), jnp.concatenate(weights, axis=1)
-
-    def last_stage(h, dscore, weights, total_gain):
+        return jnp.concatenate(dscore, axis=1), probs[0].astype(BF16)
+
+    def last_stage(h, dscore, far_weights, total_gain):
         cols = heads[h]
         keys = jnp.concatenate([fk_ref[:, cols], kv_ref[0, :, cols], near_ref[0, :, cols]], axis=0)
-        vals = jnp.concatenate([fv_ref[:, cols], kv_ref[1, :, cols], near_ref[1, :, cols]], axis=0)
         grad_qn = dot(dscore, keys, NN) * scale
-        out_ref[:, cols] = dot(weights, vals, NN).astype(BF16)
+        out_ref[:, cols] = (sum_ref[:, cols] + dot(far_weights, fv_ref[:, cols], NN)).astype(BF16)
         key_t = dot(qt_ref[cols, :], dscore, NN) * scale
         own_ref[cols, :] = key_t[:, rows : 2 * rows].astype(BF16)
         to_far_ref[cols, :] = key_t[:, :rows].astype(BF16)
@@ -347,11 +348,11 @@
     )(q, k, v, g, offsets.T, counts.T, identity, q_row, k_row)
     near = swap(kv, 0)
     (far_k,) = call(far_kernel, [flat], 2 * IDLE)(far_k, k_row)
-    probs, dprob, far_v_part, own_v_part, near_v_part = call(
+    probs, dprob, near_sum, far_v_part, own_v_part, near_v_part = call(
         side_kernel,
-        [like(3, rows, columns, dtype=F32), wide, turned, turned, turned],
+        [like(3, rows, columns, dtype=F32), wide, wide, turned, turned, turned],
         6 * products,
-    )(qn, g, gt, near, far_k, mask, terms)
+    )(qn, g, gt, near, far_k, kv, mask, terms)
     spread_one = like(lax.axis_size("seq"), 1, width, dtype=F32)
     out, q_grad, own_k_part, to_far, to_near, spread = call(
         attend_kernel,
@@ -366,7 +367,7 @@
             pltpu.VMEM(spread_one.shape, F32),
             pltpu.SemaphoreType.DMA((heads // GROUP + 1, 4)),
         ],
-    )(g, qt, kv, near, far_k, far_v, probs, dprob, far_v_part, near_v_part, unit, inverse, terms, q_row)
+    )(g, qt, kv, near, far_k, far_v, probs, dprob, near_sum, far_v_part, near_v_part, unit, inverse, terms, q_row)
     from_far = swap(to_far, 1)
     from_near = swap(to_near, 0)
     k_grad, v_grad, inverse_gain = call(

time: 57.4 us -> 57.3 us (level)
  no operation moved by 1% of the time
where the time goes in v8:
time: 57.3 us; the launch traced here: 57 us
  starting transfers between devices  37.2 us (65%)
  waiting for transfers between devices  10.4 us (18%)
  Pallas kernels  8.41 us (15%)
  between operations  0.88 us (2%)
    all_to_all x2, starting transfers between devices, exchange(): return lax.all_to_all(parts, axis, 0, 0)  21.1 us
    ppermute x5, starting transfers between devices, swap(): lax.ppermute(block, 'seq', [(i, j) for i, j in route if 0 <= j < size])  16.1 us
    all_to_all x2, waiting for transfers between devices, exchange(): return lax.all_to_all(parts, axis, 0, 0)  8.85 us
    pallas_call x8, Pallas kernels, run(): pl.pallas_call(body, in_specs=in_specs or [whole] * len(args), out_specs=...  8.41 us
    ppermute x5, waiting for transfers between devices, swap(): lax.ppermute(block, 'seq', [(i, j) for i, j in route if 0 <= j < size])  1.59 us
  transfers between devices with their start and end apart: 7, of which 3 were waited for; matrix products, arithmetic and copies ran while one was open for 0% of the time, Pallas kernels for 9%

profile of v8, /device:TPU:1, one launch (start us, length us, event | category | flops | bytes accessed | tf_op | source)
XLA Modules:
  0.0 57.0 jit_solution(16807626001806312049)
XLA Ops:
  0.6 4.5 %collective-permute-start.1 = (bf16[128,1536]{1,0:T(8,128)(2,1)}, bf16[128,1536]{1,0:T(8,128)(2,1)S(1)}, u32[]{:S(2)}, u32[]{:S(2)}) collective-permute-start(bf16[128,1536]{1,0:T(8,128)(2,1)} %bitcast.18), channel_id=1, source_target_pairs={{1,2},{2,1},{3,4},{4,3},{5,6},{6,5},{7,8},{8,7},{9,10},{10,9},{11,... | collective-permute-start | bytes 1179656 | tf_op jit(solution)/shard_map/ppermute | solution.py:34
  5.2 0.0 copy-start
  5.2 0.0 copy-start.1
  5.2 0.0 copy-start.2
  5.2 2.1 %collective-permute-start.2 = (bf16[128,1536]{1,0:T(8,128)(2,1)}, bf16[128,1536]{1,0:T(8,128)(2,1)S(1)}, u32[]{:S(2)}, u32[]{:S(2)}) collective-permute-start(bf16[128,1536]{1,0:T(8,128)(2,1)} %bitcast.20), channel_id=1, source_target_pairs={{1,2},{2,1},{3,4},{4,3},{5,6},{6,5},{7,8},{8,7},{9,10},{10,9},{11,... | collective-permute-start | bytes 1179656 | tf_op jit(solution)/shard_map/ppermute | solution.py:34
  7.4 1.0 %shard_map.128 = (bf16[128,1536]{1,0:T(8,128)(2,1)S(1)}, bf16[1536,128]{1,0:T(8,128)(2,1)S(1)}, bf16[1536,128]{1,0:T(8,128)(2,1)S(1)}, bf16[2,128,1536]{2,1,0:T(...) custom-call(bf16[128,1536]{1,0:T(8,128)(2,1)S(1)} %bitcast.17, ...), custom_call_target="tpu_custom_call" | custom-call | flops 100663296 | bytes 4194304 | tf_op jit(solution)/shard_map/pallas_call | solution.py:303
  8.4 4.1 %collective-permute-start = (bf16[2,128,1536]{2,1,0:T(8,128)(2,1)S(1)}, bf16[2,128,1536]{2,1,0:T(8,128)(2,1)S(1)}, u32[]{:S(2)}, u32[]{:S(2)}) collective-permute-start(bf16[2,128,1536]{2,1,0:T(8,128)(2,1)S(1)} %get-tuple-element.33.kv_ref), channel_id=1, source_target_pairs={{0,1},{1,0},{2,3},{3,2},{4,5},{5,4},{6,7},{7,6},{8,9},{9,8},{10,11... | collective-permute-start | bytes 2359304 | tf_op jit(solution)/shard_map/ppermute | solution.py:34
  12.5 0.0 collective-permute-done.1.k_ref
  12.5 0.3 shard_map.129.fk_ref
  12.8 1.6 %collective-permute-done.near_ref = bf16[2,128,1536]{2,1,0:T(8,128)(2,1)S(1)} collective-permute-done((bf16[2,128,1536]{2,1,0:T(8,128)(2,1)S(1)}, bf16[2,128,1536]{2,1,0:T(8,128)(2,1)S(1)}, u32[]{:S(2)}, u32[]{:S(2)}) %collective-permute-start) | collective-permute-done | bytes 786464 | tf_op jit(solution)/shard_map/ppermute | solution.py:34
  14.4 1.5 %shard_map.130 = (f32[3,128,1536]{2,1,0:T(8,128)S(1)}, f32[128,1536]{1,0:T(8,128)S(1)}, f32[128,1536]{1,0:T(8,128)S(1)}, bf16[1536,128]{1,0:T(8,128)(2,1)S(1)}, ...) custom-call(bf16[128,1536]{1,0:T(8,128)(2,1)S(1)} %get-tuple-element.34.qn_ref, ...), custom_call_target="tpu_custom_call" | custom-call | flops 301989888 | bytes 4194304 | tf_op jit(solution)/shard_map/pallas_call | solution.py:303
  16.0 0.0 collective-permute-done.2.fv_ref
  16.0 2.9 %shard_map.131 = (bf16[128,1536]{1,0:T(8,128)(2,1)}, bf16[128,1536]{1,0:T(8,128)(2,1)}, bf16[1536,128]{1,0:T(8,128)(2,1)S(1)}, bf16[2,1536,128]{2,1,0:T(8,128)(2...) custom-call(bf16[128,1536]{1,0:T(8,128)(2,1)S(1)} %bitcast.16, ...), custom_call_target="tpu_custom_call" | custom-call | flops 553648128 | bytes 4194304 | tf_op jit(solution)/shard_map/pallas_call | solution.py:303
  18.9 11.1 %all-to-all-start = ((f32[64,1,128]{2,1,0:T(1,128)}), f32[64,1,128]{2,1,0:T(1,128)S(1)}, u32[]{:S(2)}, u32[]{:S(2)}) async-start(f32[64,1,128]{2,1,0:T(1,128)} %get-tuple-element.54), calls=%async_computation | async-start | bytes 65536 | tf_op jit(solution)/shard_map/all_to_all | solution.py:317
  30.0 3.5 %collective-permute-start.3 = (bf16[2,1536,128]{2,1,0:T(8,128)(2,1)}, bf16[2,1536,128]{2,1,0:T(8,128)(2,1)S(1)}, u32[]{:S(2)}, u32[]{:S(2)}) collective-permute-start(bf16[2,1536,128]{2,1,0:T(8,128)(2,1)} %get-tuple-element.50), channel_id=1, source_target_pairs={{1,2},{2,1},{3,4},{4,3},{5,6},{6,5},{7,8},{8,7},{9,10},{10,9},{11,... | collective-permute-start | bytes 2359304 | tf_op jit(solution)/shard_map/ppermute | solution.py:34
  33.5 1.9 %collective-permute-start.4 = (bf16[2,1536,128]{2,1,0:T(8,128)(2,1)}, bf16[2,1536,128]{2,1,0:T(8,128)(2,1)S(1)}, u32[]{:S(2)}, u32[]{:S(2)}) collective-permute-start(bf16[2,1536,128]{2,1,0:T(8,128)(2,1)} %get-tuple-element.51), channel_id=1, source_target_pairs={{0,1},{1,0},{2,3},{3,2},{4,5},{5,4},{6,7},{7,6},{8,9},{9,8},{10,11... | collective-permute-start | bytes 2359304 | tf_op jit(solution)/shard_map/ppermute | solution.py:34
  35.4 3.8 %all-to-all-done.parts_ref = f32[64,1,128]{2,1,0:T(1,128)S(1)} async-done(((f32[64,1,128]{2,1,0:T(1,128)}), f32[64,1,128]{2,1,0:T(1,128)S(1)}, u32[]{:S(2)}, u32[]{:S(2)}) %all-to-all-start) | async-done | bytes 32800 | tf_op jit(solution)/shard_map/all_to_all | solution.py:317
  39.3 0.7 %shard_map.133 = f32[8,1,128]{2,1,0:T(1,128)} custom-call(f32[64,1,128]{2,1,0:T(1,128)S(1)} %all-to-all-done.parts_ref), custom_call_target="tpu_custom_call" | custom-call | flops 30000001024 | bytes 4194304 | tf_op jit(solution)/shard_map/pallas_call | solution.py:303
  39.9 10.0 %all-to-all-start.1 = ((f32[8,1,128]{2,1,0:T(1,128)}), f32[8,1,128]{2,1,0:T(1,128)S(1)}, u32[]{:S(2)}, u32[]{:S(2)}) async-start(f32[8,1,128]{2,1,0:T(1,128)} %shard_map.133), calls=%async_computation.1 | async-start | bytes 8192 | tf_op jit(solution)/shard_map/all_to_all | solution.py:317
  50.0 0.0 collective-permute-done.3.far_ref
  50.0 0.0 collective-permute-done.4.near_ref
  50.0 1.5 %shard_map.132 = (bf16[128,1536]{1,0:T(8,128)(2,1)}, bf16[128,1536]{1,0:T(8,128)(2,1)}, f32[1,128]{1,0:T(1,128)S(1)}) custom-call(bf16[1536,128]{1,0:T(8,128)(2,1)S(1)} %get-tuple-element.47.kt_ref, bf16[1536,128]{1,0:T(8,128)(2,1)S(1)} %get-tuple-element.48.own_k_ref, bf16[1536,128]{1,0:T(8,128)(2,1)S(1)} %get-tuple-element.49.own_v_ref, ...), custom_call_target="tpu_custom_call" | custom-call | flops 7864320 | bytes 4194304 | tf_op jit(solution)/shard_map/pallas_call | solution.py:303
  51.5 5.0 %all-to-all-done.1.parts_ref = f32[8,1,128]{2,1,0:T(1,128)S(1)} async-done(((f32[8,1,128]{2,1,0:T(1,128)}), f32[8,1,128]{2,1,0:T(1,128)S(1)}, u32[]{:S(2)}, u32[]{:S(2)}) %all-to-all-start.1) | async-done | bytes 4128 | tf_op jit(solution)/shard_map/all_to_all | solution.py:317
  56.5 0.5 shard_map.134
  (14 shorter events, 0.0 us)
Async XLA Ops:
  0.6 11.9 %collective-permute-start.1 = (bf16[128,1536]{1,0:T(8,128)(2,1)}, bf16[128,1536]{1,0:T(8,128)(2,1)S(1)}, u32[]{:S(2)}, u32[]{:S(2)}) collective-permute-start(bf16[128,1536]{1,0:T(8,128)(2,1)} %bitcast.18), channel_id=1, source_target_pairs={{1,2},{2,1},{3,4},{4,3},{5,6},{6,5},{7,8},{8,7},{9,10},{10,9},{11,... | collective-permute-start | bytes 1179656 | tf_op jit(solution)/shard_map/ppermute | solution.py:34
  5.2 2.2 %copy-start = (bf16[1,128,1536]{2,1,0:T(8,128)(2,1)S(1)}, bf16[1,128,1536]{2,1,0:T(8,128)(2,1)}, u32[]{:S(2)}) copy-start(bf16[1,128,1536]{2,1,0:T(8,128)(2,1)} %param.11) | copy-start | bytes 1179652
  5.2 2.2 %copy-start.1 = (bf16[1,128,1536]{2,1,0:T(8,128)(2,1)S(1)}, bf16[1,128,1536]{2,1,0:T(8,128)(2,1)}, u32[]{:S(2)}) copy-start(bf16[1,128,1536]{2,1,0:T(8,128)(2,1)} %param.8) | copy-start | bytes 1179652
  5.2 2.2 %copy-start.2 = (bf16[1,128,1536]{2,1,0:T(8,128)(2,1)S(1)}, bf16[1,128,1536]{2,1,0:T(8,128)(2,1)}, u32[]{:S(2)}) copy-start(bf16[1,128,1536]{2,1,0:T(8,128)(2,1)} %param.9) | copy-start | bytes 1179652
  5.2 2.2 %copy-start.3 = (bf16[1,128,1536]{2,1,0:T(8,128)(2,1)S(1)}, bf16[1,128,1536]{2,1,0:T(8,128)(2,1)}, u32[]{:S(2)}) copy-start(bf16[1,128,1536]{2,1,0:T(8,128)(2,1)} %param.10) | copy-start | bytes 1179652
  5.2 2.2 %copy-start.4 = (s32[128,12]{0,1:T(8,128)S(1)}, s32[128,12]{0,1:T(8,128)}, u32[]{:S(2)}) copy-start(s32[128,12]{0,1:T(8,128)} %param.15) | copy-start | bytes 18436
  5.2 2.2 %copy-start.5 = (f32[128]{0:T(128)S(1)}, f32[128]{0:T(128)}, u32[]{:S(2)}) copy-start(f32[128]{0:T(128)} %param.12) | copy-start | bytes 1540
  5.2 2.2 %copy-start.6 = (s32[12,5]{0,1:T(8,128)S(1)}, s32[12,5]{0,1:T(8,128)}, u32[]{:S(2)}) copy-start(s32[12,5]{0,1:T(8,128)} %param.14) | copy-start | bytes 724
  5.2 2.2 %copy-start.7 = (f32[128]{0:T(128)S(1)}, f32[128]{0:T(128)}, u32[]{:S(2)}) copy-start(f32[128]{0:T(128)} %param.13) | copy-start | bytes 1540
  5.2 10.7 %collective-permute-start.2 = (bf16[128,1536]{1,0:T(8,128)(2,1)}, bf16[128,1536]{1,0:T(8,128)(2,1)S(1)}, u32[]{:S(2)}, u32[]{:S(2)}) collective-permute-start(bf16[128,1536]{1,0:T(8,128)(2,1)} %bitcast.20), channel_id=1, source_target_pairs={{1,2},{2,1},{3,4},{4,3},{5,6},{6,5},{7,8},{8,7},{9,10},{10,9},{11,... | collective-permute-start | bytes 1179656 | tf_op jit(solution)/shard_map/ppermute | solution.py:34
  8.4 6.0 %collective-permute-start = (bf16[2,128,1536]{2,1,0:T(8,128)(2,1)S(1)}, bf16[2,128,1536]{2,1,0:T(8,128)(2,1)S(1)}, u32[]{:S(2)}, u32[]{:S(2)}) collective-permute-start(bf16[2,128,1536]{2,1,0:T(8,128)(2,1)S(1)} %get-tuple-element.33.kv_ref), channel_id=1, source_target_pairs={{0,1},{1,0},{2,3},{3,2},{4,5},{5,4},{6,7},{7,6},{8,9},{9,8},{10,11... | collective-permute-start | bytes 2359304 | tf_op jit(solution)/shard_map/ppermute | solution.py:34
  18.9 20.4 %all-to-all-start = ((f32[64,1,128]{2,1,0:T(1,128)}), f32[64,1,128]{2,1,0:T(1,128)S(1)}, u32[]{:S(2)}, u32[]{:S(2)}) async-start(f32[64,1,128]{2,1,0:T(1,128)} %get-tuple-element.54), calls=%async_computation | async-start | bytes 65536 | tf_op jit(solution)/shard_map/all_to_all | solution.py:317
  30.0 20.0 %collective-permute-start.3 = (bf16[2,1536,128]{2,1,0:T(8,128)(2,1)}, bf16[2,1536,128]{2,1,0:T(8,128)(2,1)S(1)}, u32[]{:S(2)}, u32[]{:S(2)}) collective-permute-start(bf16[2,1536,128]{2,1,0:T(8,128)(2,1)} %get-tuple-element.50), channel_id=1, source_target_pairs={{1,2},{2,1},{3,4},{4,3},{5,6},{6,5},{7,8},{8,7},{9,10},{10,9},{11,... | collective-permute-start | bytes 2359304 | tf_op jit(solution)/shard_map/ppermute | solution.py:34
  33.5 16.5 %collective-permute-start.4 = (bf16[2,1536,128]{2,1,0:T(8,128)(2,1)}, bf16[2,1536,128]{2,1,0:T(8,128)(2,1)S(1)}, u32[]{:S(2)}, u32[]{:S(2)}) collective-permute-start(bf16[2,1536,128]{2,1,0:T(8,128)(2,1)} %get-tuple-element.51), channel_id=1, source_target_pairs={{0,1},{1,0},{2,3},{3,2},{4,5},{5,4},{6,7},{7,6},{8,9},{9,8},{10,11... | collective-permute-start | bytes 2359304 | tf_op jit(solution)/shard_map/ppermute | solution.py:34
  39.9 16.6 %all-to-all-start.1 = ((f32[8,1,128]{2,1,0:T(1,128)}), f32[8,1,128]{2,1,0:T(1,128)S(1)}, u32[]{:S(2)}, u32[]{:S(2)}) async-start(f32[8,1,128]{2,1,0:T(1,128)} %shard_map.133), calls=%async_computation.1 | async-start | bytes 8192 | tf_op jit(solution)/shard_map/all_to_all | solution.py:317
